TPU v7x, 32 devices: a whole 2x2x4 slice. The times are simulated.
32 devices in a mesh: row: 4 (over y, x), col: 8 (over z, core).
Axes of the slice: x: 2, y: 2, z: 4, core: 2. Of those that a mesh axis runs over, the one named last changes fastest.
Arguments:
- forward_state: bfloat16 [16777216], P(('row', 'col')), may hold values from -6 to 6
- adjoint_state: bfloat16 [16777216], P(('row', 'col')), may hold values from -6 to 6
- gate_matrix: bfloat16 [1024, 1024], replicated, may hold values from -1 to 1, as said below
Outputs:
- forward_final: bfloat16 [16777216], P(('row', 'col'))
- adjoint_final: bfloat16 [16777216], P(('row', 'col'))
- first_environment: float32 [1048576], P(('row', 'col'))
- second_environment: float32 [1048576], P(('row', 'col'))
Inputs may be any that keep to these rules, and one draw needn't show every extreme that they name: `gate_matrix`: an orthogonal matrix rounded to bfloat16.
All inputs are finite; a program needn't handle non-finite values.
Results may differ from a plain program's by a relative error of at most 0.0057.
Values may be sent and summed in bfloat16 or wider, within the bound.
No kernel may reach another device: no remote copies, remote signals or barrier semaphores. Data moves between devices by JAX's collectives and lax.ppermute only.
A program may use at most 128 MiB of HBM per device.

v0:
```python
import math

import jax
import jax.numpy as jnp
from jax import lax
from jax.sharding import PartitionSpec as P


def swapped(value, axis, apart):
    return lax.ppermute(value, axis, [(i, i ^ 1 << apart) for i in range(lax.axis_size(axis))])


def trade_half(state, device_bit, position, sender):
    length = state.shape[0]
    halves = state.reshape(2**position, 2, length // 2 ** (position + 1))
    lower = halves[:, 0, :]
    upper = halves[:, 1, :]
    keep_lower = device_bit == 0
    outgoing = jnp.where(keep_lower, upper, lower)
    incoming = sender(outgoing)
    new_lower = jnp.where(keep_lower, lower, incoming)
    new_upper = jnp.where(keep_lower, incoming, upper)
    return jnp.stack([new_lower, new_upper], axis=1).reshape(length)


def advance(forward, adjoint, gate_matrix, scale):
    width = gate_matrix.shape[0]
    forward_blocks = forward.reshape(width, forward.shape[0] // width)
    adjoint_blocks = adjoint.reshape(width, adjoint.shape[0] // width)
    forward_moved = jnp.dot(gate_matrix, forward_blocks, preferred_element_type=jnp.float32).astype(
        jnp.bfloat16
    )
    adjoint_moved = jnp.dot(gate_matrix, adjoint_blocks, preferred_element_type=jnp.float32).astype(
        jnp.bfloat16
    )
    partial_env = (
        lax.dot_general(
            adjoint_moved,
            forward_blocks,
            (((1,), (1,)), ((), ())),
            preferred_element_type=jnp.float32,
        )
        * scale
    )
    return (forward_moved.reshape(-1), adjoint_moved.reshape(-1), partial_env.reshape(-1))


def on_device(forward_state, adjoint_state, gate_matrix):
    col_count = lax.axis_size("col")
    top_bit = col_count.bit_length() - 2
    col_index = lax.axis_index("col")
    row_value = lax.axis_index("row") % 2
    top_value = col_index // (col_count // 2) % 2
    low_value = col_index % 2
    scale = 1.0 / math.sqrt(
        lax.axis_size("row") * col_count * forward_state.shape[0] / gate_matrix.shape[0]
    )

    def row_trade(pair):
        return tuple(
            (trade_half(one, row_value, 0, lambda piece: swapped(piece, "row", 0)) for one in pair)
        )

    def col_trade(pair, bit_index, device_bit):
        return tuple(
            (
                trade_half(one, device_bit, 1, lambda piece: swapped(piece, "col", bit_index))
                for one in pair
            )
        )

    states = (forward_state, adjoint_state)
    states = row_trade(states)
    states = col_trade(states, top_bit, top_value)
    forward_now, adjoint_now, first_partial = advance(states[0], states[1], gate_matrix, scale)
    states = (forward_now, adjoint_now)
    first_environment = lax.psum_scatter(
        first_partial, ("row", "col"), scatter_dimension=0, tiled=True
    )
    states = col_trade(states, top_bit, top_value)
    states = col_trade(states, 0, low_value)
    forward_now, adjoint_now, second_partial = advance(states[0], states[1], gate_matrix, scale)
    states = (forward_now, adjoint_now)
    states = row_trade(states)
    states = col_trade(states, 0, low_value)
    second_environment = lax.psum_scatter(
        second_partial, ("row", "col"), scatter_dimension=0, tiled=True
    )
    return (states[0], states[1], first_environment, second_environment)


def solution(mesh):
    in_specs = (P(("row", "col")), P(("row", "col")), P())
    out_specs = (P(("row", "col")), P(("row", "col")), P(("row", "col")), P(("row", "col")))
    return jax.shard_map(
        on_device, mesh=mesh, in_specs=in_specs, out_specs=out_specs, check_vma=False
    )
```

profile of v0, /device:TPU:0, one launch (start us, length us, event | category | flops | bytes accessed | tf_op | source)
XLA Modules:
  0.0 386.0 jit_solution(8008533966608488924)
XLA Ops:
  7.2 1.6 reshape.122
  8.9 2.6 broadcast_select_fusion.11
  11.5 2.9 collective-permute-start
  15.9 2.6 broadcast_select_fusion.5
  18.5 20.2 %collective-permute-done = bf16[1,262144]{1,0:T(2,128)(2,1)} collective-permute-done((bf16[1,262144]{1,0:T(2,128)(2,1)}, bf16[1,262144]{1,0:T(2,128)(2,1)}, u32[]{:S(2)}, u32[]{:S(2)}) %collective-permute-start) | collective-permute-done | bytes 524320 | tf_op jit(solution)/shard_map/ppermute | solution.py:10
  38.7 4.7 %broadcast_select_fusion.10 = (bf16[1,262144]{1,0:T(2,128)(2,1)S(1)}, bf16[1,262144]{1,0:T(2,128)(2,1)S(1)}) fusion(bf16[1,262144]{1,0:T(2,128)(2,1)} %collective-permute-done, pred[]{:T(512)S(6)} %eq.11, bf16[1,2,262144]{2,1,0:T(2,128)(2,1)} %copy-done.1), kind=kLoop, calls=%fused_computation.12 | loop fusion | flops 524288 | bytes 2621441 | tf_op jit(solution)/shard_map/jit(_where)/select_n | solution.py:21
  43.4 2.6 broadcast_select_fusion.23
  46.0 3.2 collective-permute-start.1
  49.3 11.1 %collective-permute-done.6 = bf16[1,262144]{1,0:T(2,128)(2,1)} collective-permute-done((bf16[1,262144]{1,0:T(2,128)(2,1)}, bf16[1,262144]{1,0:T(2,128)(2,1)}, u32[]{:S(2)}, u32[]{:S(2)}) %collective-permute-start.6) | collective-permute-done | bytes 524320 | tf_op jit(solution)/shard_map/ppermute | solution.py:10
  60.4 3.9 %broadcast_select_fusion.4 = (bf16[1,262144]{1,0:T(2,128)(2,1)S(1)}, bf16[1,262144]{1,0:T(2,128)(2,1)S(1)}) fusion(bf16[1,262144]{1,0:T(2,128)(2,1)} %collective-permute-done.6, pred[]{:T(512)S(6)} %eq.11, bf16[1,2,262144]{2,1,0:T(2,128)(2,1)S(1)} %reshape.124), kind=kLoop, calls=%fused_computation.6 | loop fusion | flops 524288 | bytes 2621441 | tf_op jit(solution)/shard_map/jit(_where)/select_n | solution.py:21
  64.3 3.9 %broadcast_select_fusion.17 = (bf16[2,131072]{1,0:T(2,128)(2,1)}, bf16[2,1,131072]{2,0,1:T(2,128)(2,1)}, bf16[2,131072]{1,0:T(2,128)(2,1)}) fusion(pred[]{:T(512)S(6)} %eq.12, bf16[1,2,131072]{2,0,1:T(2,128)(2,1)S(1)} %bitcast.167, bf16[1,2,131072]{2,0,1:T(2,128)(2,1)S(1)} %bitcast.166), kind=kLoop, calls=%fused_computation.49 | loop fusion | flops 2359296 | bytes 2621441 | tf_op jit(solution)/shard_map/jit(_where)/select_n | solution.py:19
  68.2 2.9 collective-permute-start.7
  74.6 1.7 reshape_reshape.28
  76.3 3.5 fusion
  81.3 1.6 reshape_reshape.29
  82.9 3.9 %fusion.31 = (bf16[2,1,131072]{2,1,0:T(2,128)(2,1)S(1)}, bf16[2,1,131072]{2,1,0:T(2,128)(2,1)S(1)}) fusion(bf16[2,2,131072]{2,1,0:T(2,128)(2,1)} %reshape_reshape.29), kind=kLoop, calls=%fused_computation.95 | loop fusion | bytes 2097152 | tf_op jit(solution)/shard_map/slice | solution.py:16
  86.9 2.1 broadcast_select_fusion.20
  89.1 17.0 %collective-permute-done.7 = bf16[2,131072]{1,0:T(2,128)(2,1)} collective-permute-done((bf16[2,131072]{1,0:T(2,128)(2,1)}, bf16[2,131072]{1,0:T(2,128)(2,1)}, u32[]{:S(2)}, u32[]{:S(2)}) %collective-permute-start.7) | collective-permute-done | bytes 524320 | tf_op jit(solution)/shard_map/ppermute | solution.py:10
  106.1 2.0 fusion.16
  109.6 2.1 copy.49
  111.7 2.8 reshape_reshape.32
  114.5 3.5 convolution_convert_fusion.1
  118.0 2.3 copy.50
  120.3 2.6 reshape_reshape.33
  122.9 3.5 fusion.30
  129.3 3.0 copy.62
  132.3 3.1 broadcast_select_fusion.35
  135.4 12.5 %collective-permute-done.8 = bf16[2,131072]{1,0:T(2,128)(2,1)S(1)} collective-permute-done((bf16[2,131072]{1,0:T(2,128)(2,1)S(1)}, bf16[2,131072]{1,0:T(2,128)(2,1)S(1)}, u32[]{:S(2)}, u32[]{:S(2)}) %collective-permute-start.8) | collective-permute-done | bytes 524320 | tf_op jit(solution)/shard_map/ppermute | solution.py:10
  147.9 3.1 broadcast_select_fusion.29
  154.7 1.7 reshape_reshape.30
  156.4 2.5 fusion.1
  160.3 2.0 reshape_reshape.31
  162.3 2.6 broadcast_select_fusion.8
  166.4 2.0 fusion.10
  169.9 2.1 copy.53
  171.9 2.8 reshape_reshape.34
  174.7 3.5 convolution_convert_fusion
  178.2 2.3 copy.54
  180.5 3.0 reshape_reshape.35
  183.5 4.5 %broadcast_select_fusion.2 = bf16[1,262144]{1,0:T(2,128)(2,1)} fusion(pred[]{:T(512)S(6)} %eq.11, bf16[1,2,262144]{2,1,0:T(2,128)(2,1)} %reshape_reshape.35), kind=kLoop, calls=%fused_computation.4 | loop fusion | flops 262144 | bytes 1572865 | tf_op jit(solution)/shard_map/jit(_where)/select_n | solution.py:19
  189.9 2.9 copy.63
  192.9 3.9 %broadcast_select_fusion.7 = (bf16[1,262144]{1,0:T(2,128)(2,1)S(1)}, bf16[1,262144]{1,0:T(2,128)(2,1)S(1)}) fusion(bf16[1,262144]{1,0:T(2,128)(2,1)} %collective-permute-done.4, pred[]{:T(512)S(6)} %eq.11, bf16[1,2,262144]{2,1,0:T(2,128)(2,1)S(1)} %reshape_reshape.31), kind=kLoop, calls=%fused_computation.9 | loop fusion | flops 524288 | bytes 2621441 | tf_op jit(solution)/shard_map/jit(_where)/select_n | solution.py:21
  196.8 2.6 broadcast_select_fusion.32
  199.5 28.0 %collective-permute-done.10 = bf16[1,262144]{1,0:T(2,128)(2,1)} collective-permute-done((bf16[1,262144]{1,0:T(2,128)(2,1)}, bf16[1,262144]{1,0:T(2,128)(2,1)}, u32[]{:S(2)}, u32[]{:S(2)}) %collective-permute-start.10) | collective-permute-done | bytes 524320 | tf_op jit(solution)/shard_map/ppermute | solution.py:10
  227.5 3.9 %broadcast_select_fusion.1 = (bf16[1,262144]{1,0:T(2,128)(2,1)S(1)}, bf16[1,262144]{1,0:T(2,128)(2,1)S(1)}) fusion(bf16[1,262144]{1,0:T(2,128)(2,1)} %collective-permute-done.10, pred[]{:T(512)S(6)} %eq.11, bf16[1,2,262144]{2,1,0:T(2,128)(2,1)S(1)} %copy-done.2), kind=kLoop, calls=%fused_computation.3 | loop fusion | flops 524288 | bytes 2621441 | tf_op jit(solution)/shard_map/jit(_where)/select_n | solution.py:21
  231.4 2.8 broadcast_select_fusion.26
  243.5 132.3 %all-reduce.5.cloned.1.call-done = (f32[1048576]{0:T(1024)}, f32[1048576]{0:T(1024)}) async-done(((f32[1048576]{0:T(1024)}, f32[1048576]{0:T(1024)}), (f32[1048576]{0:T(1024)}, f32[1048576]{0:T(1024)})) %all-reduce.5.cloned.1.call-update) | async-done | bytes 8388624
  375.8 1.6 dynamic-slice
  (67 shorter events, 31.8 us)
Async XLA Ops:
  7.2 69.1 %copy-start = (bf16[1024,1024]{1,0:T(8,128)(2,1)S(1)}, bf16[1024,1024]{1,0:T(8,128)(2,1)}, u32[]{:S(2)}) copy-start(bf16[1024,1024]{1,0:T(8,128)(2,1)} %param.5) | copy-start | bytes 6291460
  7.2 368.7 %all-reduce.5.cloned.1.call-start = ((), (), s32[]{:S(2)}) async-start(), calls=%async_computation | async-start | bytes 16777216
  8.9 2.6 copy-start.1
  11.5 27.2 %collective-permute-start = (bf16[1,262144]{1,0:T(2,128)(2,1)}, bf16[1,262144]{1,0:T(2,128)(2,1)}, u32[]{:S(2)}, u32[]{:S(2)}) collective-permute-start(bf16[1,262144]{1,0:T(2,128)(2,1)} %broadcast_select_fusion.11), channel_id=1, source_target_pairs={{0,8},{8,0},{16,24},{24,16},{1,9},{9,1},{17,25},{25,17},{2,10},{10... | collective-permute-start | bytes 1572872 | tf_op jit(solution)/shard_map/ppermute | solution.py:10
  18.5 41.8 %collective-permute-start.6 = (bf16[1,262144]{1,0:T(2,128)(2,1)}, bf16[1,262144]{1,0:T(2,128)(2,1)}, u32[]{:S(2)}, u32[]{:S(2)}) collective-permute-start(bf16[1,262144]{1,0:T(2,128)(2,1)} %broadcast_select_fusion.5), channel_id=1, source_target_pairs={{0,8},{8,0},{16,24},{24,16},{1,9},{9,1},{17,25},{25,17},{2,10},{10... | collective-permute-start | bytes 1572872 | tf_op jit(solution)/shard_map/ppermute | solution.py:10
  46.0 25.0 %collective-permute-start.1 = (bf16[2,131072]{1,0:T(2,128)(2,1)S(1)}, bf16[2,131072]{1,0:T(2,128)(2,1)S(1)}, u32[]{:S(2)}, u32[]{:S(2)}) collective-permute-start(bf16[2,131072]{1,0:T(2,128)(2,1)S(1)} %get-tuple-element.21), channel_id=1, source_target_pairs={{0,4},{1,5},{2,6},{3,7},{4,0},{5,1},{6,2},{7,3},{8,12},{9,13},{10,... | collective-permute-start | bytes 1572872 | tf_op jit(solution)/shard_map/ppermute | solution.py:10
  68.2 38.0 %collective-permute-start.7 = (bf16[2,131072]{1,0:T(2,128)(2,1)}, bf16[2,131072]{1,0:T(2,128)(2,1)}, u32[]{:S(2)}, u32[]{:S(2)}) collective-permute-start(bf16[2,131072]{1,0:T(2,128)(2,1)} %get-tuple-element.12), channel_id=1, source_target_pairs={{0,4},{1,5},{2,6},{3,7},{4,0},{5,1},{6,2},{7,3},{8,12},{9,13},{10,... | collective-permute-start | bytes 1572872 | tf_op jit(solution)/shard_map/ppermute | solution.py:10
  86.8 21.3 %copy-start.3 = (bf16[2,1,131072]{2,1,0:T(2,128)(2,1)}, bf16[2,1,131072]{2,1,0:T(2,128)(2,1)S(1)}, u32[]{:S(2)}) copy-start(bf16[2,1,131072]{2,1,0:T(2,128)(2,1)S(1)} %get-tuple-element.35) | copy-start | bytes 1572868
  86.9 19.3 %copy-start.7 = (bf16[2,1,131072]{2,0,1:T(2,128)(2,1)S(1)}, bf16[2,1,131072]{2,0,1:T(2,128)(2,1)}, u32[]{:S(2)}) copy-start(bf16[2,1,131072]{2,0,1:T(2,128)(2,1)} %get-tuple-element.13) | copy-start | bytes 1572868
  86.9 19.3 %copy-start.8 = (bf16[2,131072]{1,0:T(2,128)(2,1)S(1)}, bf16[2,131072]{1,0:T(2,128)(2,1)}, u32[]{:S(2)}) copy-start(bf16[2,131072]{1,0:T(2,128)(2,1)} %get-tuple-element.14) | copy-start | bytes 1572868
  89.0 43.2 %collective-permute-start.2 = (bf16[2,131072]{1,0:T(2,128)(2,1)}, bf16[2,131072]{1,0:T(2,128)(2,1)}, u32[]{:S(2)}, u32[]{:S(2)}) collective-permute-start(bf16[2,131072]{1,0:T(2,128)(2,1)} %broadcast_select_fusion.20), channel_id=1, source_target_pairs={{0,4},{1,5},{2,6},{3,7},{4,0},{5,1},{6,2},{7,3},{8,12},{9,13},{10,... | collective-permute-start | bytes 1572872 | tf_op jit(solution)/shard_map/ppermute | solution.py:10
  126.4 1.5 copy-start.9
  126.4 1.5 copy-start.11
  127.8 20.1 %collective-permute-start.8 = (bf16[2,131072]{1,0:T(2,128)(2,1)S(1)}, bf16[2,131072]{1,0:T(2,128)(2,1)S(1)}, u32[]{:S(2)}, u32[]{:S(2)}) collective-permute-start(bf16[2,131072]{1,0:T(2,128)(2,1)S(1)} %broadcast_select_fusion.14), channel_id=1, source_target_pairs={{0,4},{1,5},{2,6},{3,7},{4,0},{5,1},{6,2},{7,3},{8,12},{9,13},{10,... | collective-permute-start | bytes 1572872 | tf_op jit(solution)/shard_map/ppermute | solution.py:10
  129.2 3.0 copy-start.4
  135.3 15.7 %collective-permute-start.3 = (bf16[2,131072]{1,0:T(2,128)(2,1)S(1)}, bf16[2,131072]{1,0:T(2,128)(2,1)S(1)}, u32[]{:S(2)}, u32[]{:S(2)}) collective-permute-start(bf16[2,131072]{1,0:T(2,128)(2,1)S(1)} %get-tuple-element.18), channel_id=1, source_target_pairs={{0,1},{1,0},{2,3},{3,2},{4,5},{5,4},{6,7},{7,6},{8,9},{9,8},{10,11... | collective-permute-start | bytes 1572872 | tf_op jit(solution)/shard_map/ppermute | solution.py:10
  151.0 15.4 %collective-permute-start.9 = (bf16[2,131072]{1,0:T(2,128)(2,1)}, bf16[2,131072]{1,0:T(2,128)(2,1)}, u32[]{:S(2)}, u32[]{:S(2)}) collective-permute-start(bf16[2,131072]{1,0:T(2,128)(2,1)} %get-tuple-element.9), channel_id=1, source_target_pairs={{0,1},{1,0},{2,3},{3,2},{4,5},{5,4},{6,7},{7,6},{8,9},{9,8},{10,11... | collective-permute-start | bytes 1572872 | tf_op jit(solution)/shard_map/ppermute | solution.py:10
  162.3 4.1 %copy-start.5 = (bf16[2,131072]{1,0:T(2,128)(2,1)S(1)}, bf16[2,131072]{1,0:T(2,128)(2,1)}, u32[]{:S(2)}) copy-start(bf16[2,131072]{1,0:T(2,128)(2,1)} %get-tuple-element.10) | copy-start | bytes 1572868
  162.3 4.1 %copy-start.6 = (bf16[2,131072]{1,0:T(2,128)(2,1)S(1)}, bf16[2,131072]{1,0:T(2,128)(2,1)}, u32[]{:S(2)}) copy-start(bf16[2,131072]{1,0:T(2,128)(2,1)} %get-tuple-element.11) | copy-start | bytes 1572868
  164.9 27.9 %collective-permute-start.4 = (bf16[1,262144]{1,0:T(2,128)(2,1)}, bf16[1,262144]{1,0:T(2,128)(2,1)}, u32[]{:S(2)}, u32[]{:S(2)}) collective-permute-start(bf16[1,262144]{1,0:T(2,128)(2,1)} %broadcast_select_fusion.8), channel_id=1, source_target_pairs={{0,8},{8,0},{16,24},{24,16},{1,9},{9,1},{17,25},{25,17},{2,10},{10... | collective-permute-start | bytes 1572872 | tf_op jit(solution)/shard_map/ppermute | solution.py:10
  183.5 5.1 %copy-start.10 = (bf16[1024,512]{1,0:T(8,128)(2,1)S(1)}, bf16[1024,512]{1,0:T(8,128)(2,1)}, u32[]{:S(2)}) copy-start(bf16[1024,512]{1,0:T(8,128)(2,1)} %reshape_reshape.30) | copy-start | bytes 3145732
  183.5 5.1 %copy-start.12 = (bf16[512,1024]{1,0:T(8,128)(2,1)S(1)}, bf16[512,1024]{1,0:T(8,128)(2,1)}, u32[]{:S(2)}) copy-start(bf16[512,1024]{1,0:T(8,128)(2,1)} %convolution_convert_fusion) | copy-start | bytes 3145732
  188.0 39.5 %collective-permute-start.10 = (bf16[1,262144]{1,0:T(2,128)(2,1)}, bf16[1,262144]{1,0:T(2,128)(2,1)}, u32[]{:S(2)}, u32[]{:S(2)}) collective-permute-start(bf16[1,262144]{1,0:T(2,128)(2,1)} %broadcast_select_fusion.2), channel_id=1, source_target_pairs={{0,8},{8,0},{16,24},{24,16},{1,9},{9,1},{17,25},{25,17},{2,10},{10... | collective-permute-start | bytes 1572872 | tf_op jit(solution)/shard_map/ppermute | solution.py:10
  196.8 30.7 %copy-start.2 = (bf16[1,2,262144]{2,1,0:T(2,128)(2,1)S(1)}, bf16[1,2,262144]{2,1,0:T(2,128)(2,1)}, u32[]{:S(2)}) copy-start(bf16[1,2,262144]{2,1,0:T(2,128)(2,1)} %reshape_reshape.35) | copy-start | bytes 3145732
  199.4 34.8 %collective-permute-start.5 = (bf16[2,131072]{1,0:T(2,128)(2,1)S(1)}, bf16[2,131072]{1,0:T(2,128)(2,1)S(1)}, u32[]{:S(2)}, u32[]{:S(2)}) collective-permute-start(bf16[2,131072]{1,0:T(2,128)(2,1)S(1)} %get-tuple-element.15), channel_id=1, source_target_pairs={{0,1},{1,0},{2,3},{3,2},{4,5},{5,4},{6,7},{7,6},{8,9},{9,8},{10,11... | collective-permute-start | bytes 1572872 | tf_op jit(solution)/shard_map/ppermute | solution.py:10
  234.2 2.5 collective-permute-start.11
Sparse Core Ops, SparseCore 0:
  193.0 182.8 all-reduce.4
where the time goes:
time: 393 us; the launch traced here: 386 us
  waiting for transfers between devices  221 us (56%)
  other arithmetic  66.7 us (17%)
  local copies, waits for them, and re-layouts  56.3 us (14%)
  matrix products  15.7 us (4%)
  between operations  14.7 us (4%)
  starting transfers between devices  11.6 us (3%)
    unnamed x2, waiting for transfers between devices  132 us
    ppermute x12, waiting for transfers between devices, swapped(): lax.ppermute(value, axis, [(i, i ^ 1 << apart) for i in range(lax.axis_si...  88.8 us
    select_n x12, other arithmetic, trade_half(): outgoing = jnp.where(keep_lower, upper, lower)  33.9 us
    another operation x12, other arithmetic, trade_half(): return jnp.stack([new_lower, new_upper], axis=1).reshape(length)  16.5 us
    select_n x4, other arithmetic, trade_half(): new_lower = jnp.where(keep_lower, lower, incoming)  16.4 us
    ppermute x12, starting transfers between devices, swapped(): lax.ppermute(value, axis, [(i, i ^ 1 << apart) for i in range(lax.axis_si...  11.5 us
    unnamed x32, local copies, waits for them, and re-layouts  11.4 us
    another operation x4, local copies, waits for them, and re-layouts, trade_half(): halves = state.reshape(2 ** position, 2, length // 2 ** (position + 1))  9.22 us
  transfers between devices with their start and end apart: 13, of which 6 were waited for; matrix products, arithmetic and copies ran while one was open for 34% of the time, Pallas kernels for 0%

commit v1 on v0

v1 whole, which is shorter than its diff:
```python
import functools
import math

import jax
import jax.numpy as jnp
from jax import lax
from jax.experimental import pallas as pl
from jax.experimental.pallas import tpu as pltpu
from jax.sharding import PartitionSpec as P

AXES = ("row", "col")


def sent(value, target):
    count = lax.axis_size("row") * lax.axis_size("col")
    return lax.ppermute(value, AXES, [(i, target(i)) for i in range(count)])


def gate_kernel(block, col_ref, row_ref, gate_ref, *refs, n_in):
    state_refs, out_refs = refs[:n_in], refs[n_in:]

    def source(n):
        per = state_refs[0].shape[0] // block
        return state_refs[n // per][pl.ds(n % per * block, block), :]

    per_out = out_refs[0].shape[0] // block
    for m in range(per_out * len(out_refs)):
        rows = pl.ds(pl.multiple_of(row_ref[m] * block, block), block)
        total = None
        for n in range(4):
            cols = pl.ds(pl.multiple_of(col_ref[n] * block, block), block)
            term = jnp.dot(gate_ref[rows, cols], source(n), preferred_element_type=jnp.float32)
            total = term if total is None else total + term
        out_refs[m // per_out][pl.ds(m % per_out * block, block), :] = total.astype(jnp.bfloat16)


def apply_gate(gate_matrix, states, in_place, out_place, n_out):
    block = gate_matrix.shape[0] // 4
    width = states[0].shape[1]
    shape = jax.ShapeDtypeStruct((4 * block // n_out, width), jnp.bfloat16)
    smem = pl.BlockSpec(memory_space=pltpu.SMEM)
    vmem = pl.BlockSpec(memory_space=pltpu.VMEM)
    return pl.pallas_call(
        functools.partial(gate_kernel, block, n_in=len(states)),
        out_shape=[shape] * n_out,
        in_specs=[smem, smem] + [vmem] * (1 + len(states)),
        out_specs=[vmem] * n_out,
        compiler_params=pltpu.CompilerParams(vmem_limit_bytes=40 * 2**20),
        cost_estimate=pl.CostEstimate(
            flops=2 * 16 * block * block * width, bytes_accessed=32 * block * block + 16 * block * width, transcendentals=0
        ),
    )(in_place, out_place, gate_matrix, *states)


def env_kernel(block, part, scale, row_ref, col_ref, own_ref, *refs, n_left, n_right):
    left_refs, right_refs = refs[:n_left], refs[n_left : n_left + n_right]
    keep_ref, send_ref = refs[n_left + n_right :]
    own = own_ref[0]

    def pick(group, n):
        per = group[0].shape[0] // block
        return group[n // per][pl.ds(n % per * block, block), :]

    for m in range(4):
        rows = pl.ds(pl.multiple_of(row_ref[m] * (block // 2), block // 2), block // 2)
        for n in range(4):
            cols = pl.ds(pl.multiple_of(col_ref[n] * block, block), block)
            value = lax.dot_general(
                pick(left_refs, m), pick(right_refs, n), (((1,), (1,)), ((), ())), preferred_element_type=jnp.float32
            )
            value = (value * scale).reshape(block // (2 * part), 2, part, block)
            low, high = value[:, 0].reshape(block // 2, block), value[:, 1].reshape(block // 2, block)
            keep_ref[rows, cols] = jnp.where(own == 0, low, high)
            send_ref[rows, cols] = jnp.where(own == 0, high, low).astype(jnp.bfloat16)


def environment(left, right, left_place, right_place, own, part, scale):
    block = sum(one.shape[0] for one in left) // 4
    width = left[0].shape[1]
    smem = pl.BlockSpec(memory_space=pltpu.SMEM)
    vmem = pl.BlockSpec(memory_space=pltpu.VMEM)
    return pl.pallas_call(
        functools.partial(env_kernel, block, part, scale, n_left=len(left), n_right=len(right)),
        out_shape=[
            jax.ShapeDtypeStruct((2 * block, 4 * block), jnp.float32),
            jax.ShapeDtypeStruct((2 * block, 4 * block), jnp.bfloat16),
        ],
        in_specs=[smem] * 3 + [vmem] * (len(left) + len(right)),
        out_specs=[vmem, vmem],
        compiler_params=pltpu.CompilerParams(vmem_limit_bytes=40 * 2**20),
        cost_estimate=pl.CostEstimate(
            flops=2 * 16 * block * block * width, bytes_accessed=48 * block * block + 16 * block * width, transcendentals=0
        ),
    )(left_place, right_place, own.reshape(1), *left, *right)


def exchange_sum(value, bits, me):
    low, count = bits[0], 2 ** len(bits)
    mine = (me >> low) % count
    rows = value.shape[0] // count

    def piece(which):
        return lax.dynamic_slice_in_dim(value, which * rows, rows, 0)

    outgoing = [piece(mine ^ k).astype(jnp.bfloat16) for k in range(1, count)]
    incoming = [sent(one, lambda i, k=k: i ^ (k << low)) for k, one in enumerate(outgoing, 1)]
    total = piece(mine)
    for one in incoming:
        total = total + one.astype(jnp.float32)
    return total


def finish_environment(keep, send, me, row_bits, col_bits):
    total = keep + sent(send, lambda i: i ^ 1).astype(jnp.float32)
    total = exchange_sum(total, list(range(col_bits, col_bits + row_bits)), me)
    for bit in range(1, col_bits - 1):
        lead = 2 ** (col_bits - 1 - bit)
        rows = total.shape[0]
        grid = total.reshape(lead, 2, rows // (2 * lead), -1)
        grid = jnp.swapaxes(grid, 0, 1).reshape(rows, -1)
        total = exchange_sum(grid, [bit], me)
    if col_bits > 1:
        total = exchange_sum(total, [col_bits - 1], me)
    return total.reshape(-1)


def on_device(forward_state, adjoint_state, gate_matrix):
    row_count, col_count = lax.axis_size("row"), lax.axis_size("col")
    row_bits, col_bits = row_count.bit_length() - 1, col_count.bit_length() - 1
    me = lax.axis_index("row") * col_count + lax.axis_index("col")
    top, side = col_bits - 1, col_bits
    p, q, e = (me >> side) & 1, (me >> top) & 1, me & 1
    gate = gate_matrix.shape[0]
    block = gate // 4
    local = forward_state.shape[0]
    quarter = local // 4
    width = quarter // block
    scale = 1.0 / math.sqrt(row_count * col_count * local / gate)
    part = gate // (row_count * col_count)

    def across_x(value):
        return sent(value, lambda i: i ^ (1 << side))

    def across_z(value):
        return sent(value, lambda i: i ^ (1 << top))

    def across_core(value):
        return sent(value, lambda i: i ^ 1)

    def home(value, flip):
        return sent(value, lambda i: (i ^ ((i & 1) << top)) ^ flip)

    def arrive(state):
        def take(i, j):
            return lax.dynamic_slice_in_dim(state, ((p ^ i) * 2 + (q ^ j)) * quarter, quarter, 0)

        through = across_x(take(1, 1))
        direct = across_z(take(0, 1))
        beside = across_x(take(1, 0))
        through = across_z(through)
        return [one.reshape(block, width) for one in (take(0, 0), direct, beside, through)]

    forward_in = arrive(forward_state)
    adjoint_in = arrive(adjoint_state)
    first_in = jnp.stack([p * 2 + q, p * 2 + (1 - q), (1 - p) * 2 + q, (1 - p) * 2 + (1 - q)])
    kept = q ^ e
    first_out = jnp.stack([kept, 2 + kept, 1 - kept, 3 - kept])
    second_in = jnp.stack([e, 2 + e, 1 - e, 3 - e])
    second_out = jnp.stack([p * 2 + e, p * 2 + 1 - e, (1 - p) * 2 + e, (1 - p) * 2 + 1 - e])

    def middle(blocks):
        keep, send = apply_gate(gate_matrix, blocks, first_in, first_out, 2)
        return keep, send

    def leave(final):
        near, far = (one.reshape(-1) for one in final)
        far = across_x(far)
        result = jnp.zeros((local,), jnp.bfloat16)
        for i, one in enumerate((near, far)):
            for flip in range(2):
                got = home(one[flip * quarter : (flip + 1) * quarter], flip)
                place = (p ^ i) * 2 + (q ^ e ^ flip)
                result = lax.dynamic_update_slice_in_dim(result, got, place * quarter, 0)
        return result

    forward_keep, forward_send = middle(forward_in)
    forward_mid = [forward_keep, across_core(forward_send)]
    forward_out = apply_gate(gate_matrix, forward_mid, second_in, second_out, 2)
    forward_final = leave(forward_out)

    adjoint_keep, adjoint_send = middle(adjoint_in)
    first = environment([adjoint_keep, adjoint_send], forward_in, first_out, first_in, e, part, scale)
    adjoint_mid = [adjoint_keep, across_core(adjoint_send)]
    adjoint_out = apply_gate(gate_matrix, adjoint_mid, second_in, second_out, 2)
    second = environment(adjoint_out, forward_mid, second_out, second_in, e, part, scale)
    adjoint_final = leave(adjoint_out)

    first_environment = finish_environment(*first, me, row_bits, col_bits)
    second_environment = finish_environment(*second, me, row_bits, col_bits)
    return forward_final, adjoint_final, first_environment, second_environment


def solution(mesh):
    in_specs = (P(AXES), P(AXES), P())
    out_specs = (P(AXES),) * 4
    return jax.shard_map(on_device, mesh=mesh, in_specs=in_specs, out_specs=out_specs, check_vma=False)
```

time: 393 us -> 154 us (0.39); the launches traced: 386 us -> 152 us
  waiting for transfers between devices: 221 us -> 43.5 us
  other arithmetic: 66.7 us -> 1.23 us
  starting transfers between devices: 11.6 us -> 48.7 us
  matrix products: 15.7 us -> 0 us
  between operations: 14.7 us -> 1.22 us
  Pallas kernels: 0 us -> 11.9 us
  local copies, waits for them, and re-layouts: 56.3 us -> 45.6 us
    unnamed x2 -> x0, waiting for transfers between devices: 132 us -> none
    select_n x16 -> x0, other arithmetic: 50.3 us -> none  [the longest x12 33.9 us: trade_half(): outgoing = jnp.where(keep_lower, upper, lower)]
    ppermute x12 -> x32, waiting for transfers between devices: 88.8 us -> 43.5 us  [sent(): return lax.ppermute(value, AXES, [(i, target(i)) for i in range(count)])]
    ppermute x12 -> x32, starting transfers between devices: 11.5 us -> 48.7 us  [sent(): return lax.ppermute(value, AXES, [(i, target(i)) for i in range(count)])]
    dynamic_update_slice x0 -> x8, local copies, waits for them, and re-layouts: none -> 27.4 us  [leave(): result = lax.dynamic_update_slice_in_dim(result, got, place * quarter, 0)]
    another operation x14 -> x2, local copies, waits for them, and re-layouts: 26.9 us -> 0.14 us  [the longest x4 9.22 us: trade_half(): halves = state.reshape(2 ** position, 2, length // 2 ** (position + 1))]
    another operation x12 -> x3, other arithmetic: 16.5 us -> 0.24 us  [the longest x1 0.08 us: on_device(): jnp.stack([p * 2 + q, p * 2 + (1 - q), (1 - p) * 2 + q, (1 - p) * 2 + (1...]
    dot_general x6 -> x0, matrix products: 15.7 us -> none  [the longest x2 7.04 us: advance(): jnp.dot(gate_matrix, adjoint_blocks, preferred_element_type=jnp.float32)]
  transfers between devices with their start and end apart: 13 -> 32, of which waited for: 6 -> 8; matrix products, arithmetic and copies ran while one was open for 34% -> 26% of each run, Pallas kernels for 0% -> 8%
where the time goes in v1:
time: 154 us; the launch traced here: 152 us
  starting transfers between devices  48.7 us (32%)
  local copies, waits for them, and re-layouts  45.6 us (30%)
  waiting for transfers between devices  43.5 us (28%)
  Pallas kernels  11.9 us (8%)
    ppermute x32, starting transfers between devices, sent(): return lax.ppermute(value, AXES, [(i, target(i)) for i in range(count)])  48.7 us
    ppermute x32, waiting for transfers between devices, sent(): return lax.ppermute(value, AXES, [(i, target(i)) for i in range(count)])  43.5 us
    dynamic_update_slice x8, local copies, waits for them, and re-layouts, leave(): result = lax.dynamic_update_slice_in_dim(result, got, place * quarter, 0)  27.4 us
    unnamed x30, local copies, waits for them, and re-layouts  10.9 us
    pallas_call x4, Pallas kernels, apply_gate(): pl.pallas_call(functools.partial(gate_kernel, block, n_in=len(states)), o...  8.02 us
    reshape x8, local copies, waits for them, and re-layouts, arrive(): one.reshape(block, width)  4.16 us
    pallas_call x2, Pallas kernels, environment(): pl.pallas_call(functools.partial(env_kernel, block, part, scale, n_left=l...  3.9 us
  transfers between devices with their start and end apart: 32, of which 8 were waited for; matrix products, arithmetic and copies ran while one was open for 26% of the time, Pallas kernels for 8%

profile of v1, /device:TPU:0, one launch (start us, length us, event | category | flops | bytes accessed | tf_op | source)
XLA Modules:
  0.0 152.2 jit_solution(15589902414277659221)
XLA Ops:
  0.7 1.3 fusion.1
  2.0 4.1 %collective-permute-start = (bf16[131072]{0:T(1024)(128)(2,1)S(1)}, bf16[131072]{0:T(1024)(128)(2,1)}, u32[]{:S(2)}, u32[]{:S(2)}) collective-permute-start(bf16[131072]{0:T(1024)(128)(2,1)S(1)} %get-tuple-element.39), channel_id=1, source_target_pairs={{0,4},{1,5},{2,6},{3,7},{4,0},{5,1},{6,2},{7,3},{8,12},{9,13},{10,... | collective-permute-start | bytes 786440 | tf_op jit(solution)/shard_map/ppermute | solution.py:16
  6.1 1.5 collective-permute-start.1
  8.2 1.6 %collective-permute-start.12 = (bf16[131072]{0:T(1024)(128)(2,1)S(1)}, bf16[131072]{0:T(1024)(128)(2,1)}, u32[]{:S(2)}, u32[]{:S(2)}) collective-permute-start(bf16[131072]{0:T(1024)(128)(2,1)S(1)} %get-tuple-element.34), channel_id=1, source_target_pairs={{0,8},{1,9},{2,10},{3,11},{4,12},{5,13},{6,14},{7,15},{8,0},{9,1},... | collective-permute-start | bytes 786440 | tf_op jit(solution)/shard_map/ppermute | solution.py:16
  9.8 11.3 %collective-permute-done.2 = bf16[131072]{0:T(1024)(128)(2,1)} collective-permute-done((bf16[131072]{0:T(1024)(128)(2,1)S(1)}, bf16[131072]{0:T(1024)(128)(2,1)}, u32[]{:S(2)}, u32[]{:S(2)}) %collective-permute-start.2) | collective-permute-done | bytes 262176 | tf_op jit(solution)/shard_map/ppermute | solution.py:16
  21.1 2.9 %collective-permute-start.10 = (bf16[131072]{0:T(1024)(128)(2,1)S(1)}, bf16[131072]{0:T(1024)(128)(2,1)S(1)}, u32[]{:S(2)}, u32[]{:S(2)}) collective-permute-start(bf16[131072]{0:T(1024)(128)(2,1)S(1)} %get-tuple-element.35), channel_id=1, source_target_pairs={{0,4},{1,5},{2,6},{3,7},{4,0},{5,1},{6,2},{7,3},{8,12},{9,13},{10,... | collective-permute-start | bytes 786440 | tf_op jit(solution)/shard_map/ppermute | solution.py:16
  24.3 1.5 collective-permute-start.11
  25.8 1.1 reshape.65.refs_1_.refs_3_
  27.5 18.1 %collective-permute-done.3 = bf16[131072]{0:T(1024)(128)(2,1)S(1)} collective-permute-done((bf16[131072]{0:T(1024)(128)(2,1)}, bf16[131072]{0:T(1024)(128)(2,1)S(1)}, u32[]{:S(2)}, u32[]{:S(2)}) %collective-permute-start.3) | collective-permute-done | bytes 262176 | tf_op jit(solution)/shard_map/ppermute | solution.py:16
  45.8 1.6 %copy-done = bf16[1024,1024]{1,0:T(8,128)(2,1)S(1)} copy-done((bf16[1024,1024]{1,0:T(8,128)(2,1)S(1)}, bf16[1024,1024]{1,0:T(8,128)(2,1)}, u32[]{:S(2)}) %copy-start) | copy-done | bytes 2097176
  47.4 2.6 %shard_map.66 = (bf16[512,512]{1,0:T(8,128)(2,1)S(1)}, bf16[512,512]{1,0:T(8,128)(2,1)}) custom-call(s32[4]{0:T(128)S(1)} %get-tuple-element.50.col_ref, s32[4]{0:T(128)S(1)} %get-tuple-element.51.row_ref, bf16[1024,1024]{1,0:T(8,128)(2,1)S(1)} %copy-done, bf16[256,512]{1,0:T(8,128)(2,1)S(1)} %reshape.64.refs_0_.refs_2_, ...), custom_call_target="tpu_custom_call" | custom-call | flops 1073741824 | bytes 4194304 | tf_op jit(solution)/shard_map/pallas_call | solution.py:43
  51.4 1.1 reshape.71.refs_2_
  52.5 3.3 %collective-permute-done.13 = bf16[131072]{0:T(1024)(128)(2,1)} collective-permute-done((bf16[131072]{0:T(1024)(128)(2,1)}, bf16[131072]{0:T(1024)(128)(2,1)}, u32[]{:S(2)}, u32[]{:S(2)}) %collective-permute-start.13) | collective-permute-done | bytes 262176 | tf_op jit(solution)/shard_map/ppermute | solution.py:16
  55.8 1.1 reshape.72.refs_3_
  56.9 1.6 %copy-done.1 = bf16[1024,1024]{1,0:T(8,128)(2,1)S(1)} copy-done((bf16[1024,1024]{1,0:T(8,128)(2,1)S(1)}, bf16[1024,1024]{1,0:T(8,128)(2,1)}, u32[]{:S(2)}) %copy-start.1) | copy-done | bytes 2097176
  58.5 1.8 %shard_map.68 = (bf16[512,512]{1,0:T(8,128)(2,1)S(1)}, bf16[512,512]{1,0:T(8,128)(2,1)S(1)}) custom-call(s32[4]{0:T(128)S(1)} %get-tuple-element.50.col_ref, s32[4]{0:T(128)S(1)} %get-tuple-element.51.row_ref, bf16[1024,1024]{1,0:T(8,128)(2,1)S(1)} %copy-done.1, bf16[256,512]{1,0:T(8,128)(2,1)S(1)} %reshape.69.refs_0_, ...), custom_call_target="tpu_custom_call" | custom-call | flops 1073741824 | bytes 4194304 | tf_op jit(solution)/shard_map/pallas_call | solution.py:43
  60.6 1.8 %shard_map.67 = (bf16[512,512]{1,0:T(8,128)(2,1)S(1)}, bf16[512,512]{1,0:T(8,128)(2,1)S(1)}) custom-call(s32[4]{0:T(128)S(1)} %pad_add_fusion.col_ref, s32[4]{0:T(128)S(1)} %pad_add_fusion.1.row_ref, bf16[1024,1024]{1,0:T(8,128)(2,1)S(1)} %copy-done.1, bf16[512,512]{1,0:T(8,128)(2,1)S(1)} %copy-done.3, ...), custom_call_target="tpu_custom_call" | custom-call | flops 1073741824 | bytes 4194304 | tf_op jit(solution)/shard_map/pallas_call | solution.py:43
  62.4 0.8 copy.9
  63.2 1.6 %collective-permute-start.5 = (bf16[131072]{0:T(1024)(128)(2,1)}, bf16[131072]{0:T(1024)(128)(2,1)S(1)}, u32[]{:S(2)}, u32[]{:S(2)}) collective-permute-start(bf16[131072]{0:T(1024)(128)(2,1)} %bitcast.25), channel_id=1, source_target_pairs={{0,0},{1,5},{2,2},{3,7},{4,4},{5,1},{6,6},{7,3},{8,8},{9,13},{10,1... | collective-permute-start | bytes 786440 | tf_op jit(solution)/shard_map/ppermute | solution.py:16
  64.8 1.0 copy.11
  65.8 1.5 collective-permute-start.7
  67.3 1.8 %shard_map.69 = (bf16[512,512]{1,0:T(8,128)(2,1)S(1)}, bf16[512,512]{1,0:T(8,128)(2,1)S(1)}) custom-call(s32[4]{0:T(128)S(1)} %pad_add_fusion.col_ref, s32[4]{0:T(128)S(1)} %pad_add_fusion.1.row_ref, bf16[1024,1024]{1,0:T(8,128)(2,1)S(1)} %copy-done.1, bf16[512,512]{1,0:T(8,128)(2,1)S(1)} %get-tuple-element.20.refs_0_, ...), custom_call_target="tpu_custom_call" | custom-call | flops 1073741824 | bytes 4194304 | tf_op jit(solution)/shard_map/pallas_call | solution.py:43
  69.2 0.8 copy.12
  70.0 3.6 %collective-permute-start.15 = (bf16[131072]{0:T(1024)(128)(2,1)}, bf16[131072]{0:T(1024)(128)(2,1)}, u32[]{:S(2)}, u32[]{:S(2)}) collective-permute-start(bf16[131072]{0:T(1024)(128)(2,1)} %bitcast.31), channel_id=1, source_target_pairs={{0,0},{1,5},{2,2},{3,7},{4,4},{5,1},{6,6},{7,3},{8,8},{9,13},{10,1... | collective-permute-start | bytes 786440 | tf_op jit(solution)/shard_map/ppermute | solution.py:16
  74.4 1.2 collective-permute-start.6
  75.6 0.8 copy.13
  76.4 1.0 copy-done.6
  77.4 1.9 %shard_map.70 = (f32[512,1024]{1,0:T(8,128)S(1)}, bf16[512,1024]{1,0:T(8,128)(2,1)S(1)}) custom-call(s32[4]{0:T(128)S(1)} %get-tuple-element.51.row_ref, s32[4]{0:T(128)S(1)} %get-tuple-element.50.col_ref, s32[1]{0:T(128)} %bitcast.own_ref, bf16[512,512]{1,0:T(8,128)(2,1)S(1)} %copy-done.6, bf16[512,512]{1,0:T(8,128)(2,1)S(1)} %get-tuple-element.21.refs_1_, ...), custom_call_target="tpu_custom_call" | custom-call | flops 1073741824 | bytes 5242880 | tf_op jit(solution)/shard_map/pallas_call | solution.py:82
  79.6 2.0 %shard_map.71 = (f32[512,1024]{1,0:T(8,128)S(1)}, bf16[512,1024]{1,0:T(8,128)(2,1)S(1)}) custom-call(s32[4]{0:T(128)S(1)} %pad_add_fusion.1.row_ref, s32[4]{0:T(128)S(1)} %pad_add_fusion.col_ref, s32[1]{0:T(128)} %bitcast.own_ref, bf16[512,512]{1,0:T(8,128)(2,1)S(1)} %get-tuple-element.22.refs_0_, bf16[512,512]{1,0:T(8,128)(2,1)S(1)} %get-tuple-element.23.refs_1_, ...), custom_call_target="tpu_custom_call" | custom-call | flops 1073741824 | bytes 5242880 | tf_op jit(solution)/shard_map/pallas_call | solution.py:82
  82.1 2.6 %dynamic_update_slice.24 = bf16[524288]{0:T(1024)(128)(2,1)S(1)} dynamic-update-slice(bf16[524288]{0:T(1024)(128)(2,1)S(1)} %broadcast.6.clone, bf16[131072]{0:T(1024)(128)(2,1)S(1)} %collective-permute-done.5, s32[]{:T(128)S(6)} %select_n.89) | dynamic-update-slice | bytes 524292 | tf_op jit(solution)/shard_map/dynamic_update_slice | solution.py:183
  85.4 4.9 %dynamic_update_slice.28 = bf16[524288]{0:T(1024)(128)(2,1)S(1)} dynamic-update-slice(bf16[524288]{0:T(1024)(128)(2,1)S(1)} %broadcast.6.clone.1, bf16[131072]{0:T(1024)(128)(2,1)} %collective-permute-done.15, s32[]{:T(128)S(6)} %select_n.89) | dynamic-update-slice | bytes 524292 | tf_op jit(solution)/shard_map/dynamic_update_slice | solution.py:183
  90.3 2.2 %collective-permute-start.26 = (bf16[512,1024]{1,0:T(8,128)(2,1)S(1)}, bf16[512,1024]{1,0:T(8,128)(2,1)S(1)}, u32[]{:S(2)}, u32[]{:S(2)}) collective-permute-start(bf16[512,1024]{1,0:T(8,128)(2,1)S(1)} %get-tuple-element.27), channel_id=1, source_target_pairs={{0,1},{1,0},{2,3},{3,2},{4,5},{5,4},{6,7},{7,6},{8,9},{9,8},{10,11... | collective-permute-start | bytes 3145736 | tf_op jit(solution)/shard_map/ppermute | solution.py:16
  92.5 4.8 %dynamic_update_slice.25 = bf16[524288]{0:T(1024)(128)(2,1)S(1)} dynamic-update-slice(bf16[524288]{0:T(1024)(128)(2,1)S(1)} %dynamic_update_slice.24, bf16[131072]{0:T(1024)(128)(2,1)} %collective-permute-done.6, s32[]{:T(128)S(6)} %select_n.90) | dynamic-update-slice | bytes 524292 | tf_op jit(solution)/shard_map/dynamic_update_slice | solution.py:183
  97.4 4.9 %dynamic_update_slice.29 = bf16[524288]{0:T(1024)(128)(2,1)S(1)} dynamic-update-slice(bf16[524288]{0:T(1024)(128)(2,1)S(1)} %dynamic_update_slice.28, bf16[131072]{0:T(1024)(128)(2,1)} %collective-permute-done.16, s32[]{:T(128)S(6)} %select_n.90) | dynamic-update-slice | bytes 524292 | tf_op jit(solution)/shard_map/dynamic_update_slice | solution.py:183
  102.3 1.1 fusion.3
  104.1 0.9 collective-permute-start.18
  105.4 2.2 %collective-permute-start.23 = (bf16[128,1024]{1,0:T(8,128)(2,1)S(1)}, bf16[128,1024]{1,0:T(8,128)(2,1)S(1)}, u32[]{:S(2)}, u32[]{:S(2)}) collective-permute-start(bf16[128,1024]{1,0:T(8,128)(2,1)S(1)} %get-tuple-element.32), channel_id=1, source_target_pairs={{0,24},{1,25},{2,26},{3,27},{4,28},{5,29},{6,30},{7,31},{8,16},{9,... | collective-permute-start | bytes 786440 | tf_op jit(solution)/shard_map/ppermute | solution.py:16
  108.1 0.9 collective-permute-start.21
  109.4 7.0 %collective-permute-start.9 = (bf16[131072]{0:T(1024)(128)(2,1)S(1)}, bf16[131072]{0:T(1024)(128)(2,1)S(1)}, u32[]{:S(2)}, u32[]{:S(2)}) collective-permute-start(bf16[131072]{0:T(1024)(128)(2,1)S(1)} %get-tuple-element.46), channel_id=1, source_target_pairs={{0,1},{1,4},{2,3},{3,6},{4,5},{5,0},{6,7},{7,2},{8,9},{9,12},{10,1... | collective-permute-start | bytes 786440 | tf_op jit(solution)/shard_map/ppermute | solution.py:16
  116.4 5.6 %collective-permute-start.19 = (bf16[131072]{0:T(1024)(128)(2,1)S(1)}, bf16[131072]{0:T(1024)(128)(2,1)S(1)}, u32[]{:S(2)}, u32[]{:S(2)}) collective-permute-start(bf16[131072]{0:T(1024)(128)(2,1)S(1)} %get-tuple-element.42), channel_id=1, source_target_pairs={{0,1},{1,4},{2,3},{3,6},{4,5},{5,0},{6,7},{7,2},{8,9},{9,12},{10,1... | collective-permute-start | bytes 786440 | tf_op jit(solution)/shard_map/ppermute | solution.py:16
  122.1 5.1 %collective-permute-start.29 = (bf16[128,1024]{1,0:T(8,128)(2,1)S(1)}, bf16[128,1024]{1,0:T(8,128)(2,1)S(1)}, u32[]{:S(2)}, u32[]{:S(2)}) collective-permute-start(bf16[128,1024]{1,0:T(8,128)(2,1)S(1)} %get-tuple-element.29), channel_id=1, source_target_pairs={{0,24},{1,25},{2,26},{3,27},{4,28},{5,29},{6,30},{7,31},{8,16},{9,... | collective-permute-start | bytes 786440 | tf_op jit(solution)/shard_map/ppermute | solution.py:16
  128.0 2.6 %dynamic_update_slice.26 = bf16[524288]{0:T(1024)(128)(2,1)S(1)} dynamic-update-slice(bf16[524288]{0:T(1024)(128)(2,1)S(1)} %dynamic_update_slice.25, bf16[131072]{0:T(1024)(128)(2,1)S(1)} %collective-permute-done.8, s32[]{:T(128)S(6)} %select_n.91) | dynamic-update-slice | bytes 524292 | tf_op jit(solution)/shard_map/dynamic_update_slice | solution.py:183
  130.7 2.6 %dynamic_update_slice.30 = bf16[524288]{0:T(1024)(128)(2,1)S(1)} dynamic-update-slice(bf16[524288]{0:T(1024)(128)(2,1)S(1)} %dynamic_update_slice.29, bf16[131072]{0:T(1024)(128)(2,1)S(1)} %collective-permute-done.18, s32[]{:T(128)S(6)} %select_n.91) | dynamic-update-slice | bytes 524292 | tf_op jit(solution)/shard_map/dynamic_update_slice | solution.py:183
  133.4 2.5 %dynamic_update_slice.27 = bf16[524288]{0:T(1024)(128)(2,1)S(1)} dynamic-update-slice(bf16[524288]{0:T(1024)(128)(2,1)S(1)} %dynamic_update_slice.26, bf16[131072]{0:T(1024)(128)(2,1)S(1)} %collective-permute-done.9, s32[]{:T(128)S(6)} %select_n.92) | dynamic-update-slice | bytes 524292 | tf_op jit(solution)/shard_map/dynamic_update_slice | solution.py:183
  136.0 2.5 %dynamic_update_slice.31 = bf16[524288]{0:T(1024)(128)(2,1)S(1)} dynamic-update-slice(bf16[524288]{0:T(1024)(128)(2,1)S(1)} %dynamic_update_slice.30, bf16[131072]{0:T(1024)(128)(2,1)S(1)} %collective-permute-done.19, s32[]{:T(128)S(6)} %select_n.92) | dynamic-update-slice | bytes 524292 | tf_op jit(solution)/shard_map/dynamic_update_slice | solution.py:183
  139.5 1.2 collective-permute-start.30
  140.9 5.2 %collective-permute-done.30 = bf16[64,1024]{1,0:T(8,128)(2,1)S(1)} collective-permute-done((bf16[64,1024]{1,0:T(8,128)(2,1)S(1)}, bf16[64,1024]{1,0:T(8,128)(2,1)S(1)}, u32[]{:S(2)}, u32[]{:S(2)}) %collective-permute-start.30) | collective-permute-done | bytes 131104 | tf_op jit(solution)/shard_map/ppermute | solution.py:16
  147.4 4.0 %collective-permute-done.31 = bf16[32,1024]{1,0:T(8,128)(2,1)S(1)} collective-permute-done((bf16[32,1024]{1,0:T(8,128)(2,1)S(1)}, bf16[32,1024]{1,0:T(8,128)(2,1)S(1)}, u32[]{:S(2)}, u32[]{:S(2)}) %collective-permute-start.31) | collective-permute-done | bytes 65568 | tf_op jit(solution)/shard_map/ppermute | solution.py:16
  (93 shorter events, 11.8 us)
Async XLA Ops:
  0.6 7.5 %copy-start.7 = (bf16[524288]{0:T(1024)(128)(2,1)S(1)}, bf16[524288]{0:T(1024)(128)(2,1)}, u32[]{:S(2)}) copy-start(bf16[524288]{0:T(1024)(128)(2,1)} %param.4) | copy-start | bytes 3145732
  2.0 22.2 %collective-permute-start = (bf16[131072]{0:T(1024)(128)(2,1)S(1)}, bf16[131072]{0:T(1024)(128)(2,1)}, u32[]{:S(2)}, u32[]{:S(2)}) collective-permute-start(bf16[131072]{0:T(1024)(128)(2,1)S(1)} %get-tuple-element.39), channel_id=1, source_target_pairs={{0,4},{1,5},{2,6},{3,7},{4,0},{5,1},{6,2},{7,3},{8,12},{9,13},{10,... | collective-permute-start | bytes 786440 | tf_op jit(solution)/shard_map/ppermute | solution.py:16
  6.1 20.8 %collective-permute-start.1 = (bf16[131072]{0:T(1024)(128)(2,1)S(1)}, bf16[131072]{0:T(1024)(128)(2,1)S(1)}, u32[]{:S(2)}, u32[]{:S(2)}) collective-permute-start(bf16[131072]{0:T(1024)(128)(2,1)S(1)} %get-tuple-element.41), channel_id=1, source_target_pairs={{0,8},{1,9},{2,10},{3,11},{4,12},{5,13},{6,14},{7,15},{8,0},{9,1},... | collective-permute-start | bytes 786440 | tf_op jit(solution)/shard_map/ppermute | solution.py:16
  7.6 13.5 %collective-permute-start.2 = (bf16[131072]{0:T(1024)(128)(2,1)S(1)}, bf16[131072]{0:T(1024)(128)(2,1)}, u32[]{:S(2)}, u32[]{:S(2)}) collective-permute-start(bf16[131072]{0:T(1024)(128)(2,1)S(1)} %get-tuple-element.38), channel_id=1, source_target_pairs={{0,8},{1,9},{2,10},{3,11},{4,12},{5,13},{6,14},{7,15},{8,0},{9,1},... | collective-permute-start | bytes 786440 | tf_op jit(solution)/shard_map/ppermute | solution.py:16
  8.2 18.9 %collective-permute-start.12 = (bf16[131072]{0:T(1024)(128)(2,1)S(1)}, bf16[131072]{0:T(1024)(128)(2,1)}, u32[]{:S(2)}, u32[]{:S(2)}) collective-permute-start(bf16[131072]{0:T(1024)(128)(2,1)S(1)} %get-tuple-element.34), channel_id=1, source_target_pairs={{0,8},{1,9},{2,10},{3,11},{4,12},{5,13},{6,14},{7,15},{8,0},{9,1},... | collective-permute-start | bytes 786440 | tf_op jit(solution)/shard_map/ppermute | solution.py:16
  21.1 24.5 %collective-permute-start.3 = (bf16[131072]{0:T(1024)(128)(2,1)}, bf16[131072]{0:T(1024)(128)(2,1)S(1)}, u32[]{:S(2)}, u32[]{:S(2)}) collective-permute-start(bf16[131072]{0:T(1024)(128)(2,1)} %collective-permute-done.2), channel_id=1, source_target_pairs={{0,4},{1,5},{2,6},{3,7},{4,0},{5,1},{6,2},{7,3},{8,12},{9,13},{10,... | collective-permute-start | bytes 786440 | tf_op jit(solution)/shard_map/ppermute | solution.py:16
  21.1 30.1 %collective-permute-start.10 = (bf16[131072]{0:T(1024)(128)(2,1)S(1)}, bf16[131072]{0:T(1024)(128)(2,1)S(1)}, u32[]{:S(2)}, u32[]{:S(2)}) collective-permute-start(bf16[131072]{0:T(1024)(128)(2,1)S(1)} %get-tuple-element.35), channel_id=1, source_target_pairs={{0,4},{1,5},{2,6},{3,7},{4,0},{5,1},{6,2},{7,3},{8,12},{9,13},{10,... | collective-permute-start | bytes 786440 | tf_op jit(solution)/shard_map/ppermute | solution.py:16
  24.3 27.1 %collective-permute-start.11 = (bf16[131072]{0:T(1024)(128)(2,1)S(1)}, bf16[131072]{0:T(1024)(128)(2,1)}, u32[]{:S(2)}, u32[]{:S(2)}) collective-permute-start(bf16[131072]{0:T(1024)(128)(2,1)S(1)} %get-tuple-element.37), channel_id=1, source_target_pairs={{0,8},{1,9},{2,10},{3,11},{4,12},{5,13},{6,14},{7,15},{8,0},{9,1},... | collective-permute-start | bytes 786440 | tf_op jit(solution)/shard_map/ppermute | solution.py:16
  27.1 28.7 %collective-permute-start.13 = (bf16[131072]{0:T(1024)(128)(2,1)}, bf16[131072]{0:T(1024)(128)(2,1)}, u32[]{:S(2)}, u32[]{:S(2)}) collective-permute-start(bf16[131072]{0:T(1024)(128)(2,1)} %collective-permute-done.12), channel_id=1, source_target_pairs={{0,4},{1,5},{2,6},{3,7},{4,0},{5,1},{6,2},{7,3},{8,12},{9,13},{10,... | collective-permute-start | bytes 786440 | tf_op jit(solution)/shard_map/ppermute | solution.py:16
  45.8 1.6 %copy-start = (bf16[1024,1024]{1,0:T(8,128)(2,1)S(1)}, bf16[1024,1024]{1,0:T(8,128)(2,1)}, u32[]{:S(2)}) copy-start(bf16[1024,1024]{1,0:T(8,128)(2,1)} %gate_ref.7) | copy-start | bytes 6291460
  50.0 0.8 copy-start.2
  50.8 9.8 %collective-permute-start.4 = (bf16[512,512]{1,0:T(8,128)(2,1)}, bf16[512,512]{1,0:T(8,128)(2,1)S(1)}, u32[]{:S(2)}, u32[]{:S(2)}) collective-permute-start(bf16[512,512]{1,0:T(8,128)(2,1)} %get-tuple-element.17), channel_id=1, source_target_pairs={{0,1},{1,0},{2,3},{3,2},{4,5},{5,4},{6,7},{7,6},{8,9},{9,8},{10,11... | collective-permute-start | bytes 1572872 | tf_op jit(solution)/shard_map/ppermute | solution.py:16
  56.9 1.6 %copy-start.1 = (bf16[1024,1024]{1,0:T(8,128)(2,1)S(1)}, bf16[1024,1024]{1,0:T(8,128)(2,1)}, u32[]{:S(2)}) copy-start(bf16[1024,1024]{1,0:T(8,128)(2,1)} %gate_ref.7) | copy-start | bytes 6291460
  58.5 2.1 %copy-start.3 = (bf16[512,512]{1,0:T(8,128)(2,1)S(1)}, bf16[512,512]{1,0:T(8,128)(2,1)}, u32[]{:S(2)}) copy-start(bf16[512,512]{1,0:T(8,128)(2,1)} %copy-done.2) | copy-start | bytes 1572868
  60.3 7.0 %copy-start.5 = (bf16[512,512]{1,0:T(8,128)(2,1)}, bf16[512,512]{1,0:T(8,128)(2,1)S(1)}, u32[]{:S(2)}) copy-start(bf16[512,512]{1,0:T(8,128)(2,1)S(1)} %get-tuple-element.20.refs_0_) | copy-start | bytes 1572868
  60.3 7.0 %collective-permute-start.14 = (bf16[512,512]{1,0:T(8,128)(2,1)S(1)}, bf16[512,512]{1,0:T(8,128)(2,1)S(1)}, u32[]{:S(2)}, u32[]{:S(2)}) collective-permute-start(bf16[512,512]{1,0:T(8,128)(2,1)S(1)} %get-tuple-element.21.refs_1_), channel_id=1, source_target_pairs={{0,1},{1,0},{2,3},{3,2},{4,5},{5,4},{6,7},{7,6},{8,9},{9,8},{10,11... | collective-permute-start | bytes 1572872 | tf_op jit(solution)/shard_map/ppermute | solution.py:16
  63.2 18.3 %collective-permute-start.5 = (bf16[131072]{0:T(1024)(128)(2,1)}, bf16[131072]{0:T(1024)(128)(2,1)S(1)}, u32[]{:S(2)}, u32[]{:S(2)}) collective-permute-start(bf16[131072]{0:T(1024)(128)(2,1)} %bitcast.25), channel_id=1, source_target_pairs={{0,0},{1,5},{2,2},{3,7},{4,4},{5,1},{6,6},{7,3},{8,8},{9,13},{10,1... | collective-permute-start | bytes 786440 | tf_op jit(solution)/shard_map/ppermute | solution.py:16
  65.8 36.4 %collective-permute-start.7 = (bf16[262144]{0:T(1024)(128)(2,1)}, bf16[262144]{0:T(1024)(128)(2,1)}, u32[]{:S(2)}, u32[]{:S(2)}) collective-permute-start(bf16[262144]{0:T(1024)(128)(2,1)} %bitcast.29), channel_id=1, source_target_pairs={{0,8},{1,9},{2,10},{3,11},{4,12},{5,13},{6,14},{7,15},{8,0},{9,1},... | collective-permute-start | bytes 1572872 | tf_op jit(solution)/shard_map/ppermute | solution.py:16
  70.0 14.8 %collective-permute-start.15 = (bf16[131072]{0:T(1024)(128)(2,1)}, bf16[131072]{0:T(1024)(128)(2,1)}, u32[]{:S(2)}, u32[]{:S(2)}) collective-permute-start(bf16[131072]{0:T(1024)(128)(2,1)} %bitcast.31), channel_id=1, source_target_pairs={{0,0},{1,5},{2,2},{3,7},{4,4},{5,1},{6,6},{7,3},{8,8},{9,13},{10,1... | collective-permute-start | bytes 786440 | tf_op jit(solution)/shard_map/ppermute | solution.py:16
  74.4 15.9 %collective-permute-start.6 = (bf16[131072]{0:T(1024)(128)(2,1)}, bf16[131072]{0:T(1024)(128)(2,1)}, u32[]{:S(2)}, u32[]{:S(2)}) collective-permute-start(bf16[131072]{0:T(1024)(128)(2,1)} %bitcast.27), channel_id=1, source_target_pairs={{0,1},{1,4},{2,3},{3,6},{4,5},{5,0},{6,7},{7,2},{8,9},{9,12},{10,1... | collective-permute-start | bytes 786440 | tf_op jit(solution)/shard_map/ppermute | solution.py:16
  76.4 21.0 %collective-permute-start.16 = (bf16[131072]{0:T(1024)(128)(2,1)}, bf16[131072]{0:T(1024)(128)(2,1)}, u32[]{:S(2)}, u32[]{:S(2)}) collective-permute-start(bf16[131072]{0:T(1024)(128)(2,1)} %bitcast.33), channel_id=1, source_target_pairs={{0,1},{1,4},{2,3},{3,6},{4,5},{5,0},{6,7},{7,2},{8,9},{9,12},{10,1... | collective-permute-start | bytes 786440 | tf_op jit(solution)/shard_map/ppermute | solution.py:16
  76.4 1.0 copy-start.6
  77.4 2.2 %copy-start.4 = (bf16[512,512]{1,0:T(8,128)(2,1)S(1)}, bf16[512,512]{1,0:T(8,128)(2,1)}, u32[]{:S(2)}) copy-start(bf16[512,512]{1,0:T(8,128)(2,1)} %copy-done.2) | copy-start | bytes 1572868
  81.6 23.4 %collective-permute-start.20 = (bf16[512,1024]{1,0:T(8,128)(2,1)S(1)}, bf16[512,1024]{1,0:T(8,128)(2,1)S(1)}, u32[]{:S(2)}, u32[]{:S(2)}) collective-permute-start(bf16[512,1024]{1,0:T(8,128)(2,1)S(1)} %get-tuple-element.25), channel_id=1, source_target_pairs={{0,1},{1,0},{2,3},{3,2},{4,5},{5,4},{6,7},{7,6},{8,9},{9,8},{10,11... | collective-permute-start | bytes 3145736 | tf_op jit(solution)/shard_map/ppermute | solution.py:16
  84.8 19.2 %collective-permute-start.17 = (bf16[262144]{0:T(1024)(128)(2,1)S(1)}, bf16[262144]{0:T(1024)(128)(2,1)S(1)}, u32[]{:S(2)}, u32[]{:S(2)}) collective-permute-start(bf16[262144]{0:T(1024)(128)(2,1)S(1)} %bitcast.54), channel_id=1, source_target_pairs={{0,8},{1,9},{2,10},{3,11},{4,12},{5,13},{6,14},{7,15},{8,0},{9,1},... | collective-permute-start | bytes 1572872 | tf_op jit(solution)/shard_map/ppermute | solution.py:16
  90.3 17.8 %collective-permute-start.26 = (bf16[512,1024]{1,0:T(8,128)(2,1)S(1)}, bf16[512,1024]{1,0:T(8,128)(2,1)S(1)}, u32[]{:S(2)}, u32[]{:S(2)}) collective-permute-start(bf16[512,1024]{1,0:T(8,128)(2,1)S(1)} %get-tuple-element.27), channel_id=1, source_target_pairs={{0,1},{1,0},{2,3},{3,2},{4,5},{5,4},{6,7},{7,6},{8,9},{9,8},{10,11... | collective-permute-start | bytes 3145736 | tf_op jit(solution)/shard_map/ppermute | solution.py:16
  103.3 6.1 %collective-permute-start.8 = (bf16[131072]{0:T(1024)(128)(2,1)S(1)}, bf16[131072]{0:T(1024)(128)(2,1)S(1)}, u32[]{:S(2)}, u32[]{:S(2)}) collective-permute-start(bf16[131072]{0:T(1024)(128)(2,1)S(1)} %get-tuple-element.47), channel_id=1, source_target_pairs={{0,0},{1,5},{2,2},{3,7},{4,4},{5,1},{6,6},{7,3},{8,8},{9,13},{10,1... | collective-permute-start | bytes 786440 | tf_op jit(solution)/shard_map/ppermute | solution.py:16
  104.1 12.4 %collective-permute-start.18 = (bf16[131072]{0:T(1024)(128)(2,1)S(1)}, bf16[131072]{0:T(1024)(128)(2,1)S(1)}, u32[]{:S(2)}, u32[]{:S(2)}) collective-permute-start(bf16[131072]{0:T(1024)(128)(2,1)S(1)} %get-tuple-element.43), channel_id=1, source_target_pairs={{0,0},{1,5},{2,2},{3,7},{4,4},{5,1},{6,6},{7,3},{8,8},{9,13},{10,1... | collective-permute-start | bytes 786440 | tf_op jit(solution)/shard_map/ppermute | solution.py:16
  105.4 16.7 %collective-permute-start.23 = (bf16[128,1024]{1,0:T(8,128)(2,1)S(1)}, bf16[128,1024]{1,0:T(8,128)(2,1)S(1)}, u32[]{:S(2)}, u32[]{:S(2)}) collective-permute-start(bf16[128,1024]{1,0:T(8,128)(2,1)S(1)} %get-tuple-element.32), channel_id=1, source_target_pairs={{0,24},{1,25},{2,26},{3,27},{4,28},{5,29},{6,30},{7,31},{8,16},{9,... | collective-permute-start | bytes 786440 | tf_op jit(solution)/shard_map/ppermute | solution.py:16
  107.6 19.6 %collective-permute-start.22 = (bf16[128,1024]{1,0:T(8,128)(2,1)S(1)}, bf16[128,1024]{1,0:T(8,128)(2,1)S(1)}, u32[]{:S(2)}, u32[]{:S(2)}) collective-permute-start(bf16[128,1024]{1,0:T(8,128)(2,1)S(1)} %get-tuple-element.33), channel_id=1, source_target_pairs={{0,16},{1,17},{2,18},{3,19},{4,20},{5,21},{6,22},{7,23},{8,24},{9,... | collective-permute-start | bytes 786440 | tf_op jit(solution)/shard_map/ppermute | solution.py:16
  108.1 19.6 %collective-permute-start.21 = (bf16[128,1024]{1,0:T(8,128)(2,1)S(1)}, bf16[128,1024]{1,0:T(8,128)(2,1)S(1)}, u32[]{:S(2)}, u32[]{:S(2)}) collective-permute-start(bf16[128,1024]{1,0:T(8,128)(2,1)S(1)} %get-tuple-element.31), channel_id=1, source_target_pairs={{0,8},{1,9},{2,10},{3,11},{4,12},{5,13},{6,14},{7,15},{8,0},{9,1},... | collective-permute-start | bytes 786440 | tf_op jit(solution)/shard_map/ppermute | solution.py:16
  109.4 23.9 %collective-permute-start.9 = (bf16[131072]{0:T(1024)(128)(2,1)S(1)}, bf16[131072]{0:T(1024)(128)(2,1)S(1)}, u32[]{:S(2)}, u32[]{:S(2)}) collective-permute-start(bf16[131072]{0:T(1024)(128)(2,1)S(1)} %get-tuple-element.46), channel_id=1, source_target_pairs={{0,1},{1,4},{2,3},{3,6},{4,5},{5,0},{6,7},{7,2},{8,9},{9,12},{10,1... | collective-permute-start | bytes 786440 | tf_op jit(solution)/shard_map/ppermute | solution.py:16
  116.4 19.5 %collective-permute-start.19 = (bf16[131072]{0:T(1024)(128)(2,1)S(1)}, bf16[131072]{0:T(1024)(128)(2,1)S(1)}, u32[]{:S(2)}, u32[]{:S(2)}) collective-permute-start(bf16[131072]{0:T(1024)(128)(2,1)S(1)} %get-tuple-element.42), channel_id=1, source_target_pairs={{0,1},{1,4},{2,3},{3,6},{4,5},{5,0},{6,7},{7,2},{8,9},{9,12},{10,1... | collective-permute-start | bytes 786440 | tf_op jit(solution)/shard_map/ppermute | solution.py:16
  122.1 16.4 %collective-permute-start.29 = (bf16[128,1024]{1,0:T(8,128)(2,1)S(1)}, bf16[128,1024]{1,0:T(8,128)(2,1)S(1)}, u32[]{:S(2)}, u32[]{:S(2)}) collective-permute-start(bf16[128,1024]{1,0:T(8,128)(2,1)S(1)} %get-tuple-element.29), channel_id=1, source_target_pairs={{0,24},{1,25},{2,26},{3,27},{4,28},{5,29},{6,30},{7,31},{8,16},{9,... | collective-permute-start | bytes 786440 | tf_op jit(solution)/shard_map/ppermute | solution.py:16
  127.2 12.1 %collective-permute-start.28 = (bf16[128,1024]{1,0:T(8,128)(2,1)S(1)}, bf16[128,1024]{1,0:T(8,128)(2,1)S(1)}, u32[]{:S(2)}, u32[]{:S(2)}) collective-permute-start(bf16[128,1024]{1,0:T(8,128)(2,1)S(1)} %get-tuple-element.30), channel_id=1, source_target_pairs={{0,16},{1,17},{2,18},{3,19},{4,20},{5,21},{6,22},{7,23},{8,24},{9,... | collective-permute-start | bytes 786440 | tf_op jit(solution)/shard_map/ppermute | solution.py:16
  127.7 11.6 %collective-permute-start.27 = (bf16[128,1024]{1,0:T(8,128)(2,1)S(1)}, bf16[128,1024]{1,0:T(8,128)(2,1)S(1)}, u32[]{:S(2)}, u32[]{:S(2)}) collective-permute-start(bf16[128,1024]{1,0:T(8,128)(2,1)S(1)} %get-tuple-element.28), channel_id=1, source_target_pairs={{0,8},{1,9},{2,10},{3,11},{4,12},{5,13},{6,14},{7,15},{8,0},{9,1},... | collective-permute-start | bytes 786440 | tf_op jit(solution)/shard_map/ppermute | solution.py:16
  133.3 7.4 %collective-permute-start.24 = (bf16[64,1024]{1,0:T(8,128)(2,1)S(1)}, bf16[64,1024]{1,0:T(8,128)(2,1)S(1)}, u32[]{:S(2)}, u32[]{:S(2)}) collective-permute-start(bf16[64,1024]{1,0:T(8,128)(2,1)S(1)} %dynamic-slice_convert_fusion.7), channel_id=1, source_target_pairs={{0,2},{1,3},{2,0},{3,1},{4,6},{5,7},{6,4},{7,5},{8,10},{9,11},{10,... | collective-permute-start | bytes 393224 | tf_op jit(solution)/shard_map/ppermute | solution.py:16
  135.9 4.9 %copy-start.9 = (bf16[524288]{0:T(1024)(128)(2,1)}, bf16[524288]{0:T(1024)(128)(2,1)S(1)}, u32[]{:S(2)}) copy-start(bf16[524288]{0:T(1024)(128)(2,1)S(1)} %dynamic_update_slice.27) | copy-start | bytes 3145732
  138.5 7.7 %copy-start.8 = (bf16[524288]{0:T(1024)(128)(2,1)}, bf16[524288]{0:T(1024)(128)(2,1)S(1)}, u32[]{:S(2)}) copy-start(bf16[524288]{0:T(1024)(128)(2,1)S(1)} %dynamic_update_slice.31) | copy-start | bytes 3145732
  139.5 6.6 %collective-permute-start.30 = (bf16[64,1024]{1,0:T(8,128)(2,1)S(1)}, bf16[64,1024]{1,0:T(8,128)(2,1)S(1)}, u32[]{:S(2)}, u32[]{:S(2)}) collective-permute-start(bf16[64,1024]{1,0:T(8,128)(2,1)S(1)} %dynamic-slice_convert_fusion.6), channel_id=1, source_target_pairs={{0,2},{1,3},{2,0},{3,1},{4,6},{5,7},{6,4},{7,5},{8,10},{9,11},{10,... | collective-permute-start | bytes 393224 | tf_op jit(solution)/shard_map/ppermute | solution.py:16
  140.8 5.9 %collective-permute-start.25 = (bf16[32,1024]{1,0:T(8,128)(2,1)S(1)}, bf16[32,1024]{1,0:T(8,128)(2,1)S(1)}, u32[]{:S(2)}, u32[]{:S(2)}) collective-permute-start(bf16[32,1024]{1,0:T(8,128)(2,1)S(1)} %dynamic-slice_convert_fusion.9), channel_id=1, source_target_pairs={{0,4},{1,5},{2,6},{3,7},{4,0},{5,1},{6,2},{7,3},{8,12},{9,13},{10,... | collective-permute-start | bytes 196616 | tf_op jit(solution)/shard_map/ppermute | solution.py:16
  146.1 5.3 %collective-permute-start.31 = (bf16[32,1024]{1,0:T(8,128)(2,1)S(1)}, bf16[32,1024]{1,0:T(8,128)(2,1)S(1)}, u32[]{:S(2)}, u32[]{:S(2)}) collective-permute-start(bf16[32,1024]{1,0:T(8,128)(2,1)S(1)} %dynamic-slice_convert_fusion.8), channel_id=1, source_target_pairs={{0,4},{1,5},{2,6},{3,7},{4,0},{5,1},{6,2},{7,3},{8,12},{9,13},{10,... | collective-permute-start | bytes 196616 | tf_op jit(solution)/shard_map/ppermute | solution.py:16

commit v2 on v0

v2 whole, which is shorter than its diff:
```python
import functools
import math

import jax
import jax.numpy as jnp
from jax import lax
from jax.experimental import pallas as pl
from jax.experimental.pallas import tpu as pltpu
from jax.sharding import PartitionSpec as P

AXES = ("row", "col")
LANES = 128
KNOBS = {'waits': {'take2': ['Z1', 'Z2'], 'f_pack': ['Z3', 'f_X'], 'F2_0': ['f_near'], 'F1_1': ['a_X']}, 'lead': {'take2': 20000000000, 'F2_0': 12000000000}, 'free': ['take2'], 'out_f': 'packed', 'core_cuts': 4, 'env_cuts': 1, 'plan': '1G21212fa12', 'out_a': 'packed'}


SMEM = pl.BlockSpec(memory_space=pltpu.SMEM)
VMEM = pl.BlockSpec(memory_space=pltpu.VMEM)
HBM = pl.BlockSpec(memory_space=pltpu.HBM)
ANY = pl.BlockSpec(memory_space=pl.ANY)
VMEM_BYTES = 16 * 2**20
CORE_CUTS = KNOBS.get("core_cuts", 1)
ENV_CUTS = KNOBS.get("env_cuts", 1)


def sent(value, target):
    count = lax.axis_size("row") * lax.axis_size("col")
    return lax.ppermute(value, AXES, [(i, target(i)) for i in range(count)])

TOKEN = jax.ShapeDtypeStruct((8, LANES), jnp.float32)


def call(kernel, shapes, ids, arrays, after=(), scratch=(), raw_in=(), raw_out=(), work=0):
    n_in, n_out, n_after = len(arrays), len(shapes), len(after)

    def body(ids_ref, *refs):
        ins, refs = refs[:n_in], refs[n_in + n_after :]
        kernel([ids_ref[k] for k in range(4)], ins, refs[:n_out], *refs[n_out + 1 :])

    *results, token = pl.pallas_call(
        body,
        out_shape=[*shapes, TOKEN],
        in_specs=[SMEM] + [HBM if k in raw_in else VMEM for k in range(n_in)] + [ANY] * n_after,
        out_specs=[HBM if k in raw_out else VMEM for k in range(n_out)] + [ANY],
        scratch_shapes=list(scratch),
        compiler_params=pltpu.CompilerParams(vmem_limit_bytes=VMEM_BYTES),
        cost_estimate=pl.CostEstimate(flops=work, bytes_accessed=0, transcendentals=0),
    )(ids, *arrays, *after)
    return results, token


def arrived(ids, values, after=(), work=0):
    return call(lambda ids, ins, outs: None, [], ids, [], [*values, *after], work=work)[1]


def quarter_at(ids, i, j):
    return (ids[0] ^ i) * 2 + (ids[1] ^ j)


def take(ids, wanted, after=()):
    states = []
    for pieces in wanted:
        for one in pieces:
            if isinstance(one, tuple) and not any(one[0] is state for state in states):
                states.append(one[0])
    rows = states[0].shape[0] // 4
    arrays = [one for pieces in wanted for one in pieces if not isinstance(one, tuple)]
    plan = []
    for k, pieces in enumerate(wanted):
        for n, one in enumerate(pieces):
            if isinstance(one, tuple):
                plan.append((k, n, next(i for i, state in enumerate(states) if state is one[0]), one[1:]))
            else:
                plan.append((k, n, next(i for i, other in enumerate(arrays) if other is one), None))
    count = sum(at is not None for *_, at in plan)

    def kernel(ids, ins, outs, sems):
        copies = []
        for k, n, i, at in plan:
            if at is not None:
                start = pl.multiple_of(quarter_at(ids, *at) * rows, rows)
                target = outs[k].at[pl.ds(n * rows, rows)]
                copies.append(pltpu.make_async_copy(ins[i].at[pl.ds(start, rows)], target, sems.at[len(copies)]))
                copies[-1].start()
        for k, n, i, at in plan:
            if at is None:
                outs[k][n * rows : (n + 1) * rows, :] = ins[len(states) + i][...]
        for copy in copies:
            copy.wait()

    shapes = [jax.ShapeDtypeStruct((rows * len(pieces), LANES), states[0].dtype) for pieces in wanted]
    scratch = [pltpu.SemaphoreType.DMA((count,))]
    return call(kernel, shapes, ids, states + arrays, after, scratch, raw_in=range(len(states)))


def put(ids, pieces, places, after):
    count = 4
    rows = sum(piece.shape[0] for piece in pieces) // count

    def kernel(ids, ins, outs, sems):
        copies, at = [], places(ids)
        for piece in ins:
            for k in range(0, piece.shape[0], rows):
                start = pl.multiple_of(at[len(copies)] * rows, rows)
                target = outs[0].at[pl.ds(start, rows)]
                copies.append(pltpu.make_async_copy(piece.at[pl.ds(k, rows)], target, sems.at[len(copies)]))
                copies[-1].start()
        for copy in copies:
            copy.wait()

    shapes = [jax.ShapeDtypeStruct((rows * count, LANES), pieces[0].dtype)]
    scratch = [pltpu.SemaphoreType.DMA((count,))]
    return call(kernel, shapes, ids, pieces, after, scratch, raw_out=[0])


def pack(ids, groups, after):
    arrays = [one for group in groups for one in group]

    def kernel(ids, ins, outs):
        count = 0
        for group, out in zip(groups, outs, strict=True):
            row = 0
            for one in group:
                out[row : row + one.shape[0], :] = ins[count][...]
                row += one.shape[0]
                count += 1

    shapes = [jax.ShapeDtypeStruct((sum(one.shape[0] for one in group), LANES), group[0].dtype) for group in groups]
    return call(kernel, shapes, ids, arrays, after)


def load_state(block, linear, states, place_ref, moved_ref, spread):
    ratio = moved_ref.shape[1] // LANES
    if linear:
        lines, n = block * ratio, 0
        for state in states:
            for k in range(0, state.shape[0], lines):
                rows = pl.ds(pl.multiple_of(place_ref[n] * block, block), block)
                spread[...] = state[k : k + lines, :].astype(jnp.float32)
                for c in range(ratio):
                    part = spread[pl.ds(c, block, stride=ratio), :]
                    moved_ref[rows, c * LANES : (c + 1) * LANES] = part.astype(jnp.bfloat16)
                n += 1
        return
    row = 0
    for state in states:
        step = min(block, state.shape[0])
        for k in range(0, state.shape[0], step):
            start = pl.multiple_of(place_ref[row // block] * block + row % block, step)
            moved_ref[pl.ds(start, step), :] = state[k : k + step, :]
            row += step


def gate_kernel(block, linear, sizes, env, in_place, out_place, ids, ins, results, moved_ref, *refs):
    in_ref, out_ref = in_place(ids), out_place(ids)
    n_out = 4 if sizes is None else len(sizes)
    outs = results[:n_out]
    spread = refs[0]
    if env is None:
        *states, gate_ref = ins
        moved_ref = results[n_out]
    else:
        *states, other_ref, gate_ref = ins
        grid_ref, env_spread = refs[1], refs[2]
    ratio = moved_ref.shape[1] // LANES
    load_state(block, linear, states, in_ref, moved_ref, spread)
    for m in range(4):
        rows = pl.ds(pl.multiple_of(out_ref[m] * block, block), block)
        total = jnp.dot(gate_ref[rows, :], moved_ref[...], preferred_element_type=jnp.float32)
        rounded = total.astype(jnp.bfloat16)
        if env is not None:
            grid_ref[m * block : (m + 1) * block, :] = rounded
        if sizes is None:
            for c in range(ratio):
                spread[pl.ds(c, block, stride=ratio), :] = total[:, c * LANES : (c + 1) * LANES]
            outs[m][...] = spread[...].astype(jnp.bfloat16)
            continue
        row = 0
        for out in outs:
            first, last = max(row, m * block), min(row + out.shape[0], (m + 1) * block)
            if first < last:
                out[first - row : last - row, :] = rounded[first - m * block : last - m * block, :]
            row += out.shape[0]
    if env is not None:
        env_from, unit, scale = env
        env_kernel(
            block, unit, scale, env_from(ids), ids[2], grid_ref, other_ref, results[n_out], results[n_out + 1 :], env_spread
        )


def env_kernel(block, unit, scale, from_ref, own, left_ref, right_ref, keep_ref, send_refs, spread):
    ratio = 4 * block // LANES
    pairs = block * ratio // (2 * unit)
    per = send_refs[0].shape[0]
    for m in range(4):
        left = left_ref[pl.ds(pl.multiple_of(from_ref[m] * block, block), block), :]
        value = lax.dot_general(left, right_ref[...], (((1,), (1,)), ((), ())), preferred_element_type=jnp.float32)
        for c in range(ratio):
            spread[pl.ds(c, block, stride=ratio), :] = value[:, c * LANES : (c + 1) * LANES] * scale
        for g in range(pairs):
            to = (m * pairs + g) * unit
            keep_ref[to : to + unit, :] = spread[pl.ds(pl.multiple_of((2 * g + own) * unit, unit), unit), :]
            away = spread[pl.ds(pl.multiple_of((2 * g + 1 - own) * unit, unit), unit), :].astype(jnp.bfloat16)
            step = min(unit, per)
            for k in range(0, unit, step):
                at = to + k
                send_refs[at // per][at % per : at % per + step, :] = away[k : k + step, :]


def apply_gate(ids, gate_matrix, states, in_place, out_place, width, linear, sizes, after, env=None, work=0):
    gate = gate_matrix.shape[0]
    block = gate // 4
    rows = block * width // LANES
    shapes = [jax.ShapeDtypeStruct((rows, LANES), jnp.bfloat16)] * 4
    if sizes is not None:
        shapes = [jax.ShapeDtypeStruct((size, width), jnp.bfloat16) for size in sizes]
    n_out = len(shapes)
    arrays = [*states, gate_matrix]
    whole = pltpu.VMEM((gate, width), jnp.bfloat16)
    scratch = [pltpu.VMEM((rows, LANES), jnp.float32)]
    if env is None:
        shapes.append(jax.ShapeDtypeStruct((gate, width), jnp.bfloat16))
        scratch = [pltpu.VMEM((8, LANES), jnp.bfloat16)] + scratch
        numbers = None
    else:
        other, *numbers = env
        lines = gate * gate // (2 * LANES)
        shapes.append(jax.ShapeDtypeStruct((lines, LANES), jnp.float32))
        shapes += [jax.ShapeDtypeStruct((lines // ENV_CUTS, LANES), jnp.bfloat16)] * ENV_CUTS
        arrays = [*states, other, gate_matrix]
        scratch = [whole] + scratch + [whole, pltpu.VMEM((block * gate // LANES, LANES), jnp.float32)]
    kernel = functools.partial(gate_kernel, block, linear, sizes, numbers, in_place, out_place)
    got, token = call(kernel, shapes, ids, arrays, after, scratch, work=work)
    return got[:n_out], got[n_out:], token


def fold(ids, base, incoming, left, group, unit, after, work=0):
    lead = [bit for bit in left if bit not in group]
    stride = {bit: unit << (len(left) - 1 - n) for n, bit in enumerate(left)}
    flips = [sum(((k >> n) & 1) << bit for n, bit in enumerate(group)) for k in range(2 ** len(group))]
    rows = unit << len(lead)

    arrays = [piece for one in incoming for piece in one]

    def kernel(ids, ins, outs):
        def summed(at):
            value = ins[0][at, :]
            count = 1
            for one in incoming:
                per = one[0].shape[0]
                start = at.start
                inside = pl.ds(start - start // per * per if len(one) > 1 else start, unit)
                inside = pl.ds(pl.multiple_of(inside.start, unit), unit) if group else inside
                part = ins[count][inside, :].astype(jnp.float32)
                for k in range(1, len(one)):
                    part = jnp.where(start // per == k, ins[count + k][inside, :].astype(jnp.float32), part)
                value = value + part
                count += len(one)
            return value

        for n in sorted(range(len(flips)), key=lambda n: n == 0):
            origin = sum((((ids[3] ^ flips[n]) >> bit) & 1) * stride[bit] for bit in group)
            for k in range(2 ** len(lead)):
                shift = sum(((k >> (len(lead) - 1 - i)) & 1) * stride[bit] for i, bit in enumerate(lead))
                at = pl.ds(pl.multiple_of(origin + shift, unit), unit) if group else pl.ds(shift, unit)
                outs[n][k * unit : (k + 1) * unit, :] = summed(at).astype(outs[n].dtype)

    shapes = [jax.ShapeDtypeStruct((rows, LANES), jnp.float32 if flip == 0 else jnp.bfloat16) for flip in flips]
    (own, *pieces), token = call(kernel, shapes, ids, [base, *arrays], after, work=work)
    return own, pieces, flips[1:], token


def on_device(forward_state, adjoint_state, gate_matrix):
    row_count, col_count = lax.axis_size("row"), lax.axis_size("col")
    row_bits, col_bits = row_count.bit_length() - 1, col_count.bit_length() - 1
    me = lax.axis_index("row") * col_count + lax.axis_index("col")
    top, side = col_bits - 1, col_bits
    p, q, e = (me >> side) & 1, (me >> top) & 1, me & 1
    gate = gate_matrix.shape[0]
    local = forward_state.shape[0]
    width = local // gate
    scale = 1.0 / math.sqrt(row_count * col_count * local / gate)
    unit = gate * gate // (row_count * col_count * LANES)
    half = gate // 2
    ids = jnp.stack([p, q, e, me]).astype(jnp.int32)

    def across_x(value):
        return sent(value, lambda i: i ^ (1 << side))

    def across_z(value):
        return sent(value, lambda i: i ^ (1 << top))

    def across_core(value):
        return sent(value, lambda i: i ^ 1)

    def home(value, flip):
        return sent(value, lambda i: (i ^ ((i & 1) << top)) ^ flip)

    forward = forward_state.reshape(-1, LANES)
    adjoint = adjoint_state.reshape(-1, LANES)
    quarter = forward.shape[0] // 4

    def quarter_of(state, i, j):
        return lax.dynamic_slice_in_dim(state, ((p ^ i) * 2 + (q ^ j)) * quarter, quarter, 0)

    flight = {}
    chain = []

    def gates(name):
        waits = [value for key in KNOBS.get("waits", {}).get(name, ()) for value in flight[key]]
        before = chain[-1:]
        if not waits:
            return before
        free = name in KNOBS.get("free", ())
        token = arrived(ids, waits, [] if free else before, work=KNOBS.get("lead", {}).get(name, 0))
        return [token, *before] if free else [token]

    def link(token):
        chain.append(token)

    def work(name):
        return KNOBS.get("work", {}).get(name, 0)

    flight["Z1"] = [across_z(quarter_of(forward, 0, 1))]
    flight["X1"] = [across_x(quarter_of(forward, 1, 1))]
    flight["Z2"] = [across_z(flight["X1"][0])]
    (f_own, f_beside, a_relay), token = take(
        ids, [[(forward, 0, 0)], [(forward, 1, 0)], [(adjoint, 1, 1)]], [arrived(ids, flight["X1"]), *gates("take1")]
    )
    link(token)
    flight["X2"] = [across_x(f_beside)]
    flight["X3"] = [across_x(a_relay)]
    (a_own, a_beside, *a_over), token = take(
        ids,
        [[(adjoint, 0, 0)], [(adjoint, 1, 0)]]
        + (
            [[(adjoint, 0, 1), flight["X3"][0]]]
            if KNOBS.get("join_in", True)
            else [[(adjoint, 0, 1)], [flight["X3"][0]]]
        ),
        gates("take2"),
    )
    link(token)
    flight["Z3"] = [across_z(one) for one in a_over]
    flight["X4"] = [across_x(a_beside)]
    forward_in = [f_own, *flight["Z1"], *flight["X2"], *flight["Z2"]]
    adjoint_in = [a_own, *flight["Z3"], *flight["X4"]]

    def forward_place(ids):
        return [quarter_at(ids, i, j) for i in range(2) for j in range(2)]

    def adjoint_place(ids):
        return [quarter_at(ids, *at) for at in ((0, 0), (0, 1), (1, 1), (1, 0))]

    def first_out(ids):
        kept = ids[1] ^ ids[2]
        return [kept, 2 + kept, 1 - kept, 3 - kept]

    def first_from(ids):
        kept = ids[1] ^ ids[2]
        return [2 * kept, 2 * (1 - kept), 1 + 2 * kept, 1 + 2 * (1 - kept)]

    def second_in(ids):
        return [ids[2], 2 + ids[2], 1 - ids[2], 3 - ids[2]]

    def second_out(ids):
        return [(ids[0] ^ i) * 2 + (ids[2] ^ j) for i in range(2) for j in range(2)]

    def first_gate(name, blocks, place, env=None):
        sizes = [half] + [half // CORE_CUTS] * CORE_CUTS
        (keep, *send), extra, token = apply_gate(
            ids, gate_matrix, blocks, place, first_out, width, True, sizes, gates(name), env, work(name)
        )
        link(token)
        return [keep] + [across_core(one) for one in send], extra

    def second_gate(name, blocks, env=None):
        out, extra, token = apply_gate(
            ids, gate_matrix, blocks, second_in, second_out, width, False, None, gates(name), env, work(name)
        )
        link(token)
        return out, extra

    def final_place(ids, i, flip):
        return (ids[0] ^ i) * 2 + (ids[1] ^ ids[2] ^ flip)

    def by_row(ids):
        return [final_place(ids, i, flip) for i in range(2) for flip in range(2)]

    def by_flip(ids):
        return [final_place(ids, i, flip) for flip in range(2) for i in range(2)]

    def leave(name, out):
        style = KNOBS.get("out_" + name, "direct")
        flight[name + "_X"] = [across_x(one) for one in out[2:]]
        if style == "packed":
            packed, token = pack(ids, [[out[k], flight[name + "_X"][k]] for k in range(2)], gates(name + "_pack"))
            link(token)
            flight[name + "_near"] = flight[name + "_far"] = [home(one, flip) for flip, one in enumerate(packed)]
            return
        near = out[:2]
        if style == "gated":
            near, token = pack(ids, [[one] for one in near], gates(name + "_pack"))
            link(token)
        flight[name + "_near"] = [home(one, flip) for flip, one in enumerate(near)]
        far = flight[name + "_X"]
        if KNOBS.get("far_" + name, False):
            far, token = pack(ids, [[one] for one in far], gates(name + "_far_pack"))
            link(token)
        flight[name + "_far"] = [home(one, flip) for flip, one in enumerate(far)]

    def finish(name):
        if KNOBS.get("out_" + name, "direct") == "packed":
            pieces, places = flight[name + "_near"], by_flip
        else:
            pieces, places = flight[name + "_near"] + flight[name + "_far"], by_row
        (whole,), token = put(ids, pieces, places, gates("put_" + name))
        link(token)
        return whole.reshape(-1)

    upper, middle = list(range(side + 1, side + row_bits)), list(range(1, top))
    last = [[bit] for bit in middle[1:]] + [[top], []]
    orders = {
        "y_xz": [upper, [side] + middle[:1]],
        "y_x_z": [upper, [side], middle[:1]],
        "x_yz": [[side], upper + middle[:1]],
        "yx_z": [upper + [side], middle[:1]],
        "yxz": [upper + [side] + middle[:1]],
        "y_z_x": [upper, middle[:1], [side]],
    }
    order = {k: orders[KNOBS.get("order" + k, "y_xz")] + last for k in "12"}
    sums = {}

    def begin(key, extra):
        keep, *send = extra
        left = sorted((bit for group in order[key] for bit in group), reverse=True)
        sums[key] = keep, [[across_core(one) for one in send]], left, 0

    def step(key):
        base, incoming, left, n = sums[key]
        name = "F%s_%d" % (key, n)
        group = order[key][n]
        own, pieces, flips, token = fold(ids, base, incoming, left, group, unit, gates(name), work(name))
        link(token)
        come = [[sent(one, lambda i, flip=flip: i ^ flip)] for one, flip in zip(pieces, flips, strict=True)]
        flight[name] = [one for (one,) in come]
        sums[key] = own, come, [bit for bit in left if bit not in group], n + 1

    def steps_left(key):
        return len(order[key]) - sums[key][3]

    results = {}
    f_mid, (f_start,) = first_gate("G1f", forward_in, forward_place)
    f_out, (f_moved,) = second_gate("G2f", f_mid)
    leave("f", f_out)
    a_mid, extra = first_gate("GE1", adjoint_in, adjoint_place, (f_start, first_from, unit, scale))
    begin("1", extra)
    for name in KNOBS.get("plan", "1G21f122a12"):
        if name == "G":
            a_out, extra = second_gate("GE2", a_mid, (f_moved, second_out, unit, scale))
            begin("2", extra)
            leave("a", a_out)
        elif name in sums:
            if steps_left(name) > 1:
                step(name)
        else:
            results[name] = finish(name)
    for key in "12":
        while steps_left(key):
            step(key)
    return results["f"], results["a"], sums["1"][0].reshape(-1), sums["2"][0].reshape(-1)


def solution(mesh):
    in_specs = (P(AXES), P(AXES), P())
    out_specs = (P(AXES),) * 4
    return jax.shard_map(on_device, mesh=mesh, in_specs=in_specs, out_specs=out_specs, check_vma=False)
```

time: 393 us -> 133 us (0.34); the launches traced: 386 us -> 130 us
  waiting for transfers between devices: 221 us -> 62 us
  other arithmetic: 66.7 us -> 0.08 us
  local copies, waits for them, and re-layouts: 56.3 us -> 2.65 us
  starting transfers between devices: 11.6 us -> 38.1 us
  Pallas kernels: 0 us -> 26.3 us
  matrix products: 15.7 us -> 0 us
  between operations: 14.7 us -> 0.98 us
    unnamed x2 -> x0, waiting for transfers between devices: 132 us -> none
    select_n x16 -> x0, other arithmetic: 50.3 us -> none  [the longest x12 33.9 us: trade_half(): outgoing = jnp.where(keep_lower, upper, lower)]
    another operation x14 -> x0, local copies, waits for them, and re-layouts: 26.9 us -> none  [the longest x4 9.22 us: trade_half(): halves = state.reshape(2 ** position, 2, length // 2 ** (position + 1))]
    ppermute x12 -> x35, waiting for transfers between devices: 88.8 us -> 62 us  [sent(): return lax.ppermute(value, AXES, [(i, target(i)) for i in range(count)])]
    ppermute x12 -> x35, starting transfers between devices: 11.5 us -> 38.1 us  [sent(): return lax.ppermute(value, AXES, [(i, target(i)) for i in range(count)])]
    pallas_call x0 -> x23, Pallas kernels: none -> 26.3 us  [call(): pl.pallas_call(body, out_shape=[*shapes, TOKEN], in_specs=[SMEM] + [HBM i...]
    another operation x12 -> x1, other arithmetic: 16.5 us -> 0.08 us  [on_device(): ids = jnp.stack([p, q, e, me]).astype(jnp.int32)]
    dot_general x6 -> x0, matrix products: 15.7 us -> none  [the longest x2 7.04 us: advance(): jnp.dot(gate_matrix, adjoint_blocks, preferred_element_type=jnp.float32)]
  transfers between devices with their start and end apart: 13 -> 35, of which waited for: 6 -> 20; matrix products, arithmetic and copies ran while one was open for 34% -> 0% of each run, Pallas kernels for 0% -> 16%
where the time goes in v2:
time: 133 us; the launch traced here: 130 us
  waiting for transfers between devices  62 us (47%)
  starting transfers between devices  38.1 us (29%)
  Pallas kernels  26.3 us (20%)
  local copies, waits for them, and re-layouts  2.65 us (2%)
    ppermute x35, waiting for transfers between devices, sent(): return lax.ppermute(value, AXES, [(i, target(i)) for i in range(count)])  62 us
    ppermute x35, starting transfers between devices, sent(): return lax.ppermute(value, AXES, [(i, target(i)) for i in range(count)])  38.1 us
    pallas_call x23, Pallas kernels, call(): pl.pallas_call(body, out_shape=[*shapes, TOKEN], in_specs=[SMEM] + [HBM i...  26.3 us
  transfers between devices with their start and end apart: 35, of which 20 were waited for; matrix products, arithmetic and copies ran while one was open for 0% of the time, Pallas kernels for 16%

profile of v2, /device:TPU:0, one launch (start us, length us, event | category | flops | bytes accessed | tf_op | source)
XLA Modules:
  0.0 130.1 jit_solution(6092822115405549967)
XLA Ops:
  0.7 1.2 constant_dynamic-slice_fusion
  1.8 3.0 %collective-permute-start = (bf16[1024,128]{1,0:T(8,128)(2,1)S(1)}, bf16[1024,128]{1,0:T(8,128)(2,1)S(1)}, u32[]{:S(2)}, u32[]{:S(2)}) collective-permute-start(bf16[1024,128]{1,0:T(8,128)(2,1)S(1)} %get-tuple-element.147), channel_id=1, source_target_pairs={{0,8},{1,9},{2,10},{3,11},{4,12},{5,13},{6,14},{7,15},{8,0},{9,1},... | collective-permute-start | bytes 786440 | tf_op jit(solution)/shard_map/ppermute | solution.py:27
  4.8 2.6 %collective-permute-start.1 = (bf16[1024,128]{1,0:T(8,128)(2,1)S(1)}, bf16[1024,128]{1,0:T(8,128)(2,1)S(1)}, u32[]{:S(2)}, u32[]{:S(2)}) collective-permute-start(bf16[1024,128]{1,0:T(8,128)(2,1)S(1)} %get-tuple-element.146), channel_id=1, source_target_pairs={{0,4},{1,5},{2,6},{3,7},{4,0},{5,1},{6,2},{7,3},{8,12},{9,13},{10,... | collective-permute-start | bytes 786440 | tf_op jit(solution)/shard_map/ppermute | solution.py:27
  7.4 3.7 %collective-permute-done.refs_0_ = bf16[1024,128]{1,0:T(8,128)(2,1)S(1)} collective-permute-done((bf16[1024,128]{1,0:T(8,128)(2,1)S(1)}, bf16[1024,128]{1,0:T(8,128)(2,1)S(1)}, u32[]{:S(2)}, u32[]{:S(2)}) %collective-permute-start) | collective-permute-done | bytes 262176 | tf_op jit(solution)/shard_map/ppermute | solution.py:27
  11.1 2.8 %collective-permute-start.3 = (bf16[1024,128]{1,0:T(8,128)(2,1)S(1)}, bf16[1024,128]{1,0:T(8,128)(2,1)S(1)}, u32[]{:S(2)}, u32[]{:S(2)}) collective-permute-start(bf16[1024,128]{1,0:T(8,128)(2,1)S(1)} %collective-permute-done.refs_0_), channel_id=1, source_target_pairs={{0,4},{1,5},{2,6},{3,7},{4,0},{5,1},{6,2},{7,3},{8,12},{9,13},{10,... | collective-permute-start | bytes 786440 | tf_op jit(solution)/shard_map/ppermute | solution.py:27
  14.6 1.2 copy-done.2
  15.8 0.6 shard_map.67
  16.5 1.6 %collective-permute-start.2 = (bf16[1024,128]{1,0:T(8,128)(2,1)S(1)}, bf16[1024,128]{1,0:T(8,128)(2,1)S(1)}, u32[]{:S(2)}, u32[]{:S(2)}) collective-permute-start(bf16[1024,128]{1,0:T(8,128)(2,1)S(1)} %get-tuple-element.76), channel_id=1, source_target_pairs={{0,8},{1,9},{2,10},{3,11},{4,12},{5,13},{6,14},{7,15},{8,0},{9,1},... | collective-permute-start | bytes 786440 | tf_op jit(solution)/shard_map/ppermute | solution.py:27
  18.6 7.3 %collective-permute-done.1.refs_0_.refs_1_ = bf16[1024,128]{1,0:T(8,128)(2,1)S(1)} collective-permute-done((bf16[1024,128]{1,0:T(8,128)(2,1)S(1)}, bf16[1024,128]{1,0:T(8,128)(2,1)S(1)}, u32[]{:S(2)}, u32[]{:S(2)}) %collective-permute-start.1) | collective-permute-done | bytes 262176 | tf_op jit(solution)/shard_map/ppermute | solution.py:27
  25.9 4.5 %collective-permute-done.3.refs_1_.refs_3_ = bf16[1024,128]{1,0:T(8,128)(2,1)S(1)} collective-permute-done((bf16[1024,128]{1,0:T(8,128)(2,1)S(1)}, bf16[1024,128]{1,0:T(8,128)(2,1)S(1)}, u32[]{:S(2)}, u32[]{:S(2)}) %collective-permute-start.3) | collective-permute-done | bytes 262176 | tf_op jit(solution)/shard_map/ppermute | solution.py:27
  30.9 0.7 shard_map.69
  31.9 2.1 %shard_map.70 = (bf16[512,512]{1,0:T(8,128)(2,1)S(1)}, bf16[128,512]{1,0:T(8,128)(2,1)S(1)}, bf16[128,512]{1,0:T(8,128)(2,1)S(1)}, bf16[128,512]{1,0:T(8,128)(2,...) custom-call(s32[4]{0:T(128)S(1)} %pad_add_fusion.ids_ref, ...), custom_call_target="tpu_custom_call" | custom-call | tf_op jit(solution)/shard_map/pallas_call | solution.py:39
  36.2 2.0 %shard_map.71 = (bf16[1024,128]{1,0:T(8,128)(2,1)S(1)}, bf16[1024,128]{1,0:T(8,128)(2,1)S(1)}, bf16[1024,128]{1,0:T(8,128)(2,1)S(1)}, bf16[1024,128]{1,0:T(8,128...) custom-call(s32[4]{0:T(128)S(1)} %pad_add_fusion.ids_ref, ...), custom_call_target="tpu_custom_call" | custom-call | tf_op jit(solution)/shard_map/pallas_call | solution.py:39
  38.7 1.5 %collective-permute-start.10 = (bf16[1024,128]{1,0:T(8,128)(2,1)S(1)}, bf16[1024,128]{1,0:T(8,128)(2,1)S(1)}, u32[]{:S(2)}, u32[]{:S(2)}) collective-permute-start(bf16[1024,128]{1,0:T(8,128)(2,1)S(1)} %get-tuple-element.89), channel_id=1, source_target_pairs={{0,8},{1,9},{2,10},{3,11},{4,12},{5,13},{6,14},{7,15},{8,0},{9,1},... | collective-permute-start | bytes 786440 | tf_op jit(solution)/shard_map/ppermute | solution.py:27
  40.7 6.6 %collective-permute-done.9.refs_1_ = bf16[1024,128]{1,0:T(8,128)(2,1)S(1)} collective-permute-done((bf16[1024,128]{1,0:T(8,128)(2,1)S(1)}, bf16[1024,128]{1,0:T(8,128)(2,1)S(1)}, u32[]{:S(2)}, u32[]{:S(2)}) %collective-permute-start.9) | collective-permute-done | bytes 262176 | tf_op jit(solution)/shard_map/ppermute | solution.py:27
  47.3 5.6 %collective-permute-done.10.refs_2_.refs_3_ = bf16[1024,128]{1,0:T(8,128)(2,1)S(1)} collective-permute-done((bf16[1024,128]{1,0:T(8,128)(2,1)S(1)}, bf16[1024,128]{1,0:T(8,128)(2,1)S(1)}, u32[]{:S(2)}, u32[]{:S(2)}) %collective-permute-start.10) | collective-permute-done | bytes 262176 | tf_op jit(solution)/shard_map/ppermute | solution.py:27
  52.9 3.6 %collective-permute-done.11.refs_0_.refs_1_ = bf16[2048,128]{1,0:T(8,128)(2,1)S(1)} collective-permute-done((bf16[2048,128]{1,0:T(8,128)(2,1)S(1)}, bf16[2048,128]{1,0:T(8,128)(2,1)S(1)}, u32[]{:S(2)}, u32[]{:S(2)}) %collective-permute-start.11) | collective-permute-done | bytes 524320 | tf_op jit(solution)/shard_map/ppermute | solution.py:27
  57.1 0.6 shard_map.73
  58.0 3.9 %shard_map.74 = (bf16[512,512]{1,0:T(8,128)(2,1)S(1)}, bf16[128,512]{1,0:T(8,128)(2,1)S(1)}, bf16[128,512]{1,0:T(8,128)(2,1)S(1)}, bf16[128,512]{1,0:T(8,128)(2,...) custom-call(s32[4]{0:T(128)S(1)} %pad_add_fusion.ids_ref, ...), custom_call_target="tpu_custom_call" | custom-call | tf_op jit(solution)/shard_map/pallas_call | solution.py:39
  62.4 0.7 collective-permute-start.12
  63.1 3.7 %collective-permute-start.13 = (bf16[2048,128]{1,0:T(8,128)(2,1)S(1)}, bf16[2048,128]{1,0:T(8,128)(2,1)S(1)}, u32[]{:S(2)}, u32[]{:S(2)}) collective-permute-start(bf16[2048,128]{1,0:T(8,128)(2,1)S(1)} %get-tuple-element.93), channel_id=1, source_target_pairs={{0,1},{1,4},{2,3},{3,6},{4,5},{5,0},{6,7},{7,2},{8,9},{9,12},{10,1... | collective-permute-start | bytes 1572872 | tf_op jit(solution)/shard_map/ppermute | solution.py:27
  67.4 0.7 shard_map.75
  68.9 3.7 %shard_map.76 = (bf16[1024,128]{1,0:T(8,128)(2,1)S(1)}, bf16[1024,128]{1,0:T(8,128)(2,1)S(1)}, bf16[1024,128]{1,0:T(8,128)(2,1)S(1)}, bf16[1024,128]{1,0:T(8,128...) custom-call(s32[4]{0:T(128)S(1)} %pad_add_fusion.ids_ref, ...), custom_call_target="tpu_custom_call" | custom-call | tf_op jit(solution)/shard_map/pallas_call | solution.py:39
  73.2 1.6 %collective-permute-start.22 = (bf16[1024,128]{1,0:T(8,128)(2,1)S(1)}, bf16[1024,128]{1,0:T(8,128)(2,1)S(1)}, u32[]{:S(2)}, u32[]{:S(2)}) collective-permute-start(bf16[1024,128]{1,0:T(8,128)(2,1)S(1)} %get-tuple-element.113), channel_id=1, source_target_pairs={{0,8},{1,9},{2,10},{3,11},{4,12},{5,13},{6,14},{7,15},{8,0},{9,1},... | collective-permute-start | bytes 786440 | tf_op jit(solution)/shard_map/ppermute | solution.py:27
  74.7 1.5 %collective-permute-start.24 = (bf16[2048,128]{1,0:T(8,128)(2,1)S(1)}, bf16[2048,128]{1,0:T(8,128)(2,1)S(1)}, u32[]{:S(2)}, u32[]{:S(2)}) collective-permute-start(bf16[2048,128]{1,0:T(8,128)(2,1)S(1)} %get-tuple-element.119), channel_id=1, source_target_pairs={{0,16},{1,17},{2,18},{3,19},{4,20},{5,21},{6,22},{7,23},{8,24},{9,... | collective-permute-start | bytes 1572872 | tf_op jit(solution)/shard_map/ppermute | solution.py:27
  76.2 5.6 %collective-permute-done.21.refs_1_.refs_0_ = bf16[1024,128]{1,0:T(8,128)(2,1)S(1)} collective-permute-done((bf16[1024,128]{1,0:T(8,128)(2,1)S(1)}, bf16[1024,128]{1,0:T(8,128)(2,1)S(1)}, u32[]{:S(2)}, u32[]{:S(2)}) %collective-permute-start.21) | collective-permute-done | bytes 262176 | tf_op jit(solution)/shard_map/ppermute | solution.py:27
  81.8 5.1 %collective-permute-done.22.refs_3_.refs_1_ = bf16[1024,128]{1,0:T(8,128)(2,1)S(1)} collective-permute-done((bf16[1024,128]{1,0:T(8,128)(2,1)S(1)}, bf16[1024,128]{1,0:T(8,128)(2,1)S(1)}, u32[]{:S(2)}, u32[]{:S(2)}) %collective-permute-start.22) | collective-permute-done | bytes 262176 | tf_op jit(solution)/shard_map/ppermute | solution.py:27
  87.5 2.8 %collective-permute-done.13.refs_1_ = bf16[2048,128]{1,0:T(8,128)(2,1)S(1)} collective-permute-done((bf16[2048,128]{1,0:T(8,128)(2,1)S(1)}, bf16[2048,128]{1,0:T(8,128)(2,1)S(1)}, u32[]{:S(2)}, u32[]{:S(2)}) %collective-permute-start.13) | collective-permute-done | bytes 524320 | tf_op jit(solution)/shard_map/ppermute | solution.py:27
  90.9 0.7 shard_map.79
  91.6 1.6 %collective-permute-start.23 = (bf16[2048,128]{1,0:T(8,128)(2,1)S(1)}, bf16[2048,128]{1,0:T(8,128)(2,1)S(1)}, u32[]{:S(2)}, u32[]{:S(2)}) collective-permute-start(bf16[2048,128]{1,0:T(8,128)(2,1)S(1)} %get-tuple-element.117), channel_id=1, source_target_pairs={{0,16},{1,17},{2,18},{3,19},{4,20},{5,21},{6,22},{7,23},{8,24},{9,... | collective-permute-start | bytes 1572872 | tf_op jit(solution)/shard_map/ppermute | solution.py:27
  93.2 0.7 collective-permute-start.31
  94.8 0.6 shard_map.81
  96.0 1.4 %collective-permute-start.29 = (bf16[512,128]{1,0:T(8,128)(2,1)S(1)}, bf16[512,128]{1,0:T(8,128)(2,1)S(1)}, u32[]{:S(2)}, u32[]{:S(2)}) collective-permute-start(bf16[512,128]{1,0:T(8,128)(2,1)S(1)} %get-tuple-element.128), channel_id=1, source_target_pairs={{0,2},{1,3},{2,0},{3,1},{4,6},{5,7},{6,4},{7,5},{8,10},{9,11},{10,... | collective-permute-start | bytes 393224 | tf_op jit(solution)/shard_map/ppermute | solution.py:27
  97.5 4.8 %collective-permute-done.23.refs_1_ = bf16[2048,128]{1,0:T(8,128)(2,1)S(1)} collective-permute-done((bf16[2048,128]{1,0:T(8,128)(2,1)S(1)}, bf16[2048,128]{1,0:T(8,128)(2,1)S(1)}, u32[]{:S(2)}, u32[]{:S(2)}) %collective-permute-start.23) | collective-permute-done | bytes 524320 | tf_op jit(solution)/shard_map/ppermute | solution.py:27
  102.3 1.6 %collective-permute-start.30 = (bf16[512,128]{1,0:T(8,128)(2,1)S(1)}, bf16[512,128]{1,0:T(8,128)(2,1)S(1)}, u32[]{:S(2)}, u32[]{:S(2)}) collective-permute-start(bf16[512,128]{1,0:T(8,128)(2,1)S(1)} %get-tuple-element.129), channel_id=1, source_target_pairs={{0,10},{1,11},{2,8},{3,9},{4,14},{5,15},{6,12},{7,13},{8,2},{9,3},... | collective-permute-start | bytes 393224 | tf_op jit(solution)/shard_map/ppermute | solution.py:27
  103.9 0.7 shard_map.82
  104.6 1.5 %collective-permute-start.25 = (bf16[512,128]{1,0:T(8,128)(2,1)S(1)}, bf16[512,128]{1,0:T(8,128)(2,1)S(1)}, u32[]{:S(2)}, u32[]{:S(2)}) collective-permute-start(bf16[512,128]{1,0:T(8,128)(2,1)S(1)} %get-tuple-element.123), channel_id=1, source_target_pairs={{0,8},{1,9},{2,10},{3,11},{4,12},{5,13},{6,14},{7,15},{8,0},{9,1},... | collective-permute-start | bytes 393224 | tf_op jit(solution)/shard_map/ppermute | solution.py:27
  106.5 3.3 %collective-permute-done.30.refs_3_ = bf16[512,128]{1,0:T(8,128)(2,1)S(1)} collective-permute-done((bf16[512,128]{1,0:T(8,128)(2,1)S(1)}, bf16[512,128]{1,0:T(8,128)(2,1)S(1)}, u32[]{:S(2)}, u32[]{:S(2)}) %collective-permute-start.30) | collective-permute-done | bytes 131104 | tf_op jit(solution)/shard_map/ppermute | solution.py:27
  109.8 1.4 %collective-permute-start.27 = (bf16[512,128]{1,0:T(8,128)(2,1)S(1)}, bf16[512,128]{1,0:T(8,128)(2,1)S(1)}, u32[]{:S(2)}, u32[]{:S(2)}) collective-permute-start(bf16[512,128]{1,0:T(8,128)(2,1)S(1)} %get-tuple-element.125), channel_id=1, source_target_pairs={{0,10},{1,11},{2,8},{3,9},{4,14},{5,15},{6,12},{7,13},{8,2},{9,3},... | collective-permute-start | bytes 393224 | tf_op jit(solution)/shard_map/ppermute | solution.py:27
  111.2 0.6 shard_map.83
  111.8 2.4 %collective-permute-start.33 = (bf16[256,128]{1,0:T(8,128)(2,1)S(1)}, bf16[256,128]{1,0:T(8,128)(2,1)S(1)}, u32[]{:S(2)}, u32[]{:S(2)}) collective-permute-start(bf16[256,128]{1,0:T(8,128)(2,1)S(1)} %get-tuple-element.139), channel_id=1, source_target_pairs={{0,4},{1,5},{2,6},{3,7},{4,0},{5,1},{6,2},{7,3},{8,12},{9,13},{10,... | collective-permute-start | bytes 196616 | tf_op jit(solution)/shard_map/ppermute | solution.py:27
  114.3 7.0 %collective-permute-done.27.refs_3_ = bf16[512,128]{1,0:T(8,128)(2,1)S(1)} collective-permute-done((bf16[512,128]{1,0:T(8,128)(2,1)S(1)}, bf16[512,128]{1,0:T(8,128)(2,1)S(1)}, u32[]{:S(2)}, u32[]{:S(2)}) %collective-permute-start.27) | collective-permute-done | bytes 131104 | tf_op jit(solution)/shard_map/ppermute | solution.py:27
  121.2 0.6 shard_map.84
  121.8 2.7 %collective-permute-start.34 = (bf16[256,128]{1,0:T(8,128)(2,1)S(1)}, bf16[256,128]{1,0:T(8,128)(2,1)S(1)}, u32[]{:S(2)}, u32[]{:S(2)}) collective-permute-start(bf16[256,128]{1,0:T(8,128)(2,1)S(1)} %get-tuple-element.143), channel_id=1, source_target_pairs={{0,4},{1,5},{2,6},{3,7},{4,0},{5,1},{6,2},{7,3},{8,12},{9,13},{10,... | collective-permute-start | bytes 196616 | tf_op jit(solution)/shard_map/ppermute | solution.py:27
  124.5 1.5 %shard_map.85 = (bf16[4096,128]{1,0:T(8,128)(2,1)}, f32[8,128]{1,0:T(8,128)S(1)}) custom-call(s32[4]{0:T(128)S(1)} %pad_add_fusion.ids_ref, bf16[2048,128]{1,0:T(8,128)(2,1)S(1)} %collective-permute-done.12.refs_0_, bf16[2048,128]{1,0:T(8,128)(2,1)S(1)} %collective-permute-done.13.refs_1_, f32[8,128]{1,0:T(8,128)S(1)} %get-tuple-element.132.refs_2_), custom_call_target="tpu_custom_call" | custom-call | tf_op jit(solution)/shard_map/pallas_call | solution.py:39
  126.1 1.5 %shard_map.86 = (bf16[4096,128]{1,0:T(8,128)(2,1)}, f32[8,128]{1,0:T(8,128)S(1)}) custom-call(s32[4]{0:T(128)S(1)} %pad_add_fusion.ids_ref, bf16[2048,128]{1,0:T(8,128)(2,1)S(1)} %collective-permute-done.31.refs_0_, bf16[2048,128]{1,0:T(8,128)(2,1)S(1)} %collective-permute-done.32.refs_1_, f32[8,128]{1,0:T(8,128)S(1)} %get-tuple-element.136.refs_2_), custom_call_target="tpu_custom_call" | custom-call | tf_op jit(solution)/shard_map/pallas_call | solution.py:39
  127.7 1.2 shard_map.87
  128.9 1.2 shard_map.88
  (53 shorter events, 11.6 us)
Async XLA Ops:
  0.6 14.0 %copy-start.1 = (bf16[524288]{0:T(1024)(128)(2,1)S(1)}, bf16[524288]{0:T(1024)(128)(2,1)}, u32[]{:S(2)}) copy-start(bf16[524288]{0:T(1024)(128)(2,1)} %param.4) | copy-start | bytes 3145732
  1.8 9.3 %collective-permute-start = (bf16[1024,128]{1,0:T(8,128)(2,1)S(1)}, bf16[1024,128]{1,0:T(8,128)(2,1)S(1)}, u32[]{:S(2)}, u32[]{:S(2)}) collective-permute-start(bf16[1024,128]{1,0:T(8,128)(2,1)S(1)} %get-tuple-element.147), channel_id=1, source_target_pairs={{0,8},{1,9},{2,10},{3,11},{4,12},{5,13},{6,14},{7,15},{8,0},{9,1},... | collective-permute-start | bytes 786440 | tf_op jit(solution)/shard_map/ppermute | solution.py:27
  4.8 21.1 %collective-permute-start.1 = (bf16[1024,128]{1,0:T(8,128)(2,1)S(1)}, bf16[1024,128]{1,0:T(8,128)(2,1)S(1)}, u32[]{:S(2)}, u32[]{:S(2)}) collective-permute-start(bf16[1024,128]{1,0:T(8,128)(2,1)S(1)} %get-tuple-element.146), channel_id=1, source_target_pairs={{0,4},{1,5},{2,6},{3,7},{4,0},{5,1},{6,2},{7,3},{8,12},{9,13},{10,... | collective-permute-start | bytes 786440 | tf_op jit(solution)/shard_map/ppermute | solution.py:27
  11.1 19.2 %collective-permute-start.3 = (bf16[1024,128]{1,0:T(8,128)(2,1)S(1)}, bf16[1024,128]{1,0:T(8,128)(2,1)S(1)}, u32[]{:S(2)}, u32[]{:S(2)}) collective-permute-start(bf16[1024,128]{1,0:T(8,128)(2,1)S(1)} %collective-permute-done.refs_0_), channel_id=1, source_target_pairs={{0,4},{1,5},{2,6},{3,7},{4,0},{5,1},{6,2},{7,3},{8,12},{9,13},{10,... | collective-permute-start | bytes 786440 | tf_op jit(solution)/shard_map/ppermute | solution.py:27
  14.6 1.2 copy-start.2
  16.5 15.2 %collective-permute-start.2 = (bf16[1024,128]{1,0:T(8,128)(2,1)S(1)}, bf16[1024,128]{1,0:T(8,128)(2,1)S(1)}, u32[]{:S(2)}, u32[]{:S(2)}) collective-permute-start(bf16[1024,128]{1,0:T(8,128)(2,1)S(1)} %get-tuple-element.76), channel_id=1, source_target_pairs={{0,8},{1,9},{2,10},{3,11},{4,12},{5,13},{6,14},{7,15},{8,0},{9,1},... | collective-permute-start | bytes 786440 | tf_op jit(solution)/shard_map/ppermute | solution.py:27
  18.0 12.9 %collective-permute-start.4 = (bf16[1024,128]{1,0:T(8,128)(2,1)S(1)}, bf16[1024,128]{1,0:T(8,128)(2,1)S(1)}, u32[]{:S(2)}, u32[]{:S(2)}) collective-permute-start(bf16[1024,128]{1,0:T(8,128)(2,1)S(1)} %get-tuple-element.77), channel_id=1, source_target_pairs={{0,8},{1,9},{2,10},{3,11},{4,12},{5,13},{6,14},{7,15},{8,0},{9,1},... | collective-permute-start | bytes 786440 | tf_op jit(solution)/shard_map/ppermute | solution.py:27
  30.3 1.6 %copy-start = (bf16[1024,1024]{1,0:T(8,128)(2,1)S(1)}, bf16[1024,1024]{1,0:T(8,128)(2,1)}, u32[]{:S(2)}) copy-start(bf16[1024,1024]{1,0:T(8,128)(2,1)} %refs_6_.1) | copy-start | bytes 6291460
  31.6 25.0 %collective-permute-start.11 = (bf16[2048,128]{1,0:T(8,128)(2,1)S(1)}, bf16[2048,128]{1,0:T(8,128)(2,1)S(1)}, u32[]{:S(2)}, u32[]{:S(2)}) collective-permute-start(bf16[2048,128]{1,0:T(8,128)(2,1)S(1)} %get-tuple-element.90), channel_id=1, source_target_pairs={{0,4},{1,5},{2,6},{3,7},{4,0},{5,1},{6,2},{7,3},{8,12},{9,13},{10,... | collective-permute-start | bytes 1572872 | tf_op jit(solution)/shard_map/ppermute | solution.py:27
  34.0 1.4 %collective-permute-start.5 = (bf16[128,512]{1,0:T(8,128)(2,1)S(1)}, bf16[128,512]{1,0:T(8,128)(2,1)S(1)}, u32[]{:S(2)}, u32[]{:S(2)}) collective-permute-start(bf16[128,512]{1,0:T(8,128)(2,1)S(1)} %get-tuple-element.81), channel_id=1, source_target_pairs={{0,1},{1,0},{2,3},{3,2},{4,5},{5,4},{6,7},{7,6},{8,9},{9,8},{10,11... | collective-permute-start | bytes 393224 | tf_op jit(solution)/shard_map/ppermute | solution.py:27
  34.1 1.5 %collective-permute-start.6 = (bf16[128,512]{1,0:T(8,128)(2,1)S(1)}, bf16[128,512]{1,0:T(8,128)(2,1)S(1)}, u32[]{:S(2)}, u32[]{:S(2)}) collective-permute-start(bf16[128,512]{1,0:T(8,128)(2,1)S(1)} %get-tuple-element.82), channel_id=1, source_target_pairs={{0,1},{1,0},{2,3},{3,2},{4,5},{5,4},{6,7},{7,6},{8,9},{9,8},{10,11... | collective-permute-start | bytes 393224 | tf_op jit(solution)/shard_map/ppermute | solution.py:27
  34.6 1.3 %collective-permute-start.7 = (bf16[128,512]{1,0:T(8,128)(2,1)S(1)}, bf16[128,512]{1,0:T(8,128)(2,1)S(1)}, u32[]{:S(2)}, u32[]{:S(2)}) collective-permute-start(bf16[128,512]{1,0:T(8,128)(2,1)S(1)} %get-tuple-element.83), channel_id=1, source_target_pairs={{0,1},{1,0},{2,3},{3,2},{4,5},{5,4},{6,7},{7,6},{8,9},{9,8},{10,11... | collective-permute-start | bytes 393224 | tf_op jit(solution)/shard_map/ppermute | solution.py:27
  34.7 1.5 %collective-permute-start.8 = (bf16[128,512]{1,0:T(8,128)(2,1)S(1)}, bf16[128,512]{1,0:T(8,128)(2,1)S(1)}, u32[]{:S(2)}, u32[]{:S(2)}) collective-permute-start(bf16[128,512]{1,0:T(8,128)(2,1)S(1)} %get-tuple-element.84), channel_id=1, source_target_pairs={{0,1},{1,0},{2,3},{3,2},{4,5},{5,4},{6,7},{7,6},{8,9},{9,8},{10,11... | collective-permute-start | bytes 393224 | tf_op jit(solution)/shard_map/ppermute | solution.py:27
  38.1 9.2 %collective-permute-start.9 = (bf16[1024,128]{1,0:T(8,128)(2,1)S(1)}, bf16[1024,128]{1,0:T(8,128)(2,1)S(1)}, u32[]{:S(2)}, u32[]{:S(2)}) collective-permute-start(bf16[1024,128]{1,0:T(8,128)(2,1)S(1)} %get-tuple-element.87), channel_id=1, source_target_pairs={{0,8},{1,9},{2,10},{3,11},{4,12},{5,13},{6,14},{7,15},{8,0},{9,1},... | collective-permute-start | bytes 786440 | tf_op jit(solution)/shard_map/ppermute | solution.py:27
  38.7 14.3 %collective-permute-start.10 = (bf16[1024,128]{1,0:T(8,128)(2,1)S(1)}, bf16[1024,128]{1,0:T(8,128)(2,1)S(1)}, u32[]{:S(2)}, u32[]{:S(2)}) collective-permute-start(bf16[1024,128]{1,0:T(8,128)(2,1)S(1)} %get-tuple-element.89), channel_id=1, source_target_pairs={{0,8},{1,9},{2,10},{3,11},{4,12},{5,13},{6,14},{7,15},{8,0},{9,1},... | collective-permute-start | bytes 786440 | tf_op jit(solution)/shard_map/ppermute | solution.py:27
  40.2 17.7 %collective-permute-start.14 = (bf16[1024,128]{1,0:T(8,128)(2,1)S(1)}, bf16[1024,128]{1,0:T(8,128)(2,1)S(1)}, u32[]{:S(2)}, u32[]{:S(2)}) collective-permute-start(bf16[1024,128]{1,0:T(8,128)(2,1)S(1)} %get-tuple-element.95), channel_id=1, source_target_pairs={{0,8},{1,9},{2,10},{3,11},{4,12},{5,13},{6,14},{7,15},{8,0},{9,1},... | collective-permute-start | bytes 786440 | tf_op jit(solution)/shard_map/ppermute | solution.py:27
  61.8 5.5 %collective-permute-start.19 = (bf16[4096,128]{1,0:T(8,128)(2,1)S(1)}, bf16[4096,128]{1,0:T(8,128)(2,1)S(1)}, u32[]{:S(2)}, u32[]{:S(2)}) collective-permute-start(bf16[4096,128]{1,0:T(8,128)(2,1)S(1)} %get-tuple-element.105), channel_id=1, source_target_pairs={{0,1},{1,0},{2,3},{3,2},{4,5},{5,4},{6,7},{7,6},{8,9},{9,8},{10,11... | collective-permute-start | bytes 3145736 | tf_op jit(solution)/shard_map/ppermute | solution.py:27
  61.9 5.0 %collective-permute-start.15 = (bf16[128,512]{1,0:T(8,128)(2,1)S(1)}, bf16[128,512]{1,0:T(8,128)(2,1)S(1)}, u32[]{:S(2)}, u32[]{:S(2)}) collective-permute-start(bf16[128,512]{1,0:T(8,128)(2,1)S(1)} %get-tuple-element.99), channel_id=1, source_target_pairs={{0,1},{1,0},{2,3},{3,2},{4,5},{5,4},{6,7},{7,6},{8,9},{9,8},{10,11... | collective-permute-start | bytes 393224 | tf_op jit(solution)/shard_map/ppermute | solution.py:27
  62.4 25.1 %collective-permute-start.12 = (bf16[2048,128]{1,0:T(8,128)(2,1)S(1)}, bf16[2048,128]{1,0:T(8,128)(2,1)S(1)}, u32[]{:S(2)}, u32[]{:S(2)}) collective-permute-start(bf16[2048,128]{1,0:T(8,128)(2,1)S(1)} %get-tuple-element.92), channel_id=1, source_target_pairs={{0,0},{1,5},{2,2},{3,7},{4,4},{5,1},{6,6},{7,3},{8,8},{9,13},{10,1... | collective-permute-start | bytes 1572872 | tf_op jit(solution)/shard_map/ppermute | solution.py:27
  63.1 27.2 %collective-permute-start.13 = (bf16[2048,128]{1,0:T(8,128)(2,1)S(1)}, bf16[2048,128]{1,0:T(8,128)(2,1)S(1)}, u32[]{:S(2)}, u32[]{:S(2)}) collective-permute-start(bf16[2048,128]{1,0:T(8,128)(2,1)S(1)} %get-tuple-element.93), channel_id=1, source_target_pairs={{0,1},{1,4},{2,3},{3,6},{4,5},{5,0},{6,7},{7,2},{8,9},{9,12},{10,1... | collective-permute-start | bytes 1572872 | tf_op jit(solution)/shard_map/ppermute | solution.py:27
  66.8 1.7 %collective-permute-start.16 = (bf16[128,512]{1,0:T(8,128)(2,1)S(1)}, bf16[128,512]{1,0:T(8,128)(2,1)S(1)}, u32[]{:S(2)}, u32[]{:S(2)}) collective-permute-start(bf16[128,512]{1,0:T(8,128)(2,1)S(1)} %get-tuple-element.100), channel_id=1, source_target_pairs={{0,1},{1,0},{2,3},{3,2},{4,5},{5,4},{6,7},{7,6},{8,9},{9,8},{10,11... | collective-permute-start | bytes 393224 | tf_op jit(solution)/shard_map/ppermute | solution.py:27
  66.9 1.8 %collective-permute-start.17 = (bf16[128,512]{1,0:T(8,128)(2,1)S(1)}, bf16[128,512]{1,0:T(8,128)(2,1)S(1)}, u32[]{:S(2)}, u32[]{:S(2)}) collective-permute-start(bf16[128,512]{1,0:T(8,128)(2,1)S(1)} %get-tuple-element.101), channel_id=1, source_target_pairs={{0,1},{1,0},{2,3},{3,2},{4,5},{5,4},{6,7},{7,6},{8,9},{9,8},{10,11... | collective-permute-start | bytes 393224 | tf_op jit(solution)/shard_map/ppermute | solution.py:27
  67.3 1.6 %collective-permute-start.18 = (bf16[128,512]{1,0:T(8,128)(2,1)S(1)}, bf16[128,512]{1,0:T(8,128)(2,1)S(1)}, u32[]{:S(2)}, u32[]{:S(2)}) collective-permute-start(bf16[128,512]{1,0:T(8,128)(2,1)S(1)} %get-tuple-element.102), channel_id=1, source_target_pairs={{0,1},{1,0},{2,3},{3,2},{4,5},{5,4},{6,7},{7,6},{8,9},{9,8},{10,11... | collective-permute-start | bytes 393224 | tf_op jit(solution)/shard_map/ppermute | solution.py:27
  72.6 9.2 %collective-permute-start.21 = (bf16[1024,128]{1,0:T(8,128)(2,1)S(1)}, bf16[1024,128]{1,0:T(8,128)(2,1)S(1)}, u32[]{:S(2)}, u32[]{:S(2)}) collective-permute-start(bf16[1024,128]{1,0:T(8,128)(2,1)S(1)} %get-tuple-element.111), channel_id=1, source_target_pairs={{0,8},{1,9},{2,10},{3,11},{4,12},{5,13},{6,14},{7,15},{8,0},{9,1},... | collective-permute-start | bytes 786440 | tf_op jit(solution)/shard_map/ppermute | solution.py:27
  73.2 13.7 %collective-permute-start.22 = (bf16[1024,128]{1,0:T(8,128)(2,1)S(1)}, bf16[1024,128]{1,0:T(8,128)(2,1)S(1)}, u32[]{:S(2)}, u32[]{:S(2)}) collective-permute-start(bf16[1024,128]{1,0:T(8,128)(2,1)S(1)} %get-tuple-element.113), channel_id=1, source_target_pairs={{0,8},{1,9},{2,10},{3,11},{4,12},{5,13},{6,14},{7,15},{8,0},{9,1},... | collective-permute-start | bytes 786440 | tf_op jit(solution)/shard_map/ppermute | solution.py:27
  74.7 20.1 %collective-permute-start.24 = (bf16[2048,128]{1,0:T(8,128)(2,1)S(1)}, bf16[2048,128]{1,0:T(8,128)(2,1)S(1)}, u32[]{:S(2)}, u32[]{:S(2)}) collective-permute-start(bf16[2048,128]{1,0:T(8,128)(2,1)S(1)} %get-tuple-element.119), channel_id=1, source_target_pairs={{0,16},{1,17},{2,18},{3,19},{4,20},{5,21},{6,22},{7,23},{8,24},{9,... | collective-permute-start | bytes 1572872 | tf_op jit(solution)/shard_map/ppermute | solution.py:27
  81.8 9.0 %collective-permute-start.20 = (bf16[4096,128]{1,0:T(8,128)(2,1)S(1)}, bf16[4096,128]{1,0:T(8,128)(2,1)S(1)}, u32[]{:S(2)}, u32[]{:S(2)}) collective-permute-start(bf16[4096,128]{1,0:T(8,128)(2,1)S(1)} %get-tuple-element.109), channel_id=1, source_target_pairs={{0,1},{1,0},{2,3},{3,2},{4,5},{5,4},{6,7},{7,6},{8,9},{9,8},{10,11... | collective-permute-start | bytes 3145736 | tf_op jit(solution)/shard_map/ppermute | solution.py:27
  91.6 10.7 %collective-permute-start.23 = (bf16[2048,128]{1,0:T(8,128)(2,1)S(1)}, bf16[2048,128]{1,0:T(8,128)(2,1)S(1)}, u32[]{:S(2)}, u32[]{:S(2)}) collective-permute-start(bf16[2048,128]{1,0:T(8,128)(2,1)S(1)} %get-tuple-element.117), channel_id=1, source_target_pairs={{0,16},{1,17},{2,18},{3,19},{4,20},{5,21},{6,22},{7,23},{8,24},{9,... | collective-permute-start | bytes 1572872 | tf_op jit(solution)/shard_map/ppermute | solution.py:27
  93.2 32.9 %collective-permute-start.31 = (bf16[2048,128]{1,0:T(8,128)(2,1)S(1)}, bf16[2048,128]{1,0:T(8,128)(2,1)S(1)}, u32[]{:S(2)}, u32[]{:S(2)}) collective-permute-start(bf16[2048,128]{1,0:T(8,128)(2,1)S(1)} %get-tuple-element.134), channel_id=1, source_target_pairs={{0,0},{1,5},{2,2},{3,7},{4,4},{5,1},{6,6},{7,3},{8,8},{9,13},{10,1... | collective-permute-start | bytes 1572872 | tf_op jit(solution)/shard_map/ppermute | solution.py:27
  93.9 32.2 %collective-permute-start.32 = (bf16[2048,128]{1,0:T(8,128)(2,1)S(1)}, bf16[2048,128]{1,0:T(8,128)(2,1)S(1)}, u32[]{:S(2)}, u32[]{:S(2)}) collective-permute-start(bf16[2048,128]{1,0:T(8,128)(2,1)S(1)} %get-tuple-element.135), channel_id=1, source_target_pairs={{0,1},{1,4},{2,3},{3,6},{4,5},{5,0},{6,7},{7,2},{8,9},{9,12},{10,1... | collective-permute-start | bytes 1572872 | tf_op jit(solution)/shard_map/ppermute | solution.py:27
  95.4 9.1 %collective-permute-start.28 = (bf16[512,128]{1,0:T(8,128)(2,1)S(1)}, bf16[512,128]{1,0:T(8,128)(2,1)S(1)}, u32[]{:S(2)}, u32[]{:S(2)}) collective-permute-start(bf16[512,128]{1,0:T(8,128)(2,1)S(1)} %get-tuple-element.127), channel_id=1, source_target_pairs={{0,8},{1,9},{2,10},{3,11},{4,12},{5,13},{6,14},{7,15},{8,0},{9,1},... | collective-permute-start | bytes 393224 | tf_op jit(solution)/shard_map/ppermute | solution.py:27
  96.0 10.1 %collective-permute-start.29 = (bf16[512,128]{1,0:T(8,128)(2,1)S(1)}, bf16[512,128]{1,0:T(8,128)(2,1)S(1)}, u32[]{:S(2)}, u32[]{:S(2)}) collective-permute-start(bf16[512,128]{1,0:T(8,128)(2,1)S(1)} %get-tuple-element.128), channel_id=1, source_target_pairs={{0,2},{1,3},{2,0},{3,1},{4,6},{5,7},{6,4},{7,5},{8,10},{9,11},{10,... | collective-permute-start | bytes 393224 | tf_op jit(solution)/shard_map/ppermute | solution.py:27
  102.3 7.6 %collective-permute-start.30 = (bf16[512,128]{1,0:T(8,128)(2,1)S(1)}, bf16[512,128]{1,0:T(8,128)(2,1)S(1)}, u32[]{:S(2)}, u32[]{:S(2)}) collective-permute-start(bf16[512,128]{1,0:T(8,128)(2,1)S(1)} %get-tuple-element.129), channel_id=1, source_target_pairs={{0,10},{1,11},{2,8},{3,9},{4,14},{5,15},{6,12},{7,13},{8,2},{9,3},... | collective-permute-start | bytes 393224 | tf_op jit(solution)/shard_map/ppermute | solution.py:27
  104.6 7.3 %collective-permute-start.25 = (bf16[512,128]{1,0:T(8,128)(2,1)S(1)}, bf16[512,128]{1,0:T(8,128)(2,1)S(1)}, u32[]{:S(2)}, u32[]{:S(2)}) collective-permute-start(bf16[512,128]{1,0:T(8,128)(2,1)S(1)} %get-tuple-element.123), channel_id=1, source_target_pairs={{0,8},{1,9},{2,10},{3,11},{4,12},{5,13},{6,14},{7,15},{8,0},{9,1},... | collective-permute-start | bytes 393224 | tf_op jit(solution)/shard_map/ppermute | solution.py:27
  106.1 8.2 %collective-permute-start.26 = (bf16[512,128]{1,0:T(8,128)(2,1)S(1)}, bf16[512,128]{1,0:T(8,128)(2,1)S(1)}, u32[]{:S(2)}, u32[]{:S(2)}) collective-permute-start(bf16[512,128]{1,0:T(8,128)(2,1)S(1)} %get-tuple-element.124), channel_id=1, source_target_pairs={{0,2},{1,3},{2,0},{3,1},{4,6},{5,7},{6,4},{7,5},{8,10},{9,11},{10,... | collective-permute-start | bytes 393224 | tf_op jit(solution)/shard_map/ppermute | solution.py:27
  109.8 11.4 %collective-permute-start.27 = (bf16[512,128]{1,0:T(8,128)(2,1)S(1)}, bf16[512,128]{1,0:T(8,128)(2,1)S(1)}, u32[]{:S(2)}, u32[]{:S(2)}) collective-permute-start(bf16[512,128]{1,0:T(8,128)(2,1)S(1)} %get-tuple-element.125), channel_id=1, source_target_pairs={{0,10},{1,11},{2,8},{3,9},{4,14},{5,15},{6,12},{7,13},{8,2},{9,3},... | collective-permute-start | bytes 393224 | tf_op jit(solution)/shard_map/ppermute | solution.py:27
  111.8 15.8 %collective-permute-start.33 = (bf16[256,128]{1,0:T(8,128)(2,1)S(1)}, bf16[256,128]{1,0:T(8,128)(2,1)S(1)}, u32[]{:S(2)}, u32[]{:S(2)}) collective-permute-start(bf16[256,128]{1,0:T(8,128)(2,1)S(1)} %get-tuple-element.139), channel_id=1, source_target_pairs={{0,4},{1,5},{2,6},{3,7},{4,0},{5,1},{6,2},{7,3},{8,12},{9,13},{10,... | collective-permute-start | bytes 196616 | tf_op jit(solution)/shard_map/ppermute | solution.py:27
  121.8 7.1 %collective-permute-start.34 = (bf16[256,128]{1,0:T(8,128)(2,1)S(1)}, bf16[256,128]{1,0:T(8,128)(2,1)S(1)}, u32[]{:S(2)}, u32[]{:S(2)}) collective-permute-start(bf16[256,128]{1,0:T(8,128)(2,1)S(1)} %get-tuple-element.143), channel_id=1, source_target_pairs={{0,4},{1,5},{2,6},{3,7},{4,0},{5,1},{6,2},{7,3},{8,12},{9,13},{10,... | collective-permute-start | bytes 196616 | tf_op jit(solution)/shard_map/ppermute | solution.py:27

commit v3 on v2

--- a/solution.py
+++ b/solution.py
@@ -10,7 +10,7 @@
 
 AXES = ("row", "col")
 LANES = 128
-KNOBS = {'waits': {'take2': ['Z1', 'Z2'], 'f_pack': ['Z3', 'f_X'], 'F2_0': ['f_near'], 'F1_1': ['a_X']}, 'lead': {'take2': 20000000000, 'F2_0': 12000000000}, 'free': ['take2'], 'out_f': 'packed', 'core_cuts': 4, 'env_cuts': 1, 'plan': '1G21212fa12', 'out_a': 'packed'}
+KNOBS = {'out_f': 'packed', 'out_a': 'packed', 'plan': '1G2p12fJaE', 'free': ['take2', 'F2_0', 'GE2', 'F12_2'], 'cuts': {'G1f': 4}, 'order': 'y,xz,z', 'waits': {'take2': ['Z1', 'Z2'], 'f_pack': ['Z3', 'f_X'], 'F2_0': ['f_near'], 'GE2': ['f_X']}, 'lead': {'take2': 20000000000, 'F2_0': 20000000000, 'GE2': 20000000000, 'F12_2': 20000000000}}
 
 
 SMEM = pl.BlockSpec(memory_space=pltpu.SMEM)
@@ -18,8 +18,7 @@
 HBM = pl.BlockSpec(memory_space=pltpu.HBM)
 ANY = pl.BlockSpec(memory_space=pl.ANY)
 VMEM_BYTES = 16 * 2**20
-CORE_CUTS = KNOBS.get("core_cuts", 1)
-ENV_CUTS = KNOBS.get("env_cuts", 1)
+ENV_CUTS = 1
 
 
 def sent(value, target):
@@ -112,19 +111,13 @@
     return call(kernel, shapes, ids, pieces, after, scratch, raw_out=[0])
 
 
-def pack(ids, groups, after):
-    arrays = [one for group in groups for one in group]
-
+def pack(ids, rows, arrays, groups, after):
     def kernel(ids, ins, outs):
-        count = 0
         for group, out in zip(groups, outs, strict=True):
-            row = 0
-            for one in group:
-                out[row : row + one.shape[0], :] = ins[count][...]
-                row += one.shape[0]
-                count += 1
-
-    shapes = [jax.ShapeDtypeStruct((sum(one.shape[0] for one in group), LANES), group[0].dtype) for group in groups]
+            for n, (k, at) in enumerate(group):
+                out[n * rows : (n + 1) * rows, :] = ins[k][at * rows : (at + 1) * rows, :]
+
+    shapes = [jax.ShapeDtypeStruct((len(group) * rows, LANES), arrays[0].dtype) for group in groups]
     return call(kernel, shapes, ids, arrays, after)
 
 
@@ -152,7 +145,7 @@
 
 def gate_kernel(block, linear, sizes, env, in_place, out_place, ids, ins, results, moved_ref, *refs):
     in_ref, out_ref = in_place(ids), out_place(ids)
-    n_out = 4 if sizes is None else len(sizes)
+    n_out = (4 if env is None else 3) if sizes is None else len(sizes)
     outs = results[:n_out]
     spread = refs[0]
     if env is None:
@@ -172,7 +165,9 @@
         if sizes is None:
             for c in range(ratio):
                 spread[pl.ds(c, block, stride=ratio), :] = total[:, c * LANES : (c + 1) * LANES]
-            outs[m][...] = spread[...].astype(jnp.bfloat16)
+            out, lines = outs[min(m, n_out - 1)], spread.shape[0]
+            row = lines if m >= n_out else 0
+            out[row : row + lines, :] = spread[...].astype(jnp.bfloat16)
             continue
         row = 0
         for out in outs:
@@ -211,6 +206,8 @@
     block = gate // 4
     rows = block * width // LANES
     shapes = [jax.ShapeDtypeStruct((rows, LANES), jnp.bfloat16)] * 4
+    if sizes is None and env is not None:
+        shapes = shapes[:2] + [jax.ShapeDtypeStruct((2 * rows, LANES), jnp.bfloat16)]
     if sizes is not None:
         shapes = [jax.ShapeDtypeStruct((size, width), jnp.bfloat16) for size in sizes]
     n_out = len(shapes)
@@ -233,40 +230,48 @@
     return got[:n_out], got[n_out:], token
 
 
-def fold(ids, base, incoming, left, group, unit, after, work=0):
+def fold(ids, sums, count, left, group, unit, after, work=0):
     lead = [bit for bit in left if bit not in group]
     stride = {bit: unit << (len(left) - 1 - n) for n, bit in enumerate(left)}
     flips = [sum(((k >> n) & 1) << bit for n, bit in enumerate(group)) for k in range(2 ** len(group))]
     rows = unit << len(lead)
-
-    arrays = [piece for one in incoming for piece in one]
+    arrays = [one for base, incoming in sums for one in [base, *incoming]]
 
     def kernel(ids, ins, outs):
-        def summed(at):
-            value = ins[0][at, :]
-            count = 1
-            for one in incoming:
-                per = one[0].shape[0]
-                start = at.start
-                inside = pl.ds(start - start // per * per if len(one) > 1 else start, unit)
-                inside = pl.ds(pl.multiple_of(inside.start, unit), unit) if group else inside
-                part = ins[count][inside, :].astype(jnp.float32)
-                for k in range(1, len(one)):
-                    part = jnp.where(start // per == k, ins[count + k][inside, :].astype(jnp.float32), part)
-                value = value + part
-                count += len(one)
-            return value
-
-        for n in sorted(range(len(flips)), key=lambda n: n == 0):
-            origin = sum((((ids[3] ^ flips[n]) >> bit) & 1) * stride[bit] for bit in group)
-            for k in range(2 ** len(lead)):
-                shift = sum(((k >> (len(lead) - 1 - i)) & 1) * stride[bit] for i, bit in enumerate(lead))
-                at = pl.ds(pl.multiple_of(origin + shift, unit), unit) if group else pl.ds(shift, unit)
-                outs[n][k * unit : (k + 1) * unit, :] = summed(at).astype(outs[n].dtype)
-
-    shapes = [jax.ShapeDtypeStruct((rows, LANES), jnp.float32 if flip == 0 else jnp.bfloat16) for flip in flips]
-    (own, *pieces), token = call(kernel, shapes, ids, [base, *arrays], after, work=work)
+        for flip, out in sorted(zip(flips, outs, strict=True), key=lambda one: one[0] == 0):
+            origin = sum((((ids[3] ^ flip) >> bit) & 1) * stride[bit] for bit in group)
+            refs = list(ins)
+            for n in range(len(sums) * count):
+                if n % count == 0:
+                    mine, refs = refs[: 1 + len(sums[n // count][1])], refs[1 + len(sums[n // count][1]) :]
+                first = n % count * (unit << len(left))
+                for k in range(2 ** len(lead)):
+                    shift = sum(((k >> (len(lead) - 1 - i)) & 1) * stride[bit] for i, bit in enumerate(lead))
+                    at = pl.ds(pl.multiple_of(first + origin + shift, unit), unit)
+                    value = mine[0][at, :]
+                    for one in mine[1:]:
+                        value = value + one[at, :].astype(jnp.float32)
+                    out[n * rows + k * unit : n * rows + (k + 1) * unit, :] = value.astype(out.dtype)
+
+    shapes = [
+        jax.ShapeDtypeStruct((len(sums) * count * rows, LANES), jnp.float32 if flip == 0 else jnp.bfloat16) for flip in flips
+    ]
+    (own, *pieces), token = call(kernel, shapes, ids, arrays, after, work=work)
     return own, pieces, flips[1:], token
+
+
+def add_up(ids, base, incoming, count, after):
+    rows = base.shape[0] // count
+
+    def kernel(ids, ins, outs):
+        for n, out in enumerate(outs):
+            value = ins[0][n * rows : (n + 1) * rows, :]
+            for one in ins[1:]:
+                value = value + one[n * rows : (n + 1) * rows, :].astype(jnp.float32)
+            out[...] = value
+
+    shapes = [jax.ShapeDtypeStruct((rows, LANES), base.dtype)] * count
+    return call(kernel, shapes, ids, [base, *incoming], after)
 
 
 def on_device(forward_state, adjoint_state, gate_matrix):
@@ -366,7 +371,8 @@
         return [(ids[0] ^ i) * 2 + (ids[2] ^ j) for i in range(2) for j in range(2)]
 
     def first_gate(name, blocks, place, env=None):
-        sizes = [half] + [half // CORE_CUTS] * CORE_CUTS
+        cuts = KNOBS.get("cuts", {}).get(name, 1)
+        sizes = [half] + [half // cuts] * cuts
         (keep, *send), extra, token = apply_gate(
             ids, gate_matrix, blocks, place, first_out, width, True, sizes, gates(name), env, work(name)
         )
@@ -389,22 +395,26 @@
     def by_flip(ids):
         return [final_place(ids, i, flip) for flip in range(2) for i in range(2)]
 
+    def cross(name, out):
+        flight[name + "_X"] = [across_x(one) for one in out[2:]]
+
     def leave(name, out):
         style = KNOBS.get("out_" + name, "direct")
-        flight[name + "_X"] = [across_x(one) for one in out[2:]]
         if style == "packed":
-            packed, token = pack(ids, [[out[k], flight[name + "_X"][k]] for k in range(2)], gates(name + "_pack"))
+            joined = len(out) == 3
+            groups = [[(k, 0), (2, k) if joined else (2 + k, 0)] for k in range(2)]
+            packed, token = pack(ids, quarter, [*out[:2], *flight[name + "_X"]], groups, gates(name + "_pack"))
             link(token)
             flight[name + "_near"] = flight[name + "_far"] = [home(one, flip) for flip, one in enumerate(packed)]
             return
         near = out[:2]
         if style == "gated":
-            near, token = pack(ids, [[one] for one in near], gates(name + "_pack"))
+            near, token = pack(ids, quarter, near, [[(0, 0)], [(1, 0)]], gates(name + "_pack"))
             link(token)
         flight[name + "_near"] = [home(one, flip) for flip, one in enumerate(near)]
         far = flight[name + "_X"]
         if KNOBS.get("far_" + name, False):
-            far, token = pack(ids, [[one] for one in far], gates(name + "_far_pack"))
+            far, token = pack(ids, quarter, far, [[(0, 0)], [(1, 0)]], gates(name + "_far_pack"))
             link(token)
         flight[name + "_far"] = [home(one, flip) for flip, one in enumerate(far)]
 
@@ -418,56 +428,62 @@
         return whole.reshape(-1)
 
     upper, middle = list(range(side + 1, side + row_bits)), list(range(1, top))
-    last = [[bit] for bit in middle[1:]] + [[top], []]
-    orders = {
-        "y_xz": [upper, [side] + middle[:1]],
-        "y_x_z": [upper, [side], middle[:1]],
-        "x_yz": [[side], upper + middle[:1]],
-        "yx_z": [upper + [side], middle[:1]],
-        "yxz": [upper + [side] + middle[:1]],
-        "y_z_x": [upper, middle[:1], [side]],
-    }
-    order = {k: orders[KNOBS.get("order" + k, "y_xz")] + last for k in "12"}
+    singles = [[bit] for bit in middle[1:]]
+    order = {
+        "y,x,zz": [upper, [side], *singles, middle[:1] + [top]],
+        "y,x,z,z": [upper, [side], *singles, middle[:1], [top]],
+        "y,xz,z": [upper, [side] + middle[:1], *singles, [top]],
+        "y,z,xz": [upper, middle[:1], *singles, [side, top]],
+        "yx,zz": [upper + [side], *singles, middle[:1] + [top]],
+        "yx,z,z": [upper + [side], *singles, middle[:1], [top]],
+        "y,xzz": [upper, *singles, [side] + middle[:1] + [top]],
+    }[KNOBS.get("order", "y,x,zz")]
+    everything = sorted((bit for group in order for bit in group), reverse=True)
     sums = {}
 
     def begin(key, extra):
         keep, *send = extra
-        left = sorted((bit for group in order[key] for bit in group), reverse=True)
-        sums[key] = keep, [[across_core(one) for one in send]], left, 0
-
-    def step(key):
-        base, incoming, left, n = sums[key]
-        name = "F%s_%d" % (key, n)
-        group = order[key][n]
-        own, pieces, flips, token = fold(ids, base, incoming, left, group, unit, gates(name), work(name))
+        sums[key] = keep, [across_core(one) for one in send], everything, 0
+
+    def step(keys):
+        known = [keys] if keys in sums else list(keys)
+        _, _, left, n = sums[known[0]]
+        name = "F%s_%d" % (keys, n)
+        group = order[n]
+        parts = [sums[key][:2] for key in known]
+        own, pieces, flips, token = fold(ids, parts, len(keys) // len(known), left, group, unit, gates(name), work(name))
         link(token)
-        come = [[sent(one, lambda i, flip=flip: i ^ flip)] for one, flip in zip(pieces, flips, strict=True)]
-        flight[name] = [one for (one,) in come]
-        sums[key] = own, come, [bit for bit in left if bit not in group], n + 1
-
-    def steps_left(key):
-        return len(order[key]) - sums[key][3]
+        come = [sent(one, lambda i, flip=flip: i ^ flip) for one, flip in zip(pieces, flips, strict=True)]
+        flight[name] = come
+        sums[keys] = own, come, [bit for bit in left if bit not in group], n + 1
 
     results = {}
     f_mid, (f_start,) = first_gate("G1f", forward_in, forward_place)
     f_out, (f_moved,) = second_gate("G2f", f_mid)
+    cross("f", f_out)
     leave("f", f_out)
     a_mid, extra = first_gate("GE1", adjoint_in, adjoint_place, (f_start, first_from, unit, scale))
     begin("1", extra)
-    for name in KNOBS.get("plan", "1G21f122a12"):
+    for name in KNOBS["plan"]:
         if name == "G":
             a_out, extra = second_gate("GE2", a_mid, (f_moved, second_out, unit, scale))
             begin("2", extra)
+            cross("a", a_out)
+        elif name == "p":
             leave("a", a_out)
-        elif name in sums:
-            if steps_left(name) > 1:
-                step(name)
+        elif name in "12":
+            step(name)
+        elif name == "J":
+            while "12" not in sums and sums["2"][3] < len(order) - 1:
+                step("1")
+                step("2")
+            step("12")
+        elif name == "E":
+            (env_one, env_two), token = add_up(ids, *sums["12"][:2], 2, gates("end"))
+            link(token)
         else:
             results[name] = finish(name)
-    for key in "12":
-        while steps_left(key):
-            step(key)
-    return results["f"], results["a"], sums["1"][0].reshape(-1), sums["2"][0].reshape(-1)
+    return results["f"], results["a"], env_one.reshape(-1), env_two.reshape(-1)
 
 
 def solution(mesh):

time: 133 us -> 125 us (0.940)
  the two profiles are of different devices: /device:TPU:0 before, /device:TPU:1 now
where the time goes in v3:
time: 125 us
  waiting for transfers between devices  57.7 us (46%)
  starting transfers between devices  39.4 us (32%)
  Pallas kernels  24.2 us (19%)
  local copies, waits for them, and re-layouts  2.65 us (2%)
    ppermute x30, waiting for transfers between devices, sent(): return lax.ppermute(value, AXES, [(i, target(i)) for i in range(count)])  57.7 us
    ppermute x30, starting transfers between devices, sent(): return lax.ppermute(value, AXES, [(i, target(i)) for i in range(count)])  39.4 us
    pallas_call x21, Pallas kernels, call(): pl.pallas_call(body, out_shape=[*shapes, TOKEN], in_specs=[SMEM] + [HBM i...  24.2 us
  transfers between devices with their start and end apart: 30, of which 18 were waited for; matrix products, arithmetic and copies ran while one was open for 0% of the time, Pallas kernels for 18%

profile of v3, /device:TPU:1, one launch (start us, length us, event | category | flops | bytes accessed | tf_op | source)
XLA Modules:
  0.0 125.0 jit_solution(16092902743835714230)
XLA Ops:
  0.7 1.2 constant_dynamic-slice_fusion
  1.8 2.1 %collective-permute-start = (bf16[1024,128]{1,0:T(8,128)(2,1)S(1)}, bf16[1024,128]{1,0:T(8,128)(2,1)S(1)}, u32[]{:S(2)}, u32[]{:S(2)}) collective-permute-start(bf16[1024,128]{1,0:T(8,128)(2,1)S(1)} %get-tuple-element.131), channel_id=1, source_target_pairs={{0,8},{1,9},{2,10},{3,11},{4,12},{5,13},{6,14},{7,15},{8,0},{9,1},... | collective-permute-start | bytes 786440 | tf_op jit(solution)/shard_map/ppermute | solution.py:26
  3.9 2.3 %collective-permute-start.1 = (bf16[1024,128]{1,0:T(8,128)(2,1)S(1)}, bf16[1024,128]{1,0:T(8,128)(2,1)S(1)}, u32[]{:S(2)}, u32[]{:S(2)}) collective-permute-start(bf16[1024,128]{1,0:T(8,128)(2,1)S(1)} %get-tuple-element.130), channel_id=1, source_target_pairs={{0,4},{1,5},{2,6},{3,7},{4,0},{5,1},{6,2},{7,3},{8,12},{9,13},{10,... | collective-permute-start | bytes 786440 | tf_op jit(solution)/shard_map/ppermute | solution.py:26
  6.2 3.7 %collective-permute-done.refs_0_ = bf16[1024,128]{1,0:T(8,128)(2,1)S(1)} collective-permute-done((bf16[1024,128]{1,0:T(8,128)(2,1)S(1)}, bf16[1024,128]{1,0:T(8,128)(2,1)S(1)}, u32[]{:S(2)}, u32[]{:S(2)}) %collective-permute-start) | collective-permute-done | bytes 262176 | tf_op jit(solution)/shard_map/ppermute | solution.py:26
  10.0 2.2 %collective-permute-start.3 = (bf16[1024,128]{1,0:T(8,128)(2,1)S(1)}, bf16[1024,128]{1,0:T(8,128)(2,1)S(1)}, u32[]{:S(2)}, u32[]{:S(2)}) collective-permute-start(bf16[1024,128]{1,0:T(8,128)(2,1)S(1)} %collective-permute-done.refs_0_), channel_id=1, source_target_pairs={{0,4},{1,5},{2,6},{3,7},{4,0},{5,1},{6,2},{7,3},{8,12},{9,13},{10,... | collective-permute-start | bytes 786440 | tf_op jit(solution)/shard_map/ppermute | solution.py:26
  12.8 1.2 copy-done.2
  14.1 0.6 shard_map.67
  14.7 1.3 %collective-permute-start.2 = (bf16[1024,128]{1,0:T(8,128)(2,1)S(1)}, bf16[1024,128]{1,0:T(8,128)(2,1)S(1)}, u32[]{:S(2)}, u32[]{:S(2)}) collective-permute-start(bf16[1024,128]{1,0:T(8,128)(2,1)S(1)} %get-tuple-element.68), channel_id=1, source_target_pairs={{0,8},{1,9},{2,10},{3,11},{4,12},{5,13},{6,14},{7,15},{8,0},{9,1},... | collective-permute-start | bytes 786440 | tf_op jit(solution)/shard_map/ppermute | solution.py:26
  16.2 7.0 %collective-permute-done.1.refs_0_.refs_1_ = bf16[1024,128]{1,0:T(8,128)(2,1)S(1)} collective-permute-done((bf16[1024,128]{1,0:T(8,128)(2,1)S(1)}, bf16[1024,128]{1,0:T(8,128)(2,1)S(1)}, u32[]{:S(2)}, u32[]{:S(2)}) %collective-permute-start.1) | collective-permute-done | bytes 262176 | tf_op jit(solution)/shard_map/ppermute | solution.py:26
  23.2 5.6 %collective-permute-done.3.refs_1_.refs_3_ = bf16[1024,128]{1,0:T(8,128)(2,1)S(1)} collective-permute-done((bf16[1024,128]{1,0:T(8,128)(2,1)S(1)}, bf16[1024,128]{1,0:T(8,128)(2,1)S(1)}, u32[]{:S(2)}, u32[]{:S(2)}) %collective-permute-start.3) | collective-permute-done | bytes 262176 | tf_op jit(solution)/shard_map/ppermute | solution.py:26
  29.4 0.7 shard_map.69
  30.4 2.1 %shard_map.70 = (bf16[512,512]{1,0:T(8,128)(2,1)S(1)}, bf16[128,512]{1,0:T(8,128)(2,1)S(1)}, bf16[128,512]{1,0:T(8,128)(2,1)S(1)}, bf16[128,512]{1,0:T(8,128)(2,...) custom-call(s32[4]{0:T(128)S(1)} %pad_add_fusion.ids_ref, ...), custom_call_target="tpu_custom_call" | custom-call | tf_op jit(solution)/shard_map/pallas_call | solution.py:38
  32.5 1.6 %collective-permute-start.5 = (bf16[128,512]{1,0:T(8,128)(2,1)S(1)}, bf16[128,512]{1,0:T(8,128)(2,1)S(1)}, u32[]{:S(2)}, u32[]{:S(2)}) collective-permute-start(bf16[128,512]{1,0:T(8,128)(2,1)S(1)} %get-tuple-element.73), channel_id=1, source_target_pairs={{0,1},{1,0},{2,3},{3,2},{4,5},{5,4},{6,7},{7,6},{8,9},{9,8},{10,11... | collective-permute-start | bytes 393224 | tf_op jit(solution)/shard_map/ppermute | solution.py:26
  36.0 2.0 %shard_map.71 = (bf16[1024,128]{1,0:T(8,128)(2,1)S(1)}, bf16[1024,128]{1,0:T(8,128)(2,1)S(1)}, bf16[1024,128]{1,0:T(8,128)(2,1)S(1)}, bf16[1024,128]{1,0:T(8,128...) custom-call(s32[4]{0:T(128)S(1)} %pad_add_fusion.ids_ref, ...), custom_call_target="tpu_custom_call" | custom-call | tf_op jit(solution)/shard_map/pallas_call | solution.py:38
  38.3 1.3 %collective-permute-start.10 = (bf16[1024,128]{1,0:T(8,128)(2,1)S(1)}, bf16[1024,128]{1,0:T(8,128)(2,1)S(1)}, u32[]{:S(2)}, u32[]{:S(2)}) collective-permute-start(bf16[1024,128]{1,0:T(8,128)(2,1)S(1)} %get-tuple-element.81), channel_id=1, source_target_pairs={{0,8},{1,9},{2,10},{3,11},{4,12},{5,13},{6,14},{7,15},{8,0},{9,1},... | collective-permute-start | bytes 786440 | tf_op jit(solution)/shard_map/ppermute | solution.py:26
  39.7 6.1 %collective-permute-done.9.refs_1_.refs_2_.refs_0_ = bf16[1024,128]{1,0:T(8,128)(2,1)S(1)} collective-permute-done((bf16[1024,128]{1,0:T(8,128)(2,1)S(1)}, bf16[1024,128]{1,0:T(8,128)(2,1)S(1)}, u32[]{:S(2)}, u32[]{:S(2)}) %collective-permute-start.9) | collective-permute-done | bytes 262176 | tf_op jit(solution)/shard_map/ppermute | solution.py:26
  45.8 5.6 %collective-permute-done.10.refs_2_.refs_3_.refs_1_ = bf16[1024,128]{1,0:T(8,128)(2,1)S(1)} collective-permute-done((bf16[1024,128]{1,0:T(8,128)(2,1)S(1)}, bf16[1024,128]{1,0:T(8,128)(2,1)S(1)}, u32[]{:S(2)}, u32[]{:S(2)}) %collective-permute-start.10) | collective-permute-done | bytes 262176 | tf_op jit(solution)/shard_map/ppermute | solution.py:26
  51.4 2.7 %collective-permute-done.11.refs_0_.refs_1_ = bf16[2048,128]{1,0:T(8,128)(2,1)S(1)} collective-permute-done((bf16[2048,128]{1,0:T(8,128)(2,1)S(1)}, bf16[2048,128]{1,0:T(8,128)(2,1)S(1)}, u32[]{:S(2)}, u32[]{:S(2)}) %collective-permute-start.11) | collective-permute-done | bytes 524320 | tf_op jit(solution)/shard_map/ppermute | solution.py:26
  54.7 0.6 shard_map.73
  55.3 1.9 %collective-permute-start.12 = (bf16[2048,128]{1,0:T(8,128)(2,1)S(1)}, bf16[2048,128]{1,0:T(8,128)(2,1)S(1)}, u32[]{:S(2)}, u32[]{:S(2)}) collective-permute-start(bf16[2048,128]{1,0:T(8,128)(2,1)S(1)} %get-tuple-element.84), channel_id=1, source_target_pairs={{0,0},{1,5},{2,2},{3,7},{4,4},{5,1},{6,6},{7,3},{8,8},{9,13},{10,1... | collective-permute-start | bytes 1572872 | tf_op jit(solution)/shard_map/ppermute | solution.py:26
  57.7 3.6 %shard_map.74 = (bf16[512,512]{1,0:T(8,128)(2,1)S(1)}, bf16[512,512]{1,0:T(8,128)(2,1)S(1)}, f32[4096,128]{1,0:T(8,128)S(1)}, bf16[4096,128]{1,0:T(8,128)(2,1)S(1)}, f32[8,128]{1,0:T(8,128)S(1)}) custom-call(s32[4]{0:T(128)S(1)} %pad_add_fusion.ids_ref, bf16[1024,128]{1,0:T(8,128)(2,1)S(1)} %get-tuple-element.86.refs_0_, ...), custom_call_target="tpu_custom_call" | custom-call | tf_op jit(solution)/shard_map/pallas_call | solution.py:38
  61.3 0.9 collective-permute-start.15
  62.9 2.4 %collective-permute-done.16.refs_1_ = bf16[4096,128]{1,0:T(8,128)(2,1)S(1)} collective-permute-done((bf16[4096,128]{1,0:T(8,128)(2,1)S(1)}, bf16[4096,128]{1,0:T(8,128)(2,1)S(1)}, u32[]{:S(2)}, u32[]{:S(2)}) %collective-permute-start.16) | collective-permute-done | bytes 1048608 | tf_op jit(solution)/shard_map/ppermute | solution.py:26
  65.3 0.7 shard_map.76
  66.0 3.5 %shard_map.77 = (bf16[1024,128]{1,0:T(8,128)(2,1)S(1)}, bf16[1024,128]{1,0:T(8,128)(2,1)S(1)}, bf16[2048,128]{1,0:T(8,128)(2,1)S(1)}, f32[4096,128]{1,0:T(8,128)...) custom-call(s32[4]{0:T(128)S(1)} %pad_add_fusion.ids_ref, bf16[512,512]{1,0:T(8,128)(2,1)S(1)} %get-tuple-element.90.refs_0_, ...), custom_call_target="tpu_custom_call" | custom-call | tf_op jit(solution)/shard_map/pallas_call | solution.py:38
  70.0 1.2 collective-permute-start.19
  71.5 5.9 %collective-permute-done.12.refs_0_ = bf16[2048,128]{1,0:T(8,128)(2,1)S(1)} collective-permute-done((bf16[2048,128]{1,0:T(8,128)(2,1)S(1)}, bf16[2048,128]{1,0:T(8,128)(2,1)S(1)}, u32[]{:S(2)}, u32[]{:S(2)}) %collective-permute-start.12) | collective-permute-done | bytes 524320 | tf_op jit(solution)/shard_map/ppermute | solution.py:26
  77.9 0.7 shard_map.79
  78.6 1.3 %collective-permute-start.18 = (bf16[2048,128]{1,0:T(8,128)(2,1)S(1)}, bf16[2048,128]{1,0:T(8,128)(2,1)S(1)}, u32[]{:S(2)}, u32[]{:S(2)}) collective-permute-start(bf16[2048,128]{1,0:T(8,128)(2,1)S(1)} %get-tuple-element.101), channel_id=1, source_target_pairs={{0,16},{1,17},{2,18},{3,19},{4,20},{5,21},{6,22},{7,23},{8,24},{9,... | collective-permute-start | bytes 1572872 | tf_op jit(solution)/shard_map/ppermute | solution.py:26
  79.9 4.3 %collective-permute-done.20.refs_2_ = bf16[2048,128]{1,0:T(8,128)(2,1)S(1)} collective-permute-done((bf16[2048,128]{1,0:T(8,128)(2,1)S(1)}, bf16[2048,128]{1,0:T(8,128)(2,1)S(1)}, u32[]{:S(2)}, u32[]{:S(2)}) %collective-permute-start.20) | collective-permute-done | bytes 524320 | tf_op jit(solution)/shard_map/ppermute | solution.py:26
  84.3 0.6 shard_map.80
  84.9 4.0 %collective-permute-start.21 = (bf16[2048,128]{1,0:T(8,128)(2,1)S(1)}, bf16[2048,128]{1,0:T(8,128)(2,1)S(1)}, u32[]{:S(2)}, u32[]{:S(2)}) collective-permute-start(bf16[2048,128]{1,0:T(8,128)(2,1)S(1)} %get-tuple-element.112), channel_id=1, source_target_pairs={{0,0},{1,5},{2,2},{3,7},{4,4},{5,1},{6,6},{7,3},{8,8},{9,13},{10,1... | collective-permute-start | bytes 1572872 | tf_op jit(solution)/shard_map/ppermute | solution.py:26
  89.2 0.7 shard_map.81
  90.2 0.7 collective-permute-start.24
  90.9 6.7 %collective-permute-start.25 = (bf16[512,128]{1,0:T(8,128)(2,1)S(1)}, bf16[512,128]{1,0:T(8,128)(2,1)S(1)}, u32[]{:S(2)}, u32[]{:S(2)}) collective-permute-start(bf16[512,128]{1,0:T(8,128)(2,1)S(1)} %get-tuple-element.117), channel_id=1, source_target_pairs={{0,10},{1,11},{2,8},{3,9},{4,14},{5,15},{6,12},{7,13},{8,2},{9,3},... | collective-permute-start | bytes 393224 | tf_op jit(solution)/shard_map/ppermute | solution.py:26
  97.6 0.6 shard_map.82
  98.2 1.3 %collective-permute-start.26 = (bf16[512,128]{1,0:T(8,128)(2,1)S(1)}, bf16[512,128]{1,0:T(8,128)(2,1)S(1)}, u32[]{:S(2)}, u32[]{:S(2)}) collective-permute-start(bf16[512,128]{1,0:T(8,128)(2,1)S(1)} %get-tuple-element.119), channel_id=1, source_target_pairs={{0,8},{1,9},{2,10},{3,11},{4,12},{5,13},{6,14},{7,15},{8,0},{9,1},... | collective-permute-start | bytes 393224 | tf_op jit(solution)/shard_map/ppermute | solution.py:26
  99.5 6.9 %collective-permute-done.24.refs_2_ = bf16[512,128]{1,0:T(8,128)(2,1)S(1)} collective-permute-done((bf16[512,128]{1,0:T(8,128)(2,1)S(1)}, bf16[512,128]{1,0:T(8,128)(2,1)S(1)}, u32[]{:S(2)}, u32[]{:S(2)}) %collective-permute-start.24) | collective-permute-done | bytes 131104 | tf_op jit(solution)/shard_map/ppermute | solution.py:26
  106.4 2.2 %collective-permute-start.27 = (bf16[512,128]{1,0:T(8,128)(2,1)S(1)}, bf16[512,128]{1,0:T(8,128)(2,1)S(1)}, u32[]{:S(2)}, u32[]{:S(2)}) collective-permute-start(bf16[512,128]{1,0:T(8,128)(2,1)S(1)} %get-tuple-element.120), channel_id=1, source_target_pairs={{0,2},{1,3},{2,0},{3,1},{4,6},{5,7},{6,4},{7,5},{8,10},{9,11},{10,... | collective-permute-start | bytes 393224 | tf_op jit(solution)/shard_map/ppermute | solution.py:26
  108.6 3.1 %collective-permute-start.28 = (bf16[512,128]{1,0:T(8,128)(2,1)S(1)}, bf16[512,128]{1,0:T(8,128)(2,1)S(1)}, u32[]{:S(2)}, u32[]{:S(2)}) collective-permute-start(bf16[512,128]{1,0:T(8,128)(2,1)S(1)} %get-tuple-element.121), channel_id=1, source_target_pairs={{0,10},{1,11},{2,8},{3,9},{4,14},{5,15},{6,12},{7,13},{8,2},{9,3},... | collective-permute-start | bytes 393224 | tf_op jit(solution)/shard_map/ppermute | solution.py:26
  111.7 1.5 %shard_map.83 = (bf16[4096,128]{1,0:T(8,128)(2,1)}, f32[8,128]{1,0:T(8,128)S(1)}) custom-call(s32[4]{0:T(128)S(1)} %pad_add_fusion.ids_ref, bf16[2048,128]{1,0:T(8,128)(2,1)S(1)} %collective-permute-done.12.refs_0_, bf16[2048,128]{1,0:T(8,128)(2,1)S(1)} %collective-permute-done.13.refs_1_, f32[8,128]{1,0:T(8,128)S(1)} %get-tuple-element.110.refs_2_), custom_call_target="tpu_custom_call" | custom-call | tf_op jit(solution)/shard_map/pallas_call | solution.py:38
  113.3 0.8 collective-permute-done.27.refs_6_
  114.1 1.3 %collective-permute-done.28.refs_7_ = bf16[512,128]{1,0:T(8,128)(2,1)S(1)} collective-permute-done((bf16[512,128]{1,0:T(8,128)(2,1)S(1)}, bf16[512,128]{1,0:T(8,128)(2,1)S(1)}, u32[]{:S(2)}, u32[]{:S(2)}) %collective-permute-start.28) | collective-permute-done | bytes 131104 | tf_op jit(solution)/shard_map/ppermute | solution.py:26
  115.5 0.7 shard_map.84
  116.1 2.1 %collective-permute-start.29 = (bf16[512,128]{1,0:T(8,128)(2,1)S(1)}, bf16[512,128]{1,0:T(8,128)(2,1)S(1)}, u32[]{:S(2)}, u32[]{:S(2)}) collective-permute-start(bf16[512,128]{1,0:T(8,128)(2,1)S(1)} %get-tuple-element.126), channel_id=1, source_target_pairs={{0,4},{1,5},{2,6},{3,7},{4,0},{5,1},{6,2},{7,3},{8,12},{9,13},{10,... | collective-permute-start | bytes 393224 | tf_op jit(solution)/shard_map/ppermute | solution.py:26
  118.2 1.5 %shard_map.85 = (bf16[4096,128]{1,0:T(8,128)(2,1)}, f32[8,128]{1,0:T(8,128)S(1)}) custom-call(s32[4]{0:T(128)S(1)} %pad_add_fusion.ids_ref, bf16[2048,128]{1,0:T(8,128)(2,1)S(1)} %collective-permute-done.21.refs_0_, bf16[2048,128]{1,0:T(8,128)(2,1)S(1)} %collective-permute-done.22.refs_1_, f32[8,128]{1,0:T(8,128)S(1)} %get-tuple-element.123.refs_2_), custom_call_target="tpu_custom_call" | custom-call | tf_op jit(solution)/shard_map/pallas_call | solution.py:38
  119.8 3.9 %collective-permute-done.29.refs_1_ = bf16[512,128]{1,0:T(8,128)(2,1)S(1)} collective-permute-done((bf16[512,128]{1,0:T(8,128)(2,1)S(1)}, bf16[512,128]{1,0:T(8,128)(2,1)S(1)}, u32[]{:S(2)}, u32[]{:S(2)}) %collective-permute-start.29) | collective-permute-done | bytes 131104 | tf_op jit(solution)/shard_map/ppermute | solution.py:26
  123.7 1.3 %shard_map.86 = (f32[256,128]{1,0:T(8,128)}, f32[256,128]{1,0:T(8,128)}, f32[8,128]{1,0:T(8,128)}) custom-call(s32[4]{0:T(128)S(1)} %pad_add_fusion.ids_ref, f32[512,128]{1,0:T(8,128)S(1)} %get-tuple-element.125.refs_0_, bf16[512,128]{1,0:T(8,128)(2,1)S(1)} %collective-permute-done.29.refs_1_, f32[8,128]{1,0:T(8,128)S(1)} %get-tuple-element.127.refs_2_), custom_call_target="tpu_custom_call" | custom-call | tf_op jit(solution)/shard_map/pallas_call | solution.py:38
  (41 shorter events, 7.6 us)
Async XLA Ops:
  0.6 12.2 %copy-start.1 = (bf16[524288]{0:T(1024)(128)(2,1)S(1)}, bf16[524288]{0:T(1024)(128)(2,1)}, u32[]{:S(2)}) copy-start(bf16[524288]{0:T(1024)(128)(2,1)} %param.4) | copy-start | bytes 3145732
  1.8 8.1 %collective-permute-start = (bf16[1024,128]{1,0:T(8,128)(2,1)S(1)}, bf16[1024,128]{1,0:T(8,128)(2,1)S(1)}, u32[]{:S(2)}, u32[]{:S(2)}) collective-permute-start(bf16[1024,128]{1,0:T(8,128)(2,1)S(1)} %get-tuple-element.131), channel_id=1, source_target_pairs={{0,8},{1,9},{2,10},{3,11},{4,12},{5,13},{6,14},{7,15},{8,0},{9,1},... | collective-permute-start | bytes 786440 | tf_op jit(solution)/shard_map/ppermute | solution.py:26
  3.9 19.3 %collective-permute-start.1 = (bf16[1024,128]{1,0:T(8,128)(2,1)S(1)}, bf16[1024,128]{1,0:T(8,128)(2,1)S(1)}, u32[]{:S(2)}, u32[]{:S(2)}) collective-permute-start(bf16[1024,128]{1,0:T(8,128)(2,1)S(1)} %get-tuple-element.130), channel_id=1, source_target_pairs={{0,4},{1,5},{2,6},{3,7},{4,0},{5,1},{6,2},{7,3},{8,12},{9,13},{10,... | collective-permute-start | bytes 786440 | tf_op jit(solution)/shard_map/ppermute | solution.py:26
  10.0 18.9 %collective-permute-start.3 = (bf16[1024,128]{1,0:T(8,128)(2,1)S(1)}, bf16[1024,128]{1,0:T(8,128)(2,1)S(1)}, u32[]{:S(2)}, u32[]{:S(2)}) collective-permute-start(bf16[1024,128]{1,0:T(8,128)(2,1)S(1)} %collective-permute-done.refs_0_), channel_id=1, source_target_pairs={{0,4},{1,5},{2,6},{3,7},{4,0},{5,1},{6,2},{7,3},{8,12},{9,13},{10,... | collective-permute-start | bytes 786440 | tf_op jit(solution)/shard_map/ppermute | solution.py:26
  12.8 1.2 copy-start.2
  14.7 15.4 %collective-permute-start.2 = (bf16[1024,128]{1,0:T(8,128)(2,1)S(1)}, bf16[1024,128]{1,0:T(8,128)(2,1)S(1)}, u32[]{:S(2)}, u32[]{:S(2)}) collective-permute-start(bf16[1024,128]{1,0:T(8,128)(2,1)S(1)} %get-tuple-element.68), channel_id=1, source_target_pairs={{0,8},{1,9},{2,10},{3,11},{4,12},{5,13},{6,14},{7,15},{8,0},{9,1},... | collective-permute-start | bytes 786440 | tf_op jit(solution)/shard_map/ppermute | solution.py:26
  16.0 13.4 %collective-permute-start.4 = (bf16[1024,128]{1,0:T(8,128)(2,1)S(1)}, bf16[1024,128]{1,0:T(8,128)(2,1)S(1)}, u32[]{:S(2)}, u32[]{:S(2)}) collective-permute-start(bf16[1024,128]{1,0:T(8,128)(2,1)S(1)} %get-tuple-element.69), channel_id=1, source_target_pairs={{0,8},{1,9},{2,10},{3,11},{4,12},{5,13},{6,14},{7,15},{8,0},{9,1},... | collective-permute-start | bytes 786440 | tf_op jit(solution)/shard_map/ppermute | solution.py:26
  28.8 1.6 %copy-start = (bf16[1024,1024]{1,0:T(8,128)(2,1)S(1)}, bf16[1024,1024]{1,0:T(8,128)(2,1)}, u32[]{:S(2)}) copy-start(bf16[1024,1024]{1,0:T(8,128)(2,1)} %refs_3_.1) | copy-start | bytes 6291460
  30.1 24.1 %collective-permute-start.11 = (bf16[2048,128]{1,0:T(8,128)(2,1)S(1)}, bf16[2048,128]{1,0:T(8,128)(2,1)S(1)}, u32[]{:S(2)}, u32[]{:S(2)}) collective-permute-start(bf16[2048,128]{1,0:T(8,128)(2,1)S(1)} %get-tuple-element.82), channel_id=1, source_target_pairs={{0,4},{1,5},{2,6},{3,7},{4,0},{5,1},{6,2},{7,3},{8,12},{9,13},{10,... | collective-permute-start | bytes 1572872 | tf_op jit(solution)/shard_map/ppermute | solution.py:26
  32.5 2.6 %collective-permute-start.5 = (bf16[128,512]{1,0:T(8,128)(2,1)S(1)}, bf16[128,512]{1,0:T(8,128)(2,1)S(1)}, u32[]{:S(2)}, u32[]{:S(2)}) collective-permute-start(bf16[128,512]{1,0:T(8,128)(2,1)S(1)} %get-tuple-element.73), channel_id=1, source_target_pairs={{0,1},{1,0},{2,3},{3,2},{4,5},{5,4},{6,7},{7,6},{8,9},{9,8},{10,11... | collective-permute-start | bytes 393224 | tf_op jit(solution)/shard_map/ppermute | solution.py:26
  34.2 1.3 %collective-permute-start.6 = (bf16[128,512]{1,0:T(8,128)(2,1)S(1)}, bf16[128,512]{1,0:T(8,128)(2,1)S(1)}, u32[]{:S(2)}, u32[]{:S(2)}) collective-permute-start(bf16[128,512]{1,0:T(8,128)(2,1)S(1)} %get-tuple-element.74), channel_id=1, source_target_pairs={{0,1},{1,0},{2,3},{3,2},{4,5},{5,4},{6,7},{7,6},{8,9},{9,8},{10,11... | collective-permute-start | bytes 393224 | tf_op jit(solution)/shard_map/ppermute | solution.py:26
  34.2 1.5 %collective-permute-start.7 = (bf16[128,512]{1,0:T(8,128)(2,1)S(1)}, bf16[128,512]{1,0:T(8,128)(2,1)S(1)}, u32[]{:S(2)}, u32[]{:S(2)}) collective-permute-start(bf16[128,512]{1,0:T(8,128)(2,1)S(1)} %get-tuple-element.75), channel_id=1, source_target_pairs={{0,1},{1,0},{2,3},{3,2},{4,5},{5,4},{6,7},{7,6},{8,9},{9,8},{10,11... | collective-permute-start | bytes 393224 | tf_op jit(solution)/shard_map/ppermute | solution.py:26
  34.7 1.3 %collective-permute-start.8 = (bf16[128,512]{1,0:T(8,128)(2,1)S(1)}, bf16[128,512]{1,0:T(8,128)(2,1)S(1)}, u32[]{:S(2)}, u32[]{:S(2)}) collective-permute-start(bf16[128,512]{1,0:T(8,128)(2,1)S(1)} %get-tuple-element.76), channel_id=1, source_target_pairs={{0,1},{1,0},{2,3},{3,2},{4,5},{5,4},{6,7},{7,6},{8,9},{9,8},{10,11... | collective-permute-start | bytes 393224 | tf_op jit(solution)/shard_map/ppermute | solution.py:26
  38.0 7.8 %collective-permute-start.9 = (bf16[1024,128]{1,0:T(8,128)(2,1)S(1)}, bf16[1024,128]{1,0:T(8,128)(2,1)S(1)}, u32[]{:S(2)}, u32[]{:S(2)}) collective-permute-start(bf16[1024,128]{1,0:T(8,128)(2,1)S(1)} %get-tuple-element.80), channel_id=1, source_target_pairs={{0,8},{1,9},{2,10},{3,11},{4,12},{5,13},{6,14},{7,15},{8,0},{9,1},... | collective-permute-start | bytes 786440 | tf_op jit(solution)/shard_map/ppermute | solution.py:26
  38.3 13.1 %collective-permute-start.10 = (bf16[1024,128]{1,0:T(8,128)(2,1)S(1)}, bf16[1024,128]{1,0:T(8,128)(2,1)S(1)}, u32[]{:S(2)}, u32[]{:S(2)}) collective-permute-start(bf16[1024,128]{1,0:T(8,128)(2,1)S(1)} %get-tuple-element.81), channel_id=1, source_target_pairs={{0,8},{1,9},{2,10},{3,11},{4,12},{5,13},{6,14},{7,15},{8,0},{9,1},... | collective-permute-start | bytes 786440 | tf_op jit(solution)/shard_map/ppermute | solution.py:26
  39.5 18.1 %collective-permute-start.14 = (bf16[1024,128]{1,0:T(8,128)(2,1)S(1)}, bf16[1024,128]{1,0:T(8,128)(2,1)S(1)}, u32[]{:S(2)}, u32[]{:S(2)}) collective-permute-start(bf16[1024,128]{1,0:T(8,128)(2,1)S(1)} %get-tuple-element.87), channel_id=1, source_target_pairs={{0,8},{1,9},{2,10},{3,11},{4,12},{5,13},{6,14},{7,15},{8,0},{9,1},... | collective-permute-start | bytes 786440 | tf_op jit(solution)/shard_map/ppermute | solution.py:26
  55.3 22.1 %collective-permute-start.12 = (bf16[2048,128]{1,0:T(8,128)(2,1)S(1)}, bf16[2048,128]{1,0:T(8,128)(2,1)S(1)}, u32[]{:S(2)}, u32[]{:S(2)}) collective-permute-start(bf16[2048,128]{1,0:T(8,128)(2,1)S(1)} %get-tuple-element.84), channel_id=1, source_target_pairs={{0,0},{1,5},{2,2},{3,7},{4,4},{5,1},{6,6},{7,3},{8,8},{9,13},{10,1... | collective-permute-start | bytes 1572872 | tf_op jit(solution)/shard_map/ppermute | solution.py:26
  57.2 20.1 %collective-permute-start.13 = (bf16[2048,128]{1,0:T(8,128)(2,1)S(1)}, bf16[2048,128]{1,0:T(8,128)(2,1)S(1)}, u32[]{:S(2)}, u32[]{:S(2)}) collective-permute-start(bf16[2048,128]{1,0:T(8,128)(2,1)S(1)} %get-tuple-element.85), channel_id=1, source_target_pairs={{0,1},{1,4},{2,3},{3,6},{4,5},{5,0},{6,7},{7,2},{8,9},{9,12},{10,1... | collective-permute-start | bytes 1572872 | tf_op jit(solution)/shard_map/ppermute | solution.py:26
  61.3 4.7 %collective-permute-start.15 = (bf16[512,512]{1,0:T(8,128)(2,1)S(1)}, bf16[512,512]{1,0:T(8,128)(2,1)S(1)}, u32[]{:S(2)}, u32[]{:S(2)}) collective-permute-start(bf16[512,512]{1,0:T(8,128)(2,1)S(1)} %get-tuple-element.91), channel_id=1, source_target_pairs={{0,1},{1,0},{2,3},{3,2},{4,5},{5,4},{6,7},{7,6},{8,9},{9,8},{10,11... | collective-permute-start | bytes 1572872 | tf_op jit(solution)/shard_map/ppermute | solution.py:26
  62.3 3.0 %collective-permute-start.16 = (bf16[4096,128]{1,0:T(8,128)(2,1)S(1)}, bf16[4096,128]{1,0:T(8,128)(2,1)S(1)}, u32[]{:S(2)}, u32[]{:S(2)}) collective-permute-start(bf16[4096,128]{1,0:T(8,128)(2,1)S(1)} %get-tuple-element.94), channel_id=1, source_target_pairs={{0,1},{1,0},{2,3},{3,2},{4,5},{5,4},{6,7},{7,6},{8,9},{9,8},{10,11... | collective-permute-start | bytes 3145736 | tf_op jit(solution)/shard_map/ppermute | solution.py:26
  69.6 8.3 %collective-permute-start.17 = (bf16[4096,128]{1,0:T(8,128)(2,1)S(1)}, bf16[4096,128]{1,0:T(8,128)(2,1)S(1)}, u32[]{:S(2)}, u32[]{:S(2)}) collective-permute-start(bf16[4096,128]{1,0:T(8,128)(2,1)S(1)} %get-tuple-element.98), channel_id=1, source_target_pairs={{0,1},{1,0},{2,3},{3,2},{4,5},{5,4},{6,7},{7,6},{8,9},{9,8},{10,11... | collective-permute-start | bytes 3145736 | tf_op jit(solution)/shard_map/ppermute | solution.py:26
  70.0 19.2 %collective-permute-start.19 = (bf16[2048,128]{1,0:T(8,128)(2,1)S(1)}, bf16[2048,128]{1,0:T(8,128)(2,1)S(1)}, u32[]{:S(2)}, u32[]{:S(2)}) collective-permute-start(bf16[2048,128]{1,0:T(8,128)(2,1)S(1)} %get-tuple-element.103), channel_id=1, source_target_pairs={{0,16},{1,17},{2,18},{3,19},{4,20},{5,21},{6,22},{7,23},{8,24},{9,... | collective-permute-start | bytes 1572872 | tf_op jit(solution)/shard_map/ppermute | solution.py:26
  71.2 13.1 %collective-permute-start.20 = (bf16[2048,128]{1,0:T(8,128)(2,1)S(1)}, bf16[2048,128]{1,0:T(8,128)(2,1)S(1)}, u32[]{:S(2)}, u32[]{:S(2)}) collective-permute-start(bf16[2048,128]{1,0:T(8,128)(2,1)S(1)} %get-tuple-element.106), channel_id=1, source_target_pairs={{0,8},{1,9},{2,10},{3,11},{4,12},{5,13},{6,14},{7,15},{8,0},{9,1},... | collective-permute-start | bytes 1572872 | tf_op jit(solution)/shard_map/ppermute | solution.py:26
  78.6 12.2 %collective-permute-start.18 = (bf16[2048,128]{1,0:T(8,128)(2,1)S(1)}, bf16[2048,128]{1,0:T(8,128)(2,1)S(1)}, u32[]{:S(2)}, u32[]{:S(2)}) collective-permute-start(bf16[2048,128]{1,0:T(8,128)(2,1)S(1)} %get-tuple-element.101), channel_id=1, source_target_pairs={{0,16},{1,17},{2,18},{3,19},{4,20},{5,21},{6,22},{7,23},{8,24},{9,... | collective-permute-start | bytes 1572872 | tf_op jit(solution)/shard_map/ppermute | solution.py:26
  84.9 33.3 %collective-permute-start.21 = (bf16[2048,128]{1,0:T(8,128)(2,1)S(1)}, bf16[2048,128]{1,0:T(8,128)(2,1)S(1)}, u32[]{:S(2)}, u32[]{:S(2)}) collective-permute-start(bf16[2048,128]{1,0:T(8,128)(2,1)S(1)} %get-tuple-element.112), channel_id=1, source_target_pairs={{0,0},{1,5},{2,2},{3,7},{4,4},{5,1},{6,6},{7,3},{8,8},{9,13},{10,1... | collective-permute-start | bytes 1572872 | tf_op jit(solution)/shard_map/ppermute | solution.py:26
  89.0 29.3 %collective-permute-start.22 = (bf16[2048,128]{1,0:T(8,128)(2,1)S(1)}, bf16[2048,128]{1,0:T(8,128)(2,1)S(1)}, u32[]{:S(2)}, u32[]{:S(2)}) collective-permute-start(bf16[2048,128]{1,0:T(8,128)(2,1)S(1)} %get-tuple-element.113), channel_id=1, source_target_pairs={{0,1},{1,4},{2,3},{3,6},{4,5},{5,0},{6,7},{7,2},{8,9},{9,12},{10,1... | collective-permute-start | bytes 1572872 | tf_op jit(solution)/shard_map/ppermute | solution.py:26
  89.9 8.3 %collective-permute-start.23 = (bf16[512,128]{1,0:T(8,128)(2,1)S(1)}, bf16[512,128]{1,0:T(8,128)(2,1)S(1)}, u32[]{:S(2)}, u32[]{:S(2)}) collective-permute-start(bf16[512,128]{1,0:T(8,128)(2,1)S(1)} %get-tuple-element.115), channel_id=1, source_target_pairs={{0,8},{1,9},{2,10},{3,11},{4,12},{5,13},{6,14},{7,15},{8,0},{9,1},... | collective-permute-start | bytes 393224 | tf_op jit(solution)/shard_map/ppermute | solution.py:26
  90.2 16.2 %collective-permute-start.24 = (bf16[512,128]{1,0:T(8,128)(2,1)S(1)}, bf16[512,128]{1,0:T(8,128)(2,1)S(1)}, u32[]{:S(2)}, u32[]{:S(2)}) collective-permute-start(bf16[512,128]{1,0:T(8,128)(2,1)S(1)} %get-tuple-element.116), channel_id=1, source_target_pairs={{0,2},{1,3},{2,0},{3,1},{4,6},{5,7},{6,4},{7,5},{8,10},{9,11},{10,... | collective-permute-start | bytes 393224 | tf_op jit(solution)/shard_map/ppermute | solution.py:26
  90.9 17.7 %collective-permute-start.25 = (bf16[512,128]{1,0:T(8,128)(2,1)S(1)}, bf16[512,128]{1,0:T(8,128)(2,1)S(1)}, u32[]{:S(2)}, u32[]{:S(2)}) collective-permute-start(bf16[512,128]{1,0:T(8,128)(2,1)S(1)} %get-tuple-element.117), channel_id=1, source_target_pairs={{0,10},{1,11},{2,8},{3,9},{4,14},{5,15},{6,12},{7,13},{8,2},{9,3},... | collective-permute-start | bytes 393224 | tf_op jit(solution)/shard_map/ppermute | solution.py:26
  98.2 15.1 %collective-permute-start.26 = (bf16[512,128]{1,0:T(8,128)(2,1)S(1)}, bf16[512,128]{1,0:T(8,128)(2,1)S(1)}, u32[]{:S(2)}, u32[]{:S(2)}) collective-permute-start(bf16[512,128]{1,0:T(8,128)(2,1)S(1)} %get-tuple-element.119), channel_id=1, source_target_pairs={{0,8},{1,9},{2,10},{3,11},{4,12},{5,13},{6,14},{7,15},{8,0},{9,1},... | collective-permute-start | bytes 393224 | tf_op jit(solution)/shard_map/ppermute | solution.py:26
  106.4 7.8 %collective-permute-start.27 = (bf16[512,128]{1,0:T(8,128)(2,1)S(1)}, bf16[512,128]{1,0:T(8,128)(2,1)S(1)}, u32[]{:S(2)}, u32[]{:S(2)}) collective-permute-start(bf16[512,128]{1,0:T(8,128)(2,1)S(1)} %get-tuple-element.120), channel_id=1, source_target_pairs={{0,2},{1,3},{2,0},{3,1},{4,6},{5,7},{6,4},{7,5},{8,10},{9,11},{10,... | collective-permute-start | bytes 393224 | tf_op jit(solution)/shard_map/ppermute | solution.py:26
  108.6 6.8 %collective-permute-start.28 = (bf16[512,128]{1,0:T(8,128)(2,1)S(1)}, bf16[512,128]{1,0:T(8,128)(2,1)S(1)}, u32[]{:S(2)}, u32[]{:S(2)}) collective-permute-start(bf16[512,128]{1,0:T(8,128)(2,1)S(1)} %get-tuple-element.121), channel_id=1, source_target_pairs={{0,10},{1,11},{2,8},{3,9},{4,14},{5,15},{6,12},{7,13},{8,2},{9,3},... | collective-permute-start | bytes 393224 | tf_op jit(solution)/shard_map/ppermute | solution.py:26
  116.1 7.6 %collective-permute-start.29 = (bf16[512,128]{1,0:T(8,128)(2,1)S(1)}, bf16[512,128]{1,0:T(8,128)(2,1)S(1)}, u32[]{:S(2)}, u32[]{:S(2)}) collective-permute-start(bf16[512,128]{1,0:T(8,128)(2,1)S(1)} %get-tuple-element.126), channel_id=1, source_target_pairs={{0,4},{1,5},{2,6},{3,7},{4,0},{5,1},{6,2},{7,3},{8,12},{9,13},{10,... | collective-permute-start | bytes 393224 | tf_op jit(solution)/shard_map/ppermute | solution.py:26

commit v4 on v3

--- a/solution.py
+++ b/solution.py
@@ -10,7 +10,7 @@
 
 AXES = ("row", "col")
 LANES = 128
-KNOBS = {'out_f': 'packed', 'out_a': 'packed', 'plan': '1G2p12fJaE', 'free': ['take2', 'F2_0', 'GE2', 'F12_2'], 'cuts': {'G1f': 4}, 'order': 'y,xz,z', 'waits': {'take2': ['Z1', 'Z2'], 'f_pack': ['Z3', 'f_X'], 'F2_0': ['f_near'], 'GE2': ['f_X']}, 'lead': {'take2': 20000000000, 'F2_0': 20000000000, 'GE2': 20000000000, 'F12_2': 20000000000}}
+KNOBS = {'out_f': 'packed', 'out_a': 'packed', 'plan': '1G2p12JfaE', 'free': ['take2', 'F2_0', 'GE2', 'F12_2'], 'cuts': {'G1f': 4}, 'order': 'y,xz,z', 'waits': {'take2': ['Z1', 'Z2'], 'f_pack': ['Z3', 'f_X'], 'F2_0': ['f_near'], 'GE2': ['f_X']}, 'lead': {'take2': 20000000000, 'F2_0': 20000000000, 'GE2': 20000000000, 'F12_2': 20000000000}, 'direct': ['f_pack', 'take1']}
 
 
 SMEM = pl.BlockSpec(memory_space=pltpu.SMEM)
@@ -315,6 +315,8 @@
         before = chain[-1:]
         if not waits:
             return before
+        if name in KNOBS.get("direct", ()):
+            return [*waits, *before]
         free = name in KNOBS.get("free", ())
         token = arrived(ids, waits, [] if free else before, work=KNOBS.get("lead", {}).get(name, 0))
         return [token, *before] if free else [token]
@@ -326,10 +328,14 @@
         return KNOBS.get("work", {}).get(name, 0)
 
     flight["Z1"] = [across_z(quarter_of(forward, 0, 1))]
-    flight["X1"] = [across_x(quarter_of(forward, 1, 1))]
+    if KNOBS.get("take0", False):
+        (through,), _ = take(ids, [[(forward, 1, 1)]])
+    else:
+        through = quarter_of(forward, 1, 1)
+    flight["X1"] = [across_x(through)]
     flight["Z2"] = [across_z(flight["X1"][0])]
     (f_own, f_beside, a_relay), token = take(
-        ids, [[(forward, 0, 0)], [(forward, 1, 0)], [(adjoint, 1, 1)]], [arrived(ids, flight["X1"]), *gates("take1")]
+        ids, [[(forward, 0, 0)], [(forward, 1, 0)], [(adjoint, 1, 1)]], [*(flight["X1"] if "take1" in KNOBS.get("direct", ()) else [arrived(ids, flight["X1"])]), *gates("take1")]
     )
     link(token)
     flight["X2"] = [across_x(f_beside)]

time: 125 us -> 124 us (level)
  starting transfers between devices: 39.4 us -> 36.7 us
  waiting for transfers between devices: 57.7 us -> 59.1 us
    ppermute x30, starting transfers between devices: 39.4 us -> 36.7 us  [sent(): return lax.ppermute(value, AXES, [(i, target(i)) for i in range(count)])]
    ppermute x30, waiting for transfers between devices: 57.7 us -> 59.1 us  [sent(): return lax.ppermute(value, AXES, [(i, target(i)) for i in range(count)])]
    unnamed x6 -> x8, local copies, waits for them, and re-layouts: 1.5 us -> 2.72 us
    pallas_call x21 -> x19, Pallas kernels: 24.2 us -> 23.1 us  [call(): pl.pallas_call(body, out_shape=[*shapes, TOKEN], in_specs=[SMEM] + [HBM i...]
  transfers between devices with their start and end apart: 30 -> 30, of which waited for: 18 -> 17; matrix products, arithmetic and copies ran while one was open for 0% -> 0% of each run, Pallas kernels for 18% -> 18%
where the time goes in v4:
time: 124 us
  waiting for transfers between devices  59.1 us (48%)
  starting transfers between devices  36.7 us (30%)
  Pallas kernels  23.1 us (19%)
  local copies, waits for them, and re-layouts  3.79 us (3%)
    ppermute x30, waiting for transfers between devices, sent(): return lax.ppermute(value, AXES, [(i, target(i)) for i in range(count)])  59.1 us
    ppermute x30, starting transfers between devices, sent(): return lax.ppermute(value, AXES, [(i, target(i)) for i in range(count)])  36.7 us
    pallas_call x19, Pallas kernels, call(): pl.pallas_call(body, out_shape=[*shapes, TOKEN], in_specs=[SMEM] + [HBM i...  23.1 us
    unnamed x8, local copies, waits for them, and re-layouts  2.72 us
  transfers between devices with their start and end apart: 30, of which 17 were waited for; matrix products, arithmetic and copies ran while one was open for 0% of the time, Pallas kernels for 18%

profile of v4, /device:TPU:1, one launch (start us, length us, event | category | flops | bytes accessed | tf_op | source)
XLA Modules:
  0.0 123.7 jit_solution(5800155958122030436)
XLA Ops:
  0.7 1.1 constant_dynamic-slice_fusion
  1.7 2.1 %collective-permute-start = (bf16[1024,128]{1,0:T(8,128)(2,1)S(1)}, bf16[1024,128]{1,0:T(8,128)(2,1)S(1)}, u32[]{:S(2)}, u32[]{:S(2)}) collective-permute-start(bf16[1024,128]{1,0:T(8,128)(2,1)S(1)} %get-tuple-element.131), channel_id=1, source_target_pairs={{0,8},{1,9},{2,10},{3,11},{4,12},{5,13},{6,14},{7,15},{8,0},{9,1},... | collective-permute-start | bytes 786440 | tf_op jit(solution)/shard_map/ppermute | solution.py:26
  3.8 2.3 %collective-permute-start.1 = (bf16[1024,128]{1,0:T(8,128)(2,1)S(1)}, bf16[1024,128]{1,0:T(8,128)(2,1)S(1)}, u32[]{:S(2)}, u32[]{:S(2)}) collective-permute-start(bf16[1024,128]{1,0:T(8,128)(2,1)S(1)} %get-tuple-element.130), channel_id=1, source_target_pairs={{0,4},{1,5},{2,6},{3,7},{4,0},{5,1},{6,2},{7,3},{8,12},{9,13},{10,... | collective-permute-start | bytes 786440 | tf_op jit(solution)/shard_map/ppermute | solution.py:26
  6.1 3.7 %collective-permute-done.refs_2_ = bf16[1024,128]{1,0:T(8,128)(2,1)S(1)} collective-permute-done((bf16[1024,128]{1,0:T(8,128)(2,1)S(1)}, bf16[1024,128]{1,0:T(8,128)(2,1)S(1)}, u32[]{:S(2)}, u32[]{:S(2)}) %collective-permute-start) | collective-permute-done | bytes 262176 | tf_op jit(solution)/shard_map/ppermute | solution.py:26
  9.9 2.2 %collective-permute-start.3 = (bf16[1024,128]{1,0:T(8,128)(2,1)S(1)}, bf16[1024,128]{1,0:T(8,128)(2,1)S(1)}, u32[]{:S(2)}, u32[]{:S(2)}) collective-permute-start(bf16[1024,128]{1,0:T(8,128)(2,1)S(1)} %collective-permute-done.refs_2_), channel_id=1, source_target_pairs={{0,4},{1,5},{2,6},{3,7},{4,0},{5,1},{6,2},{7,3},{8,12},{9,13},{10,... | collective-permute-start | bytes 786440 | tf_op jit(solution)/shard_map/ppermute | solution.py:26
  12.2 1.2 copy-done.1
  13.4 1.2 copy-done.3
  14.6 0.6 shard_map.66
  15.3 1.3 %collective-permute-start.2 = (bf16[1024,128]{1,0:T(8,128)(2,1)S(1)}, bf16[1024,128]{1,0:T(8,128)(2,1)S(1)}, u32[]{:S(2)}, u32[]{:S(2)}) collective-permute-start(bf16[1024,128]{1,0:T(8,128)(2,1)S(1)} %get-tuple-element.68), channel_id=1, source_target_pairs={{0,8},{1,9},{2,10},{3,11},{4,12},{5,13},{6,14},{7,15},{8,0},{9,1},... | collective-permute-start | bytes 786440 | tf_op jit(solution)/shard_map/ppermute | solution.py:26
  16.8 6.3 %collective-permute-done.1.refs_0_.refs_1_ = bf16[1024,128]{1,0:T(8,128)(2,1)S(1)} collective-permute-done((bf16[1024,128]{1,0:T(8,128)(2,1)S(1)}, bf16[1024,128]{1,0:T(8,128)(2,1)S(1)}, u32[]{:S(2)}, u32[]{:S(2)}) %collective-permute-start.1) | collective-permute-done | bytes 262176 | tf_op jit(solution)/shard_map/ppermute | solution.py:26
  23.1 5.6 %collective-permute-done.3.refs_1_.refs_3_ = bf16[1024,128]{1,0:T(8,128)(2,1)S(1)} collective-permute-done((bf16[1024,128]{1,0:T(8,128)(2,1)S(1)}, bf16[1024,128]{1,0:T(8,128)(2,1)S(1)}, u32[]{:S(2)}, u32[]{:S(2)}) %collective-permute-start.3) | collective-permute-done | bytes 262176 | tf_op jit(solution)/shard_map/ppermute | solution.py:26
  29.3 0.7 shard_map.68
  30.3 2.1 %shard_map.69 = (bf16[512,512]{1,0:T(8,128)(2,1)S(1)}, bf16[128,512]{1,0:T(8,128)(2,1)S(1)}, bf16[128,512]{1,0:T(8,128)(2,1)S(1)}, bf16[128,512]{1,0:T(8,128)(2,...) custom-call(s32[4]{0:T(128)S(1)} %pad_add_fusion.ids_ref, ...), custom_call_target="tpu_custom_call" | custom-call | tf_op jit(solution)/shard_map/pallas_call | solution.py:38
  32.4 1.6 %collective-permute-start.5 = (bf16[128,512]{1,0:T(8,128)(2,1)S(1)}, bf16[128,512]{1,0:T(8,128)(2,1)S(1)}, u32[]{:S(2)}, u32[]{:S(2)}) collective-permute-start(bf16[128,512]{1,0:T(8,128)(2,1)S(1)} %get-tuple-element.73), channel_id=1, source_target_pairs={{0,1},{1,0},{2,3},{3,2},{4,5},{5,4},{6,7},{7,6},{8,9},{9,8},{10,11... | collective-permute-start | bytes 393224 | tf_op jit(solution)/shard_map/ppermute | solution.py:26
  35.9 2.0 %shard_map.70 = (bf16[1024,128]{1,0:T(8,128)(2,1)S(1)}, bf16[1024,128]{1,0:T(8,128)(2,1)S(1)}, bf16[1024,128]{1,0:T(8,128)(2,1)S(1)}, bf16[1024,128]{1,0:T(8,128...) custom-call(s32[4]{0:T(128)S(1)} %pad_add_fusion.ids_ref, ...), custom_call_target="tpu_custom_call" | custom-call | tf_op jit(solution)/shard_map/pallas_call | solution.py:38
  38.2 1.3 %collective-permute-start.10 = (bf16[1024,128]{1,0:T(8,128)(2,1)S(1)}, bf16[1024,128]{1,0:T(8,128)(2,1)S(1)}, u32[]{:S(2)}, u32[]{:S(2)}) collective-permute-start(bf16[1024,128]{1,0:T(8,128)(2,1)S(1)} %get-tuple-element.81), channel_id=1, source_target_pairs={{0,8},{1,9},{2,10},{3,11},{4,12},{5,13},{6,14},{7,15},{8,0},{9,1},... | collective-permute-start | bytes 786440 | tf_op jit(solution)/shard_map/ppermute | solution.py:26
  39.6 6.1 %collective-permute-done.9.refs_2_.refs_5_.refs_0_ = bf16[1024,128]{1,0:T(8,128)(2,1)S(1)} collective-permute-done((bf16[1024,128]{1,0:T(8,128)(2,1)S(1)}, bf16[1024,128]{1,0:T(8,128)(2,1)S(1)}, u32[]{:S(2)}, u32[]{:S(2)}) %collective-permute-start.9) | collective-permute-done | bytes 262176 | tf_op jit(solution)/shard_map/ppermute | solution.py:26
  45.7 5.6 %collective-permute-done.10.refs_3_.refs_6_.refs_1_ = bf16[1024,128]{1,0:T(8,128)(2,1)S(1)} collective-permute-done((bf16[1024,128]{1,0:T(8,128)(2,1)S(1)}, bf16[1024,128]{1,0:T(8,128)(2,1)S(1)}, u32[]{:S(2)}, u32[]{:S(2)}) %collective-permute-start.10) | collective-permute-done | bytes 262176 | tf_op jit(solution)/shard_map/ppermute | solution.py:26
  51.3 2.7 %collective-permute-done.11.refs_4_.refs_1_ = bf16[2048,128]{1,0:T(8,128)(2,1)S(1)} collective-permute-done((bf16[2048,128]{1,0:T(8,128)(2,1)S(1)}, bf16[2048,128]{1,0:T(8,128)(2,1)S(1)}, u32[]{:S(2)}, u32[]{:S(2)}) %collective-permute-start.11) | collective-permute-done | bytes 524320 | tf_op jit(solution)/shard_map/ppermute | solution.py:26
  54.7 1.9 %collective-permute-start.12 = (bf16[2048,128]{1,0:T(8,128)(2,1)S(1)}, bf16[2048,128]{1,0:T(8,128)(2,1)S(1)}, u32[]{:S(2)}, u32[]{:S(2)}) collective-permute-start(bf16[2048,128]{1,0:T(8,128)(2,1)S(1)} %get-tuple-element.84), channel_id=1, source_target_pairs={{0,0},{1,5},{2,2},{3,7},{4,4},{5,1},{6,6},{7,3},{8,8},{9,13},{10,1... | collective-permute-start | bytes 1572872 | tf_op jit(solution)/shard_map/ppermute | solution.py:26
  57.0 3.6 %shard_map.72 = (bf16[512,512]{1,0:T(8,128)(2,1)S(1)}, bf16[512,512]{1,0:T(8,128)(2,1)S(1)}, f32[4096,128]{1,0:T(8,128)S(1)}, bf16[4096,128]{1,0:T(8,128)(2,1)S(1)}, f32[8,128]{1,0:T(8,128)S(1)}) custom-call(s32[4]{0:T(128)S(1)} %pad_add_fusion.ids_ref, bf16[1024,128]{1,0:T(8,128)(2,1)S(1)} %get-tuple-element.86.refs_0_, ...), custom_call_target="tpu_custom_call" | custom-call | tf_op jit(solution)/shard_map/pallas_call | solution.py:38
  60.7 1.0 collective-permute-start.15
  62.3 1.7 %collective-permute-done.15.refs_1_ = bf16[4096,128]{1,0:T(8,128)(2,1)S(1)} collective-permute-done((bf16[4096,128]{1,0:T(8,128)(2,1)S(1)}, bf16[4096,128]{1,0:T(8,128)(2,1)S(1)}, u32[]{:S(2)}, u32[]{:S(2)}) %collective-permute-start.15) | collective-permute-done | bytes 1048608 | tf_op jit(solution)/shard_map/ppermute | solution.py:26
  63.9 0.7 shard_map.73
  64.6 1.3 %collective-permute-start.16 = (bf16[2048,128]{1,0:T(8,128)(2,1)S(1)}, bf16[2048,128]{1,0:T(8,128)(2,1)S(1)}, u32[]{:S(2)}, u32[]{:S(2)}) collective-permute-start(bf16[2048,128]{1,0:T(8,128)(2,1)S(1)} %get-tuple-element.94), channel_id=1, source_target_pairs={{0,16},{1,17},{2,18},{3,19},{4,20},{5,21},{6,22},{7,23},{8,24},{9,... | collective-permute-start | bytes 1572872 | tf_op jit(solution)/shard_map/ppermute | solution.py:26
  65.9 3.5 %shard_map.75 = (bf16[1024,128]{1,0:T(8,128)(2,1)S(1)}, bf16[1024,128]{1,0:T(8,128)(2,1)S(1)}, bf16[2048,128]{1,0:T(8,128)(2,1)S(1)}, f32[4096,128]{1,0:T(8,128)...) custom-call(s32[4]{0:T(128)S(1)} %pad_add_fusion.ids_ref, bf16[512,512]{1,0:T(8,128)(2,1)S(1)} %get-tuple-element.95.refs_0_, ...), custom_call_target="tpu_custom_call" | custom-call | tf_op jit(solution)/shard_map/pallas_call | solution.py:38
  69.8 0.9 collective-permute-start.19
  70.7 6.0 %collective-permute-done.12.refs_0_ = bf16[2048,128]{1,0:T(8,128)(2,1)S(1)} collective-permute-done((bf16[2048,128]{1,0:T(8,128)(2,1)S(1)}, bf16[2048,128]{1,0:T(8,128)(2,1)S(1)}, u32[]{:S(2)}, u32[]{:S(2)}) %collective-permute-start.12) | collective-permute-done | bytes 524320 | tf_op jit(solution)/shard_map/ppermute | solution.py:26
  77.3 0.7 shard_map.77
  78.0 1.3 %collective-permute-start.23 = (bf16[2048,128]{1,0:T(8,128)(2,1)S(1)}, bf16[2048,128]{1,0:T(8,128)(2,1)S(1)}, u32[]{:S(2)}, u32[]{:S(2)}) collective-permute-start(bf16[2048,128]{1,0:T(8,128)(2,1)S(1)} %get-tuple-element.112), channel_id=1, source_target_pairs={{0,16},{1,17},{2,18},{3,19},{4,20},{5,21},{6,22},{7,23},{8,24},{9,... | collective-permute-start | bytes 1572872 | tf_op jit(solution)/shard_map/ppermute | solution.py:26
  79.3 3.0 %collective-permute-done.18.refs_2_ = bf16[2048,128]{1,0:T(8,128)(2,1)S(1)} collective-permute-done((bf16[2048,128]{1,0:T(8,128)(2,1)S(1)}, bf16[2048,128]{1,0:T(8,128)(2,1)S(1)}, u32[]{:S(2)}, u32[]{:S(2)}) %collective-permute-start.18) | collective-permute-done | bytes 524320 | tf_op jit(solution)/shard_map/ppermute | solution.py:26
  83.0 4.7 %collective-permute-start.27 = (bf16[2048,128]{1,0:T(8,128)(2,1)S(1)}, bf16[2048,128]{1,0:T(8,128)(2,1)S(1)}, u32[]{:S(2)}, u32[]{:S(2)}) collective-permute-start(bf16[2048,128]{1,0:T(8,128)(2,1)S(1)} %get-tuple-element.121), channel_id=1, source_target_pairs={{0,0},{1,5},{2,2},{3,7},{4,4},{5,1},{6,6},{7,3},{8,8},{9,13},{10,1... | collective-permute-start | bytes 1572872 | tf_op jit(solution)/shard_map/ppermute | solution.py:26
  87.8 0.6 shard_map.79
  88.8 0.8 collective-permute-start.21
  89.6 3.7 %collective-permute-start.22 = (bf16[512,128]{1,0:T(8,128)(2,1)S(1)}, bf16[512,128]{1,0:T(8,128)(2,1)S(1)}, u32[]{:S(2)}, u32[]{:S(2)}) collective-permute-start(bf16[512,128]{1,0:T(8,128)(2,1)S(1)} %get-tuple-element.110), channel_id=1, source_target_pairs={{0,10},{1,11},{2,8},{3,9},{4,14},{5,15},{6,12},{7,13},{8,2},{9,3},... | collective-permute-start | bytes 393224 | tf_op jit(solution)/shard_map/ppermute | solution.py:26
  93.3 0.6 shard_map.80
  94.0 1.3 %collective-permute-start.24 = (bf16[512,128]{1,0:T(8,128)(2,1)S(1)}, bf16[512,128]{1,0:T(8,128)(2,1)S(1)}, u32[]{:S(2)}, u32[]{:S(2)}) collective-permute-start(bf16[512,128]{1,0:T(8,128)(2,1)S(1)} %get-tuple-element.115), channel_id=1, source_target_pairs={{0,8},{1,9},{2,10},{3,11},{4,12},{5,13},{6,14},{7,15},{8,0},{9,1},... | collective-permute-start | bytes 393224 | tf_op jit(solution)/shard_map/ppermute | solution.py:26
  95.3 11.2 %collective-permute-done.21.refs_2_ = bf16[512,128]{1,0:T(8,128)(2,1)S(1)} collective-permute-done((bf16[512,128]{1,0:T(8,128)(2,1)S(1)}, bf16[512,128]{1,0:T(8,128)(2,1)S(1)}, u32[]{:S(2)}, u32[]{:S(2)}) %collective-permute-start.21) | collective-permute-done | bytes 131104 | tf_op jit(solution)/shard_map/ppermute | solution.py:26
  106.5 1.9 %collective-permute-start.25 = (bf16[512,128]{1,0:T(8,128)(2,1)S(1)}, bf16[512,128]{1,0:T(8,128)(2,1)S(1)}, u32[]{:S(2)}, u32[]{:S(2)}) collective-permute-start(bf16[512,128]{1,0:T(8,128)(2,1)S(1)} %get-tuple-element.116), channel_id=1, source_target_pairs={{0,2},{1,3},{2,0},{3,1},{4,6},{5,7},{6,4},{7,5},{8,10},{9,11},{10,... | collective-permute-start | bytes 393224 | tf_op jit(solution)/shard_map/ppermute | solution.py:26
  108.4 2.3 %collective-permute-start.26 = (bf16[512,128]{1,0:T(8,128)(2,1)S(1)}, bf16[512,128]{1,0:T(8,128)(2,1)S(1)}, u32[]{:S(2)}, u32[]{:S(2)}) collective-permute-start(bf16[512,128]{1,0:T(8,128)(2,1)S(1)} %get-tuple-element.117), channel_id=1, source_target_pairs={{0,10},{1,11},{2,8},{3,9},{4,14},{5,15},{6,12},{7,13},{8,2},{9,3},... | collective-permute-start | bytes 393224 | tf_op jit(solution)/shard_map/ppermute | solution.py:26
  110.7 1.8 %collective-permute-done.25.refs_6_ = bf16[512,128]{1,0:T(8,128)(2,1)S(1)} collective-permute-done((bf16[512,128]{1,0:T(8,128)(2,1)S(1)}, bf16[512,128]{1,0:T(8,128)(2,1)S(1)}, u32[]{:S(2)}, u32[]{:S(2)}) %collective-permute-start.25) | collective-permute-done | bytes 131104 | tf_op jit(solution)/shard_map/ppermute | solution.py:26
  112.5 1.6 %collective-permute-done.26.refs_7_ = bf16[512,128]{1,0:T(8,128)(2,1)S(1)} collective-permute-done((bf16[512,128]{1,0:T(8,128)(2,1)S(1)}, bf16[512,128]{1,0:T(8,128)(2,1)S(1)}, u32[]{:S(2)}, u32[]{:S(2)}) %collective-permute-start.26) | collective-permute-done | bytes 131104 | tf_op jit(solution)/shard_map/ppermute | solution.py:26
  114.1 0.7 shard_map.81
  114.8 2.0 %collective-permute-start.29 = (bf16[512,128]{1,0:T(8,128)(2,1)S(1)}, bf16[512,128]{1,0:T(8,128)(2,1)S(1)}, u32[]{:S(2)}, u32[]{:S(2)}) collective-permute-start(bf16[512,128]{1,0:T(8,128)(2,1)S(1)} %get-tuple-element.126), channel_id=1, source_target_pairs={{0,4},{1,5},{2,6},{3,7},{4,0},{5,1},{6,2},{7,3},{8,12},{9,13},{10,... | collective-permute-start | bytes 393224 | tf_op jit(solution)/shard_map/ppermute | solution.py:26
  116.8 1.5 %shard_map.82 = (bf16[4096,128]{1,0:T(8,128)(2,1)}, f32[8,128]{1,0:T(8,128)S(1)}) custom-call(s32[4]{0:T(128)S(1)} %pad_add_fusion.ids_ref, bf16[2048,128]{1,0:T(8,128)(2,1)S(1)} %collective-permute-done.12.refs_0_, bf16[2048,128]{1,0:T(8,128)(2,1)S(1)} %collective-permute-done.13.refs_1_, f32[8,128]{1,0:T(8,128)S(1)} %get-tuple-element.119.refs_2_), custom_call_target="tpu_custom_call" | custom-call | tf_op jit(solution)/shard_map/pallas_call | solution.py:38
  118.4 1.5 %shard_map.83 = (bf16[4096,128]{1,0:T(8,128)(2,1)}, f32[8,128]{1,0:T(8,128)S(1)}) custom-call(s32[4]{0:T(128)S(1)} %pad_add_fusion.ids_ref, bf16[2048,128]{1,0:T(8,128)(2,1)S(1)} %collective-permute-done.27.refs_0_, bf16[2048,128]{1,0:T(8,128)(2,1)S(1)} %collective-permute-done.28.refs_1_, f32[8,128]{1,0:T(8,128)S(1)} %get-tuple-element.123.refs_2_), custom_call_target="tpu_custom_call" | custom-call | tf_op jit(solution)/shard_map/pallas_call | solution.py:38
  119.9 2.5 %collective-permute-done.29.refs_1_ = bf16[512,128]{1,0:T(8,128)(2,1)S(1)} collective-permute-done((bf16[512,128]{1,0:T(8,128)(2,1)S(1)}, bf16[512,128]{1,0:T(8,128)(2,1)S(1)}, u32[]{:S(2)}, u32[]{:S(2)}) %collective-permute-start.29) | collective-permute-done | bytes 131104 | tf_op jit(solution)/shard_map/ppermute | solution.py:26
  122.4 1.3 %shard_map.84 = (f32[256,128]{1,0:T(8,128)}, f32[256,128]{1,0:T(8,128)}, f32[8,128]{1,0:T(8,128)}) custom-call(s32[4]{0:T(128)S(1)} %pad_add_fusion.ids_ref, f32[512,128]{1,0:T(8,128)S(1)} %get-tuple-element.125.refs_0_, bf16[512,128]{1,0:T(8,128)(2,1)S(1)} %collective-permute-done.29.refs_1_, f32[8,128]{1,0:T(8,128)S(1)} %get-tuple-element.127.refs_2_), custom_call_target="tpu_custom_call" | custom-call | tf_op jit(solution)/shard_map/pallas_call | solution.py:38
  (41 shorter events, 7.1 us)
Async XLA Ops:
  1.7 8.1 %collective-permute-start = (bf16[1024,128]{1,0:T(8,128)(2,1)S(1)}, bf16[1024,128]{1,0:T(8,128)(2,1)S(1)}, u32[]{:S(2)}, u32[]{:S(2)}) collective-permute-start(bf16[1024,128]{1,0:T(8,128)(2,1)S(1)} %get-tuple-element.131), channel_id=1, source_target_pairs={{0,8},{1,9},{2,10},{3,11},{4,12},{5,13},{6,14},{7,15},{8,0},{9,1},... | collective-permute-start | bytes 786440 | tf_op jit(solution)/shard_map/ppermute | solution.py:26
  3.8 19.3 %collective-permute-start.1 = (bf16[1024,128]{1,0:T(8,128)(2,1)S(1)}, bf16[1024,128]{1,0:T(8,128)(2,1)S(1)}, u32[]{:S(2)}, u32[]{:S(2)}) collective-permute-start(bf16[1024,128]{1,0:T(8,128)(2,1)S(1)} %get-tuple-element.130), channel_id=1, source_target_pairs={{0,4},{1,5},{2,6},{3,7},{4,0},{5,1},{6,2},{7,3},{8,12},{9,13},{10,... | collective-permute-start | bytes 786440 | tf_op jit(solution)/shard_map/ppermute | solution.py:26
  9.9 18.9 %collective-permute-start.3 = (bf16[1024,128]{1,0:T(8,128)(2,1)S(1)}, bf16[1024,128]{1,0:T(8,128)(2,1)S(1)}, u32[]{:S(2)}, u32[]{:S(2)}) collective-permute-start(bf16[1024,128]{1,0:T(8,128)(2,1)S(1)} %collective-permute-done.refs_2_), channel_id=1, source_target_pairs={{0,4},{1,5},{2,6},{3,7},{4,0},{5,1},{6,2},{7,3},{8,12},{9,13},{10,... | collective-permute-start | bytes 786440 | tf_op jit(solution)/shard_map/ppermute | solution.py:26
  12.2 1.2 copy-start.1
  13.4 1.2 copy-start.3
  15.3 14.8 %collective-permute-start.2 = (bf16[1024,128]{1,0:T(8,128)(2,1)S(1)}, bf16[1024,128]{1,0:T(8,128)(2,1)S(1)}, u32[]{:S(2)}, u32[]{:S(2)}) collective-permute-start(bf16[1024,128]{1,0:T(8,128)(2,1)S(1)} %get-tuple-element.68), channel_id=1, source_target_pairs={{0,8},{1,9},{2,10},{3,11},{4,12},{5,13},{6,14},{7,15},{8,0},{9,1},... | collective-permute-start | bytes 786440 | tf_op jit(solution)/shard_map/ppermute | solution.py:26
  16.6 12.7 %copy-start.2 = (bf16[524288]{0:T(1024)(128)(2,1)S(1)}, bf16[524288]{0:T(1024)(128)(2,1)}, u32[]{:S(2)}) copy-start(bf16[524288]{0:T(1024)(128)(2,1)} %param.4) | copy-start | bytes 3145732
  16.6 12.7 %collective-permute-start.4 = (bf16[1024,128]{1,0:T(8,128)(2,1)S(1)}, bf16[1024,128]{1,0:T(8,128)(2,1)S(1)}, u32[]{:S(2)}, u32[]{:S(2)}) collective-permute-start(bf16[1024,128]{1,0:T(8,128)(2,1)S(1)} %get-tuple-element.69), channel_id=1, source_target_pairs={{0,8},{1,9},{2,10},{3,11},{4,12},{5,13},{6,14},{7,15},{8,0},{9,1},... | collective-permute-start | bytes 786440 | tf_op jit(solution)/shard_map/ppermute | solution.py:26
  28.7 1.6 %copy-start = (bf16[1024,1024]{1,0:T(8,128)(2,1)S(1)}, bf16[1024,1024]{1,0:T(8,128)(2,1)}, u32[]{:S(2)}) copy-start(bf16[1024,1024]{1,0:T(8,128)(2,1)} %refs_3_.1) | copy-start | bytes 6291460
  30.0 24.1 %collective-permute-start.11 = (bf16[2048,128]{1,0:T(8,128)(2,1)S(1)}, bf16[2048,128]{1,0:T(8,128)(2,1)S(1)}, u32[]{:S(2)}, u32[]{:S(2)}) collective-permute-start(bf16[2048,128]{1,0:T(8,128)(2,1)S(1)} %get-tuple-element.82), channel_id=1, source_target_pairs={{0,4},{1,5},{2,6},{3,7},{4,0},{5,1},{6,2},{7,3},{8,12},{9,13},{10,... | collective-permute-start | bytes 1572872 | tf_op jit(solution)/shard_map/ppermute | solution.py:26
  32.4 2.6 %collective-permute-start.5 = (bf16[128,512]{1,0:T(8,128)(2,1)S(1)}, bf16[128,512]{1,0:T(8,128)(2,1)S(1)}, u32[]{:S(2)}, u32[]{:S(2)}) collective-permute-start(bf16[128,512]{1,0:T(8,128)(2,1)S(1)} %get-tuple-element.73), channel_id=1, source_target_pairs={{0,1},{1,0},{2,3},{3,2},{4,5},{5,4},{6,7},{7,6},{8,9},{9,8},{10,11... | collective-permute-start | bytes 393224 | tf_op jit(solution)/shard_map/ppermute | solution.py:26
  34.1 1.3 %collective-permute-start.6 = (bf16[128,512]{1,0:T(8,128)(2,1)S(1)}, bf16[128,512]{1,0:T(8,128)(2,1)S(1)}, u32[]{:S(2)}, u32[]{:S(2)}) collective-permute-start(bf16[128,512]{1,0:T(8,128)(2,1)S(1)} %get-tuple-element.74), channel_id=1, source_target_pairs={{0,1},{1,0},{2,3},{3,2},{4,5},{5,4},{6,7},{7,6},{8,9},{9,8},{10,11... | collective-permute-start | bytes 393224 | tf_op jit(solution)/shard_map/ppermute | solution.py:26
  34.1 1.5 %collective-permute-start.7 = (bf16[128,512]{1,0:T(8,128)(2,1)S(1)}, bf16[128,512]{1,0:T(8,128)(2,1)S(1)}, u32[]{:S(2)}, u32[]{:S(2)}) collective-permute-start(bf16[128,512]{1,0:T(8,128)(2,1)S(1)} %get-tuple-element.75), channel_id=1, source_target_pairs={{0,1},{1,0},{2,3},{3,2},{4,5},{5,4},{6,7},{7,6},{8,9},{9,8},{10,11... | collective-permute-start | bytes 393224 | tf_op jit(solution)/shard_map/ppermute | solution.py:26
  34.6 1.3 %collective-permute-start.8 = (bf16[128,512]{1,0:T(8,128)(2,1)S(1)}, bf16[128,512]{1,0:T(8,128)(2,1)S(1)}, u32[]{:S(2)}, u32[]{:S(2)}) collective-permute-start(bf16[128,512]{1,0:T(8,128)(2,1)S(1)} %get-tuple-element.76), channel_id=1, source_target_pairs={{0,1},{1,0},{2,3},{3,2},{4,5},{5,4},{6,7},{7,6},{8,9},{9,8},{10,11... | collective-permute-start | bytes 393224 | tf_op jit(solution)/shard_map/ppermute | solution.py:26
  37.9 7.8 %collective-permute-start.9 = (bf16[1024,128]{1,0:T(8,128)(2,1)S(1)}, bf16[1024,128]{1,0:T(8,128)(2,1)S(1)}, u32[]{:S(2)}, u32[]{:S(2)}) collective-permute-start(bf16[1024,128]{1,0:T(8,128)(2,1)S(1)} %get-tuple-element.80), channel_id=1, source_target_pairs={{0,8},{1,9},{2,10},{3,11},{4,12},{5,13},{6,14},{7,15},{8,0},{9,1},... | collective-permute-start | bytes 786440 | tf_op jit(solution)/shard_map/ppermute | solution.py:26
  38.2 13.1 %collective-permute-start.10 = (bf16[1024,128]{1,0:T(8,128)(2,1)S(1)}, bf16[1024,128]{1,0:T(8,128)(2,1)S(1)}, u32[]{:S(2)}, u32[]{:S(2)}) collective-permute-start(bf16[1024,128]{1,0:T(8,128)(2,1)S(1)} %get-tuple-element.81), channel_id=1, source_target_pairs={{0,8},{1,9},{2,10},{3,11},{4,12},{5,13},{6,14},{7,15},{8,0},{9,1},... | collective-permute-start | bytes 786440 | tf_op jit(solution)/shard_map/ppermute | solution.py:26
  39.4 17.6 %collective-permute-start.14 = (bf16[1024,128]{1,0:T(8,128)(2,1)S(1)}, bf16[1024,128]{1,0:T(8,128)(2,1)S(1)}, u32[]{:S(2)}, u32[]{:S(2)}) collective-permute-start(bf16[1024,128]{1,0:T(8,128)(2,1)S(1)} %get-tuple-element.87), channel_id=1, source_target_pairs={{0,8},{1,9},{2,10},{3,11},{4,12},{5,13},{6,14},{7,15},{8,0},{9,1},... | collective-permute-start | bytes 786440 | tf_op jit(solution)/shard_map/ppermute | solution.py:26
  54.7 22.1 %collective-permute-start.12 = (bf16[2048,128]{1,0:T(8,128)(2,1)S(1)}, bf16[2048,128]{1,0:T(8,128)(2,1)S(1)}, u32[]{:S(2)}, u32[]{:S(2)}) collective-permute-start(bf16[2048,128]{1,0:T(8,128)(2,1)S(1)} %get-tuple-element.84), channel_id=1, source_target_pairs={{0,0},{1,5},{2,2},{3,7},{4,4},{5,1},{6,6},{7,3},{8,8},{9,13},{10,1... | collective-permute-start | bytes 1572872 | tf_op jit(solution)/shard_map/ppermute | solution.py:26
  56.6 20.1 %collective-permute-start.13 = (bf16[2048,128]{1,0:T(8,128)(2,1)S(1)}, bf16[2048,128]{1,0:T(8,128)(2,1)S(1)}, u32[]{:S(2)}, u32[]{:S(2)}) collective-permute-start(bf16[2048,128]{1,0:T(8,128)(2,1)S(1)} %get-tuple-element.85), channel_id=1, source_target_pairs={{0,1},{1,4},{2,3},{3,6},{4,5},{5,0},{6,7},{7,2},{8,9},{9,12},{10,1... | collective-permute-start | bytes 1572872 | tf_op jit(solution)/shard_map/ppermute | solution.py:26
  60.7 3.2 %collective-permute-start.15 = (bf16[4096,128]{1,0:T(8,128)(2,1)S(1)}, bf16[4096,128]{1,0:T(8,128)(2,1)S(1)}, u32[]{:S(2)}, u32[]{:S(2)}) collective-permute-start(bf16[4096,128]{1,0:T(8,128)(2,1)S(1)} %get-tuple-element.91), channel_id=1, source_target_pairs={{0,1},{1,0},{2,3},{3,2},{4,5},{5,4},{6,7},{7,6},{8,9},{9,8},{10,11... | collective-permute-start | bytes 3145736 | tf_op jit(solution)/shard_map/ppermute | solution.py:26
  61.6 4.3 %collective-permute-start.17 = (bf16[512,512]{1,0:T(8,128)(2,1)S(1)}, bf16[512,512]{1,0:T(8,128)(2,1)S(1)}, u32[]{:S(2)}, u32[]{:S(2)}) collective-permute-start(bf16[512,512]{1,0:T(8,128)(2,1)S(1)} %get-tuple-element.96), channel_id=1, source_target_pairs={{0,1},{1,0},{2,3},{3,2},{4,5},{5,4},{6,7},{7,6},{8,9},{9,8},{10,11... | collective-permute-start | bytes 1572872 | tf_op jit(solution)/shard_map/ppermute | solution.py:26
  64.6 23.2 %collective-permute-start.16 = (bf16[2048,128]{1,0:T(8,128)(2,1)S(1)}, bf16[2048,128]{1,0:T(8,128)(2,1)S(1)}, u32[]{:S(2)}, u32[]{:S(2)}) collective-permute-start(bf16[2048,128]{1,0:T(8,128)(2,1)S(1)} %get-tuple-element.94), channel_id=1, source_target_pairs={{0,16},{1,17},{2,18},{3,19},{4,20},{5,21},{6,22},{7,23},{8,24},{9,... | collective-permute-start | bytes 1572872 | tf_op jit(solution)/shard_map/ppermute | solution.py:26
  69.5 12.9 %collective-permute-start.18 = (bf16[2048,128]{1,0:T(8,128)(2,1)S(1)}, bf16[2048,128]{1,0:T(8,128)(2,1)S(1)}, u32[]{:S(2)}, u32[]{:S(2)}) collective-permute-start(bf16[2048,128]{1,0:T(8,128)(2,1)S(1)} %get-tuple-element.101), channel_id=1, source_target_pairs={{0,8},{1,9},{2,10},{3,11},{4,12},{5,13},{6,14},{7,15},{8,0},{9,1},... | collective-permute-start | bytes 1572872 | tf_op jit(solution)/shard_map/ppermute | solution.py:26
  69.8 7.5 %collective-permute-start.19 = (bf16[4096,128]{1,0:T(8,128)(2,1)S(1)}, bf16[4096,128]{1,0:T(8,128)(2,1)S(1)}, u32[]{:S(2)}, u32[]{:S(2)}) collective-permute-start(bf16[4096,128]{1,0:T(8,128)(2,1)S(1)} %get-tuple-element.103), channel_id=1, source_target_pairs={{0,1},{1,0},{2,3},{3,2},{4,5},{5,4},{6,7},{7,6},{8,9},{9,8},{10,11... | collective-permute-start | bytes 3145736 | tf_op jit(solution)/shard_map/ppermute | solution.py:26
  78.0 11.6 %collective-permute-start.23 = (bf16[2048,128]{1,0:T(8,128)(2,1)S(1)}, bf16[2048,128]{1,0:T(8,128)(2,1)S(1)}, u32[]{:S(2)}, u32[]{:S(2)}) collective-permute-start(bf16[2048,128]{1,0:T(8,128)(2,1)S(1)} %get-tuple-element.112), channel_id=1, source_target_pairs={{0,16},{1,17},{2,18},{3,19},{4,20},{5,21},{6,22},{7,23},{8,24},{9,... | collective-permute-start | bytes 1572872 | tf_op jit(solution)/shard_map/ppermute | solution.py:26
  83.0 35.4 %collective-permute-start.27 = (bf16[2048,128]{1,0:T(8,128)(2,1)S(1)}, bf16[2048,128]{1,0:T(8,128)(2,1)S(1)}, u32[]{:S(2)}, u32[]{:S(2)}) collective-permute-start(bf16[2048,128]{1,0:T(8,128)(2,1)S(1)} %get-tuple-element.121), channel_id=1, source_target_pairs={{0,0},{1,5},{2,2},{3,7},{4,4},{5,1},{6,6},{7,3},{8,8},{9,13},{10,1... | collective-permute-start | bytes 1572872 | tf_op jit(solution)/shard_map/ppermute | solution.py:26
  87.7 30.6 %collective-permute-start.28 = (bf16[2048,128]{1,0:T(8,128)(2,1)S(1)}, bf16[2048,128]{1,0:T(8,128)(2,1)S(1)}, u32[]{:S(2)}, u32[]{:S(2)}) collective-permute-start(bf16[2048,128]{1,0:T(8,128)(2,1)S(1)} %get-tuple-element.122), channel_id=1, source_target_pairs={{0,1},{1,4},{2,3},{3,6},{4,5},{5,0},{6,7},{7,2},{8,9},{9,12},{10,1... | collective-permute-start | bytes 1572872 | tf_op jit(solution)/shard_map/ppermute | solution.py:26
  88.4 5.5 %collective-permute-start.20 = (bf16[512,128]{1,0:T(8,128)(2,1)S(1)}, bf16[512,128]{1,0:T(8,128)(2,1)S(1)}, u32[]{:S(2)}, u32[]{:S(2)}) collective-permute-start(bf16[512,128]{1,0:T(8,128)(2,1)S(1)} %get-tuple-element.108), channel_id=1, source_target_pairs={{0,8},{1,9},{2,10},{3,11},{4,12},{5,13},{6,14},{7,15},{8,0},{9,1},... | collective-permute-start | bytes 393224 | tf_op jit(solution)/shard_map/ppermute | solution.py:26
  88.8 17.8 %collective-permute-start.21 = (bf16[512,128]{1,0:T(8,128)(2,1)S(1)}, bf16[512,128]{1,0:T(8,128)(2,1)S(1)}, u32[]{:S(2)}, u32[]{:S(2)}) collective-permute-start(bf16[512,128]{1,0:T(8,128)(2,1)S(1)} %get-tuple-element.109), channel_id=1, source_target_pairs={{0,2},{1,3},{2,0},{3,1},{4,6},{5,7},{6,4},{7,5},{8,10},{9,11},{10,... | collective-permute-start | bytes 393224 | tf_op jit(solution)/shard_map/ppermute | solution.py:26
  89.6 18.8 %collective-permute-start.22 = (bf16[512,128]{1,0:T(8,128)(2,1)S(1)}, bf16[512,128]{1,0:T(8,128)(2,1)S(1)}, u32[]{:S(2)}, u32[]{:S(2)}) collective-permute-start(bf16[512,128]{1,0:T(8,128)(2,1)S(1)} %get-tuple-element.110), channel_id=1, source_target_pairs={{0,10},{1,11},{2,8},{3,9},{4,14},{5,15},{6,12},{7,13},{8,2},{9,3},... | collective-permute-start | bytes 393224 | tf_op jit(solution)/shard_map/ppermute | solution.py:26
  94.0 16.7 %collective-permute-start.24 = (bf16[512,128]{1,0:T(8,128)(2,1)S(1)}, bf16[512,128]{1,0:T(8,128)(2,1)S(1)}, u32[]{:S(2)}, u32[]{:S(2)}) collective-permute-start(bf16[512,128]{1,0:T(8,128)(2,1)S(1)} %get-tuple-element.115), channel_id=1, source_target_pairs={{0,8},{1,9},{2,10},{3,11},{4,12},{5,13},{6,14},{7,15},{8,0},{9,1},... | collective-permute-start | bytes 393224 | tf_op jit(solution)/shard_map/ppermute | solution.py:26
  106.5 6.0 %collective-permute-start.25 = (bf16[512,128]{1,0:T(8,128)(2,1)S(1)}, bf16[512,128]{1,0:T(8,128)(2,1)S(1)}, u32[]{:S(2)}, u32[]{:S(2)}) collective-permute-start(bf16[512,128]{1,0:T(8,128)(2,1)S(1)} %get-tuple-element.116), channel_id=1, source_target_pairs={{0,2},{1,3},{2,0},{3,1},{4,6},{5,7},{6,4},{7,5},{8,10},{9,11},{10,... | collective-permute-start | bytes 393224 | tf_op jit(solution)/shard_map/ppermute | solution.py:26
  108.4 5.7 %collective-permute-start.26 = (bf16[512,128]{1,0:T(8,128)(2,1)S(1)}, bf16[512,128]{1,0:T(8,128)(2,1)S(1)}, u32[]{:S(2)}, u32[]{:S(2)}) collective-permute-start(bf16[512,128]{1,0:T(8,128)(2,1)S(1)} %get-tuple-element.117), channel_id=1, source_target_pairs={{0,10},{1,11},{2,8},{3,9},{4,14},{5,15},{6,12},{7,13},{8,2},{9,3},... | collective-permute-start | bytes 393224 | tf_op jit(solution)/shard_map/ppermute | solution.py:26
  114.8 7.6 %collective-permute-start.29 = (bf16[512,128]{1,0:T(8,128)(2,1)S(1)}, bf16[512,128]{1,0:T(8,128)(2,1)S(1)}, u32[]{:S(2)}, u32[]{:S(2)}) collective-permute-start(bf16[512,128]{1,0:T(8,128)(2,1)S(1)} %get-tuple-element.126), channel_id=1, source_target_pairs={{0,4},{1,5},{2,6},{3,7},{4,0},{5,1},{6,2},{7,3},{8,12},{9,13},{10,... | collective-permute-start | bytes 393224 | tf_op jit(solution)/shard_map/ppermute | solution.py:26
